TPU v7x, 512 devices: a whole 4x4x16 slice. The times are simulated.
512 devices in a mesh: dp: 16 (over y, x_hi, core), row: 32 (over x_lo, z).
Axes of the slice: x: 4 (x_hi: 2, x_lo: 2; x = x_hi * 2 + x_lo), y: 4, z: 16, core: 2. Of those that a mesh axis runs over, the one named last changes fastest.
Arguments:
- embedding_row_values: bfloat16 [26, 8192, 128], P(None, 'row'), may hold values from -2 to 2
- accum: float32 [26, 8192], P(None, 'row'), may hold values from 0.01 to 0.1
- bag_ids: int32 [8192, 26, 8], P('dp'), may hold values from 0 to 8191
- cross_v: bfloat16 [3328, 256], P('row'), may hold values from -0.109375 to 0.109375
- cross_u: bfloat16 [3328, 256], P('row'), may hold values from -0.375 to 0.375
- cross_bias: float32 [3328], P('row'), may hold values from -3 to 3
- upstream: bfloat16 [8192, 3328], P('dp', 'row'), may hold values from -0.125 to 0.125
Outputs:
- crossed: bfloat16 [8192, 3328], P('dp', 'row')
- new_rows: bfloat16 [26, 8192, 128], P(None, 'row')
- new_accum: float32 [26, 8192], P(None, 'row')
- grad_v: float32 [3328, 256], P('row')
- grad_u: float32 [3328, 256], P('row')
- grad_bias: float32 [3328], P('row')
All inputs are finite; a program needn't handle non-finite values.
Results may differ from a plain program's by a relative error of at most 0.0068.
Values may be sent and summed in bfloat16 or wider, within the bound.
No kernel may reach another device: no remote copies, remote signals or barrier semaphores. Data moves between devices by JAX's collectives and lax.ppermute only.
A program may use at most 64 MiB of HBM per device.

v0:
```python
import jax
import jax.numpy as jnp
from jax import lax
from jax.sharding import PartitionSpec as P

learn_rate = 0.3
epsilon = 1e-06


def adagrad_step(rows_in, accum_in, grads_in):
    accum_out = accum_in + jnp.mean(grads_in * grads_in, axis=2)
    step_scale = lax.rsqrt(accum_out + epsilon)
    rows_out = (
        rows_in.astype(jnp.float32) - learn_rate * grads_in * step_scale[:, :, None]
    ).astype(jnp.bfloat16)
    return (rows_out, accum_out)


def body(embedding_row_values, accum, bag_ids, cross_v, cross_u, cross_bias, upstream):
    samples, tables, bag_size = bag_ids.shape
    row_count = embedding_row_values.shape[1]
    feat_width = embedding_row_values.shape[2]
    row_start = lax.axis_index("row") * row_count
    row_slots = lax.broadcasted_iota(jnp.int32, (1, 1, row_count), 2) + row_start
    visit_counts = jnp.zeros((samples, tables, row_count), jnp.bfloat16)
    for slot in range(bag_size):
        visit_counts = visit_counts + (bag_ids[:, :, slot, None] == row_slots).astype(jnp.bfloat16)
    partial_cross_value = jnp.einsum(
        "khb,hbm->khm", visit_counts, embedding_row_values, preferred_element_type=jnp.float32
    )
    partial_bf = partial_cross_value.astype(jnp.bfloat16).reshape(1, samples, tables * feat_width)
    received = lax.all_to_all(partial_bf, "row", split_axis=2, concat_axis=0, tiled=True)
    pooled = jnp.sum(received.astype(jnp.float32), axis=0).astype(jnp.bfloat16)
    rank_part = jnp.dot(pooled, cross_v, preferred_element_type=jnp.float32)
    rank_bf = lax.psum(rank_part, "row").astype(jnp.bfloat16)
    gate_term = (
        jnp.einsum("sr,fr->sf", rank_bf, cross_u, preferred_element_type=jnp.float32) + cross_bias
    )
    pooled_f = pooled.astype(jnp.float32)
    crossed = (pooled_f * gate_term + pooled_f).astype(jnp.bfloat16)
    cotangent = upstream.astype(jnp.float32)
    gate_grad = cotangent * pooled_f
    gate_bf = gate_grad.astype(jnp.bfloat16)
    grad_u_part = jnp.einsum("sf,sr->fr", gate_bf, rank_bf, preferred_element_type=jnp.float32)
    bias_part = jnp.sum(gate_grad, axis=0)
    rank_term = jnp.dot(gate_bf, cross_u, preferred_element_type=jnp.float32)
    rank_grad = lax.psum(rank_term, "row").astype(jnp.bfloat16)
    grad_v_part = jnp.einsum("sf,sr->fr", pooled, rank_grad, preferred_element_type=jnp.float32)
    back_proj = jnp.einsum("sr,fr->sf", rank_grad, cross_v, preferred_element_type=jnp.float32)
    pooled_grad = (cotangent * (gate_term + 1.0) + back_proj).astype(jnp.bfloat16)
    collected_rows = lax.all_gather(pooled_grad, "row", axis=1, tiled=True)
    collected_rows = collected_rows.reshape(samples, tables, feat_width)
    row_portion = jnp.einsum(
        "dhw,dhu->hwu", visit_counts, collected_rows, preferred_element_type=jnp.float32
    )
    row_grad, grad_v, grad_u, grad_bias = lax.psum(
        (row_portion, grad_v_part, grad_u_part, bias_part), "dp"
    )
    new_rows, new_accum = adagrad_step(embedding_row_values, accum, row_grad)
    return (crossed, new_rows, new_accum, grad_v, grad_u, grad_bias)


def solution(mesh):
    return jax.shard_map(
        body,
        mesh=mesh,
        in_specs=(
            P(None, "row", None),
            P(None, "row"),
            P("dp", None, None),
            P("row", None),
            P("row", None),
            P("row"),
            P("dp", "row"),
        ),
        out_specs=(
            P("dp", "row"),
            P(None, "row", None),
            P(None, "row"),
            P("row", None),
            P("row", None),
            P("row"),
        ),
        check_vma=False,
    )
```

profile of v0, /device:TPU:1, one launch (start us, length us, event | category | flops | bytes accessed | tf_op | source)
XLA Modules:
  0.0 724.1 jit_solution(5222311921187796714)
XLA Ops:
  7.2 0.0 copy-start
  7.2 0.0 all-gather.2.cloned.1.call-start
  7.2 3.1 fusion.23
  10.4 0.0 copy-start.5
  10.4 0.0 copy-start.6
  10.4 0.0 copy-start.7
  10.4 0.0 copy-start.8
  10.4 0.0 copy-start.9
  10.5 0.0 copy-start.10
  10.5 0.0 copy-start.11
  10.5 0.0 copy-start.12
  10.5 12.3 %convolution_convert_fusion = bf16[26,512,128]{1,2,0:T(8,128)(2,1)S(1)} fusion(bf16[26,256,128]{2,1,0:T(8,128)(2,1)} %param.7, s32[512,26]{0,1:T(8,128)S(1)} %get-tuple-element.24, s32[512,26]{0,1:T(8,128)S(1)} %get-tuple-element.25, s32[512,26]{0,1:T(8,128)S(1)} %get-tuple-element.26, s32[512,26]{0,1:T(8,128)S(1)} %get-tuple-element.27, ...), kind=kOutput, calls=%fused_computation.17 | convolution fusion | flops 952500224 | bytes 5538816 | tf_op jit(solution)/shard_map/khb,hbm->khm/dot_general | solution.py:28
  22.9 0.0 copy-done.5
  22.9 0.0 copy-done.6
  22.9 0.0 copy-done.7
  22.9 0.0 copy-done.8
  22.9 0.0 copy-done.9
  22.9 0.0 copy-done.10
  22.9 0.0 copy-done.11
  22.9 0.0 copy-done.12
  22.9 29.8 %copy.72 = bf16[1,512,3328]{1,0,2:T(2,128)(2,1)} copy(bf16[1,512,3328]{1,2,0:T(8,128)(2,1)S(1)} %bitcast.40) | data formatting | bytes 6815744 | tf_op jit(solution)/shard_map/reshape | solution.py:31
  52.7 0.5 broadcast.9
  53.2 21.9 %reduce.4 = bf16[3328,512]{1,0:T(8,128)(2,1)S(1)} reduce(bf16[3328,1,512]{2,1,0:T(2,128)(2,1)} %bitcast.37, bf16[]{:T(256)} %broadcast.9), dimensions={1}, to_apply=%bitcast.36.reduce_sub_computation | reduce | bytes 6815746
  75.1 2.8 reshape.28
  77.9 171.9 %all_to_all.12 = bf16[32,2,26624]{2,1,0:T(2,128)(2,1)S(1)} all-to-all(bf16[32,2,26624]{2,1,0:T(2,128)(2,1)} %reshape.28), channel_id=1, replica_groups=mesh['dp'=16,'row'=32] {'row'}, dimensions={0} | all-to-all | bytes 6815744 | tf_op jit(solution)/shard_map/all_to_all | solution.py:32
  249.9 12.7 %reshape.29 = bf16[3328,1,512]{2,1,0:T(2,128)(2,1)} reshape(bf16[32,2,26624]{2,1,0:T(2,128)(2,1)S(1)} %all_to_all.12) | data formatting | bytes 6815744
  262.6 0.0 copy-start.2
  262.6 0.0 copy-start.14
  262.6 3.9 copy.54
  266.5 1.2 reduce_sum.30
  267.7 0.0 copy-done.2
  267.7 1.1 fusion.24
  268.9 0.0 copy-done
  268.9 1.2 fusion.21
  270.1 104.7 %all-reduce.6 = (bf16[512,256]{1,0:T(8,128)(2,1)S(1)}, bf16[512,256]{1,0:T(8,128)(2,1)S(1)}) all-reduce(f32[512,256]{1,0:T(8,128)S(1)} %fusion.24, f32[512,256]{1,0:T(8,128)S(1)} %fusion.21), channel_id=1, replica_groups=mesh['dp'=16,'row'=32] {'row'}, use_global_device_ids=true, to_apply=%region_1.0 | all-reduce | flops 262144 | bytes 1572864 | tf_op jit(solution)/shard_map/psum | solution.py:35
  374.8 0.0 copy-done.14
  374.8 1.9 fusion.12
  376.7 1.8 fusion.10
  378.5 0.0 all-gather.2.cloned.1.call-update
  378.5 0.0 all-reduce.5.cloned.1.call-start
  378.6 1.7 fusion.25
  380.3 1.8 fusion.17
  382.1 133.3 %all-gather.2.cloned.1.call-done = bf16[512,3328]{0,1:T(8,128)(2,1)} async-done(((bf16[512,104]{0,1:T(8,128)(2,1)}), bf16[512,3328]{0,1:T(8,128)(2,1)}) %all-gather.2.cloned.1.call-update) | async-done | bytes 3407888 | tf_op jit(solution)/shard_map/all_gather | solution.py:51
  515.4 13.6 %fusion.7 = f32[26,256,128]{2,1,0:T(8,128)} fusion(bf16[512,26,128]{0,2,1:T(8,128)(2,1)} %bitcast.41, s32[512,26]{0,1:T(8,128)} %copy-done.7, s32[512,26]{0,1:T(8,128)} %copy-done.8, s32[512,26]{0,1:T(8,128)} %copy-done.9, s32[512,26]{0,1:T(8,128)} %copy-done.10, s32[512,26]{0,1:T(8,128)} %copy-done.11, s32[512,26]{0,1:T(8,128)} %copy-done.12, ...), kind=kOutput, calls=%fused_computation.18 | convolution fusion | flops 950796288 | bytes 7242752 | tf_op jit(solution)/shard_map/dhw,dhu->hwu/dot_general | solution.py:53
  529.0 0.0 copy-start.13
  529.0 0.0 copy-start.1
  529.0 0.0 all-reduce.5.cloned.1.call-update
  529.0 53.0 %psum.47 = f32[104]{0:T(128)} all-reduce(f32[104]{0:T(128)S(1)} %get-tuple-element.21), channel_id=1, replica_groups=mesh['dp'=16,'row'=32] {'dp'}, use_global_device_ids=true, to_apply=%region_8.0 | all-reduce | flops 104 | bytes 832 | tf_op jit(solution)/shard_map/psum | solution.py:56
  582.0 126.9 %all-reduce.5.cloned.1.call-done = (f32[26,256,128]{2,1,0:T(8,128)}, f32[104,256]{1,0:T(8,128)}, f32[104,256]{1,0:T(8,128)}) async-done(((f32[26,256,128]{2,1,0:T(8,128)}, f32[104,256]{1,0:T(8,128)}, f32[104,256]{1,0:T(8,128)}), (f32[26,256,128]{2,1,0:T(8,128)}, f32[104,256]{1,0:T(8,128)}, f32[104,256]{1,0:T(8,128)})) %all-reduce.5.cloned.1.call-update) | async-done | bytes 3620880 | tf_op jit(solution)/shard_map/psum | solution.py:56
  708.9 0.0 copy-start.4
  708.9 0.0 copy-start.3
  708.9 3.0 multiply_reduce_fusion
  711.9 0.0 copy-done.13
  711.9 0.6 rsqrt_multiply_fusion
  712.5 0.0 copy-done.1
  712.5 3.4 subtract_convert_fusion
  716.0 0.0 copy-done.4
  716.0 0.6 copy.80
  716.6 0.0 copy-done.3
  716.6 0.6 copy.81
  (5 shorter events, 0.1 us)
Async XLA Ops:
  7.2 261.7 %copy-start = (bf16[104,256]{1,0:T(8,128)(2,1)S(1)}, bf16[104,256]{1,0:T(8,128)(2,1)}, u32[]{:S(2)}) copy-start(bf16[104,256]{1,0:T(8,128)(2,1)} %param.11) | copy-start | bytes 159748
  7.2 508.2 %all-gather.2.cloned.1.call-start = ((), (), s32[]{:S(2)}) async-start(), calls=%async_computation.1 | async-start | bytes 3514368 | tf_op jit(solution)/shard_map/all_gather | solution.py:51
  10.4 12.5 %copy-start.5 = (s32[512,26]{0,1:T(8,128)}, s32[512,26]{0,1:T(8,128)S(1)}, u32[]{:S(2)}) copy-start(s32[512,26]{0,1:T(8,128)S(1)} %get-tuple-element.30) | copy-start | bytes 159748
  10.4 12.5 %copy-start.6 = (s32[512,26]{0,1:T(8,128)}, s32[512,26]{0,1:T(8,128)S(1)}, u32[]{:S(2)}) copy-start(s32[512,26]{0,1:T(8,128)S(1)} %get-tuple-element.31) | copy-start | bytes 159748
  10.4 12.5 %copy-start.7 = (s32[512,26]{0,1:T(8,128)}, s32[512,26]{0,1:T(8,128)S(1)}, u32[]{:S(2)}) copy-start(s32[512,26]{0,1:T(8,128)S(1)} %get-tuple-element.24) | copy-start | bytes 159748
  10.4 12.5 %copy-start.8 = (s32[512,26]{0,1:T(8,128)}, s32[512,26]{0,1:T(8,128)S(1)}, u32[]{:S(2)}) copy-start(s32[512,26]{0,1:T(8,128)S(1)} %get-tuple-element.25) | copy-start | bytes 159748
  10.4 12.5 %copy-start.9 = (s32[512,26]{0,1:T(8,128)}, s32[512,26]{0,1:T(8,128)S(1)}, u32[]{:S(2)}) copy-start(s32[512,26]{0,1:T(8,128)S(1)} %get-tuple-element.26) | copy-start | bytes 159748
  10.5 12.5 %copy-start.10 = (s32[512,26]{0,1:T(8,128)}, s32[512,26]{0,1:T(8,128)S(1)}, u32[]{:S(2)}) copy-start(s32[512,26]{0,1:T(8,128)S(1)} %get-tuple-element.27) | copy-start | bytes 159748
  10.5 12.4 %copy-start.11 = (s32[512,26]{0,1:T(8,128)}, s32[512,26]{0,1:T(8,128)S(1)}, u32[]{:S(2)}) copy-start(s32[512,26]{0,1:T(8,128)S(1)} %get-tuple-element.28) | copy-start | bytes 159748
  10.5 12.4 %copy-start.12 = (s32[512,26]{0,1:T(8,128)}, s32[512,26]{0,1:T(8,128)S(1)}, u32[]{:S(2)}) copy-start(s32[512,26]{0,1:T(8,128)S(1)} %get-tuple-element.29) | copy-start | bytes 159748
  262.6 5.1 copy-start.2
  262.6 112.2 %copy-start.14 = (f32[104]{0:T(128)S(1)}, f32[104]{0:T(128)}, u32[]{:S(2)}) copy-start(f32[104]{0:T(128)} %param.12) | copy-start | bytes 1252
  378.5 330.4 %all-reduce.5.cloned.1.call-start = ((), (), s32[]{:S(2)}) async-start(), calls=%async_computation.2 | async-start | bytes 7241728 | tf_op jit(solution)/shard_map/psum | solution.py:56
  529.0 182.9 %copy-start.13 = (f32[26,256]{1,0:T(8,128)S(1)}, f32[26,256]{1,0:T(8,128)}, u32[]{:S(2)}) copy-start(f32[26,256]{1,0:T(8,128)} %param.8) | copy-start | bytes 79876
  529.0 183.5 %copy-start.1 = (bf16[26,256,128]{2,1,0:T(8,128)(2,1)S(1)}, bf16[26,256,128]{2,1,0:T(8,128)(2,1)}, u32[]{:S(2)}) copy-start(bf16[26,256,128]{2,1,0:T(8,128)(2,1)} %param.7) | copy-start | bytes 5111812
  708.9 7.0 copy-start.4
  708.9 7.7 %copy-start.3 = (f32[104,256]{1,0:T(8,128)S(1)}, f32[104,256]{1,0:T(8,128)}, u32[]{:S(2)}) copy-start(f32[104,256]{1,0:T(8,128)} %get-tuple-element.36) | copy-start | bytes 319492
Sparse Core Ops, SparseCore 0:
  378.7 136.6 all-gather.1
  529.2 179.7 all-reduce.4
where the time goes:
time: 726 us; the launch traced here: 724 us
  blocking collectives  330 us (45%)
  waiting for transfers between devices  260 us (36%)
  local copies, waits for them, and re-layouts  54.3 us (7%)
  matrix products  35.5 us (5%)
  other arithmetic  30.1 us (4%)
  between operations  14.3 us (2%)
    all_to_all x1, blocking collectives, body(): lax.all_to_all(partial_bf, 'row', split_axis=2, concat_axis=0, tiled=True)  172 us
    all_gather x1, waiting for transfers between devices, body(): collected_rows = lax.all_gather(pooled_grad, 'row', axis=1, tiled=True)  133 us
    psum x1, waiting for transfers between devices, body(): lax.psum((row_portion, grad_v_part, grad_u_part, bias_part), 'dp')  127 us
    psum x1, blocking collectives, body(): rank_bf = lax.psum(rank_part, 'row').astype(jnp.bfloat16)  105 us
    psum x1, blocking collectives, body(): lax.psum((row_portion, grad_v_part, grad_u_part, bias_part), 'dp')  53 us
    reshape x1, local copies, waits for them, and re-layouts, body(): partial_cross_value.astype(jnp.bfloat16)  29.8 us
    unnamed x1, other arithmetic  21.9 us
    unnamed x36, local copies, waits for them, and re-layouts  21.3 us
  transfers between devices with their start and end apart: 2, of which 2 were waited for; matrix products, arithmetic and copies ran while one was open for 0% of the time, Pallas kernels for 0%

commit v1 on v0

v1 whole, which is shorter than its diff:
```python
import jax
import jax.numpy as jnp
from jax import lax
from jax.experimental import pallas as pl
from jax.experimental.pallas import tpu as pltpu
from jax.sharding import Mesh
from jax.sharding import PartitionSpec as P

bf16 = jnp.bfloat16
f32 = jnp.float32
learn_rate = 0.3
epsilon = 1e-06

SAMPLES, TABLES, BAG, ROWS, WIDTH, FEATS, RANK = 512, 26, 8, 256, 128, 104, 256
N_ROW, N_DP, PART = 32, 16, 16
STEP_ROWS = N_ROW * PART
WORDS = STEP_ROWS // 8
GRAD_ROWS = 8
OUT_ROWS = FEATS + GRAD_ROWS
DP_OUTER = ("y", "x_hi")
VMEM = 40 << 20

NT_DIMS = (((1,), (1,)), ((), ()))
TN_DIMS = (((0,), (0,)), ((), ()))


def counts_of(words):
    columns = []
    for lane in range(0, SAMPLES, 128):
        blocks = []
        for group in range(0, WORDS, 8):
            word = words[group : group + 8, lane : lane + 128]
            digits = [lax.shift_right_logical(word, jnp.int32(4 * j)) & 15 for j in range(8)]
            blocks.append(jnp.concatenate(digits, axis=0).astype(f32).astype(bf16))
        columns.append(jnp.concatenate(blocks, axis=0))
    return jnp.concatenate(columns, axis=1)


def words_of(place):
    inside = (place >= 0) & (place < STEP_ROWS)
    word = jnp.where(inside, ((place >> 6) << 3) | (place & 7), -1)
    unit = jnp.left_shift(jnp.int32(1), ((place >> 3) & 7) * 4)
    columns = []
    for lane in range(0, SAMPLES, 128):
        slots = lax.broadcasted_iota(jnp.int32, (WORDS, 128), 0)
        total = jnp.zeros((WORDS, 128), jnp.int32)
        for k in range(BAG):
            here = word[k : k + 1, lane : lane + 128] == slots
            total = total + jnp.where(here, unit[k : k + 1, lane : lane + 128], 0)
        columns.append(total)
    return jnp.concatenate(columns, axis=1)


def forward_kernel(
    scalars, ids_a, ids_b, own, other, v, u, upstream, pooled_out, words_out, ranks_out, places, total
):
    step = pl.program_id(0)
    core = scalars[2]

    @pl.when(step == 0)
    def _():
        total[...] = jnp.zeros_like(total)
        for table, ids in enumerate((ids_a, ids_b)):
            row = ids[0]
            part = (row >> 4) & 15
            turn = (part & 1) ^ core
            places[table] = turn * 4096 + (part >> 1) * 512 + (row >> 8) * 16 + (row & 15)

    rows = jnp.where(step < 8, own[0].astype(f32), other[0].astype(f32)).astype(bf16)
    for table in range(2):
        words = words_of(places[table] - step * STEP_ROWS)
        words_out[table, 0] = words
        total[table] += jnp.dot(rows, counts_of(words), preferred_element_type=f32)

    @pl.when(step == N_DP - 1)
    def _():
        feature = lax.broadcasted_iota(jnp.int32, (FEATS, SAMPLES), 0)
        pooled = jnp.where(feature < scalars[3], total[0], total[1]).astype(bf16)
        pooled_out[...] = pooled
        gate_grad = (upstream[...].astype(f32) * pooled.astype(f32)).astype(bf16)
        ranks_out[:RANK] = lax.dot_general(v[...], pooled, TN_DIMS, preferred_element_type=f32).astype(bf16)
        ranks_out[RANK:] = lax.dot_general(u[...], gate_grad, TN_DIMS, preferred_element_type=f32).astype(bf16)


def forward(scalars, ids, own, other, v, u, upstream):
    whole = lambda *shape: pl.BlockSpec(shape, lambda g, s: (0,) * len(shape))
    return pl.pallas_call(
        forward_kernel,
        grid_spec=pltpu.PrefetchScalarGridSpec(
            num_scalar_prefetch=1,
            grid=(N_DP,),
            in_specs=[
                pl.BlockSpec((1, BAG, SAMPLES), lambda g, s: (s[0], 0, 0)),
                pl.BlockSpec((1, BAG, SAMPLES), lambda g, s: (s[1], 0, 0)),
                pl.BlockSpec((1, FEATS, STEP_ROWS), lambda g, s: (jnp.minimum(g, 7), 0, 0)),
                pl.BlockSpec((1, FEATS, STEP_ROWS), lambda g, s: (jnp.maximum(g - 8, 0), 0, 0)),
                whole(FEATS, RANK),
                whole(FEATS, RANK),
                whole(FEATS, SAMPLES),
            ],
            out_specs=[
                whole(FEATS, SAMPLES),
                pl.BlockSpec((2, 1, WORDS, SAMPLES), lambda g, s: (0, g, 0, 0)),
                whole(2 * RANK, SAMPLES),
            ],
            scratch_shapes=[
                pltpu.VMEM((2, BAG, SAMPLES), jnp.int32),
                pltpu.VMEM((2, FEATS, SAMPLES), f32),
            ],
        ),
        out_shape=[
            jax.ShapeDtypeStruct((FEATS, SAMPLES), bf16),
            jax.ShapeDtypeStruct((2, N_DP, WORDS, SAMPLES), jnp.int32),
            jax.ShapeDtypeStruct((2 * RANK, SAMPLES), bf16),
        ],
        compiler_params=pltpu.CompilerParams(vmem_limit_bytes=VMEM),
        name="bags_and_ranks",
    )(scalars, ids, ids, own, other, v, u, upstream)


def backward_kernel(
    scalars, words, ranks, pooled_in, v, u, bias, upstream_in, crossed_out, own_out, other_out, grads, cross_grads
):
    step = pl.program_id(0)

    @pl.when(step == 0)
    def _():
        rank = ranks[:RANK]
        rank_grad = ranks[RANK:]
        pooled_bf = pooled_in[...]
        pooled = pooled_bf.astype(f32)
        upstream = upstream_in[...].astype(f32)
        gate = jnp.dot(u[...], rank, preferred_element_type=f32) + bias[...]
        crossed_out[...] = (pooled * gate + pooled).astype(bf16)
        back = jnp.dot(v[...], rank_grad, preferred_element_type=f32)
        grad = (upstream * (gate + 1.0) + back).astype(bf16).astype(f32)
        feature = lax.broadcasted_iota(jnp.int32, (FEATS, SAMPLES), 0)
        grads[0] = jnp.where(feature < scalars[1], grad, 0.0).astype(bf16)
        grads[1] = jnp.where(feature < scalars[1], 0.0, grad).astype(bf16)
        gate_grad = upstream * pooled
        gate_bf = gate_grad.astype(bf16)
        gate_rest = (gate_grad - gate_bf.astype(f32)).astype(bf16)
        cross_grads[...] = jnp.zeros_like(cross_grads)
        cross_grads[:FEATS, :RANK] = lax.dot_general(gate_bf, rank, NT_DIMS, preferred_element_type=f32)
        cross_grads[:FEATS, RANK:] = lax.dot_general(pooled_bf, rank_grad, NT_DIMS, preferred_element_type=f32)
        ones = jnp.ones((16, SAMPLES), bf16)
        bias_sum = lax.dot_general(ones, gate_bf, NT_DIMS, preferred_element_type=f32) + lax.dot_general(
            ones, gate_rest, NT_DIMS, preferred_element_type=f32
        )
        cross_grads[FEATS : FEATS + 8, :FEATS] = bias_sum[:8]

    turn = step // 8
    part = 2 * (step - 8 * turn) + (turn ^ scalars[0])
    result = lax.dot_general(grads[0], counts_of(words[0, 0]), NT_DIMS, preferred_element_type=f32)
    result = result + lax.dot_general(grads[1], counts_of(words[1, 0]), NT_DIMS, preferred_element_type=f32)
    extra = cross_grads[pl.ds(pl.multiple_of(part * GRAD_ROWS, GRAD_ROWS), GRAD_ROWS), :]
    block = jnp.concatenate([result, extra], axis=0).astype(bf16)

    @pl.when(turn == 0)
    def _():
        own_out[0] = block

    @pl.when(turn == 1)
    def _():
        other_out[0] = block


def backward(scalars, words, ranks, pooled, v, u, bias, upstream):
    whole = lambda *shape: pl.BlockSpec(shape, lambda g, s: (0,) * len(shape))
    return pl.pallas_call(
        backward_kernel,
        grid_spec=pltpu.PrefetchScalarGridSpec(
            num_scalar_prefetch=1,
            grid=(N_DP,),
            in_specs=[
                pl.BlockSpec((2, 1, WORDS, SAMPLES), lambda g, s: (0, g, 0, 0)),
                whole(2 * RANK, SAMPLES),
                whole(FEATS, SAMPLES),
                whole(FEATS, RANK),
                whole(FEATS, RANK),
                whole(FEATS, 1),
                whole(FEATS, SAMPLES),
            ],
            out_specs=[
                whole(FEATS, SAMPLES),
                pl.BlockSpec((1, OUT_ROWS, STEP_ROWS), lambda g, s: (jnp.minimum(g, 7), 0, 0)),
                pl.BlockSpec((1, OUT_ROWS, STEP_ROWS), lambda g, s: (jnp.maximum(g - 8, 0), 0, 0)),
            ],
            scratch_shapes=[
                pltpu.VMEM((2, FEATS, SAMPLES), bf16),
                pltpu.VMEM((N_DP * GRAD_ROWS, 2 * RANK), f32),
            ],
        ),
        out_shape=[
            jax.ShapeDtypeStruct((FEATS, SAMPLES), bf16),
            jax.ShapeDtypeStruct((8, OUT_ROWS, STEP_ROWS), bf16),
            jax.ShapeDtypeStruct((8, OUT_ROWS, STEP_ROWS), bf16),
        ],
        compiler_params=pltpu.CompilerParams(vmem_limit_bytes=VMEM),
        name="cross_and_row_grads",
    )(scalars, words, ranks, pooled, v, u, bias, upstream)


def exchange(x, axes):
    return lax.all_to_all(x, axes, 0, 0, tiled=True)


def spread(x, axes, count):
    return exchange(jnp.broadcast_to(x, (count,) + x.shape), axes)


def to_other_core(x):
    return lax.ppermute(x, "core", [(0, 1), (1, 0)])


def in_order(own, other, core):
    first = jnp.where(core == 0, own, other)
    second = jnp.where(core == 0, other, own)
    return jnp.stack([first, second], axis=1)


def body(rows_in, accum, bag_ids, cross_v, cross_u, cross_bias, upstream):
    block = lax.axis_index("row")
    core = lax.axis_index("core")
    part = lax.axis_index(DP_OUTER) * 2 + core
    table_a = (block * FEATS) // WIDTH
    table_b = jnp.minimum(table_a + 1, TABLES - 1)
    n_a = jnp.minimum(FEATS, WIDTH * (table_a + 1) - FEATS * block)

    my_rows = lax.dynamic_slice(rows_in, (0, part * PART, 0), (TABLES, PART, WIDTH))
    my_accum = lax.dynamic_slice(accum, (0, part * PART), (TABLES, PART))

    packed = my_rows.transpose(1, 0, 2).reshape(PART, N_ROW, FEATS).transpose(1, 0, 2)
    mine = exchange(packed, "row").reshape(STEP_ROWS, FEATS).T
    own = spread(mine, DP_OUTER, 8)
    other = to_other_core(own)

    upstream_t = upstream.T
    scalars = jnp.stack([table_a, table_b, core, n_a]).astype(jnp.int32)
    pooled, words, rank_parts = forward(
        scalars, bag_ids.transpose(1, 2, 0), own, other, cross_v, cross_u, upstream_t
    )

    gathered = exchange(rank_parts.reshape(N_ROW, 16, SAMPLES), "row")
    ranks = spread(jnp.sum(gathered.astype(f32), axis=0).astype(bf16), "row", N_ROW).reshape(2 * RANK, SAMPLES)

    scalars = jnp.stack([core, n_a]).astype(jnp.int32)
    crossed, own, other = backward(
        scalars, words, ranks, pooled, cross_v, cross_u, cross_bias.reshape(FEATS, 1), upstream_t
    )

    chip_sum = (own.astype(f32) + to_other_core(other).astype(f32)).astype(bf16)
    sums = jnp.sum(exchange(chip_sum, DP_OUTER).astype(f32), axis=0)
    row_grad = sums[:FEATS].astype(bf16).T.reshape(N_ROW, PART, FEATS)
    row_grad = exchange(row_grad, "row").transpose(1, 0, 2).reshape(PART, TABLES, WIDTH)
    row_grad = row_grad.transpose(1, 0, 2).astype(f32)

    accum_out = my_accum + jnp.mean(row_grad * row_grad, axis=2)
    scale = lax.rsqrt(accum_out + epsilon)
    rows_out = (my_rows.astype(f32) - learn_rate * row_grad * scale[:, :, None]).astype(bf16)

    high = accum_out.astype(bf16)
    rest = accum_out - high.astype(f32)
    middle = rest.astype(bf16)
    low = (rest - middle.astype(f32)).astype(bf16)
    accum_terms = jnp.stack([high, middle, low, jnp.zeros_like(low)]).reshape(13, WIDTH)
    cross_grads = sums[FEATS:].astype(bf16).reshape(32, WIDTH)
    result = jnp.concatenate([rows_out.reshape(TABLES * PART, WIDTH), accum_terms, cross_grads], axis=0)
    own = spread(result, DP_OUTER, 8)
    result = in_order(own, to_other_core(own), core)

    new_rows = result[:, :, :416].reshape(N_DP, TABLES, PART, WIDTH).transpose(1, 0, 2, 3).reshape(TABLES, ROWS, WIDTH)
    terms = result[:, :, 416:429].reshape(N_DP, 4, TABLES, PART).astype(f32)
    new_accum = (terms[:, 0] + terms[:, 1] + terms[:, 2]).transpose(1, 0, 2).reshape(TABLES, ROWS)
    cross_grads = result[:, :, 429:].reshape(N_DP * GRAD_ROWS, 2 * RANK).astype(f32)
    grad_u = cross_grads[:FEATS, :RANK]
    grad_v = cross_grads[:FEATS, RANK:]
    grad_bias = cross_grads[FEATS, :FEATS]
    return (crossed.T, new_rows, new_accum, grad_v, grad_u, grad_bias)


def solution(mesh):
    inner = Mesh(mesh.devices.reshape(4, 2, 2, N_ROW), DP_OUTER + ("core", "row"))
    dp = DP_OUTER + ("core",)
    return jax.shard_map(
        body,
        mesh=inner,
        in_specs=(
            P(None, "row", None),
            P(None, "row"),
            P(dp, None, None),
            P("row", None),
            P("row", None),
            P("row"),
            P(dp, "row"),
        ),
        out_specs=(
            P(dp, "row"),
            P(None, "row", None),
            P(None, "row"),
            P("row", None),
            P("row", None),
            P("row"),
        ),
        check_vma=False,
    )
```

time: 726 us -> 248 us (0.34)
  blocking collectives: 330 us -> 119 us
  waiting for transfers between devices: 260 us -> 50.5 us
  local copies, waits for them, and re-layouts: 54.3 us -> 18.7 us
  matrix products: 35.5 us -> 0 us
  starting transfers between devices: 0.08 us -> 26.8 us
  Pallas kernels: 0 us -> 24.7 us
  other arithmetic: 30.1 us -> 6.67 us
  between operations: 14.3 us -> 0.98 us
    psum x2 -> x0, blocking collectives: 158 us -> none  [the longest x1 105 us: body(): rank_bf = lax.psum(rank_part, 'row').astype(jnp.bfloat16)]
    all_gather x1 -> x0, waiting for transfers between devices: 133 us -> none  [body(): collected_rows = lax.all_gather(pooled_grad, 'row', axis=1, tiled=True)]
    psum x1 -> x0, waiting for transfers between devices: 127 us -> none  [body(): lax.psum((row_portion, grad_v_part, grad_u_part, bias_part), 'dp')]
    all_to_all x1 -> x5, blocking collectives: 172 us -> 119 us  [exchange(): return lax.all_to_all(x, axes, 0, 0, tiled=True)]
    all_to_all x0 -> x2, waiting for transfers between devices: none -> 44.2 us  [exchange(): return lax.all_to_all(x, axes, 0, 0, tiled=True)]
    dot_general x8 -> x0, matrix products: 35.5 us -> none  [the longest x1 13.6 us: body(): jnp.einsum('dhw,dhu->hwu', visit_counts, collected_rows, preferred_elemen...]
    reshape x1 -> x5, local copies, waits for them, and re-layouts: 29.8 us -> 2.21 us  [the longest x1 1.67 us: body(): (terms[:, 0] + terms[:, 1] + terms[:, 2]).transpose(1, 0, 2)]
    pallas_call x0 -> x2, Pallas kernels: none -> 24.7 us  [the longest x1 14.7 us: forward(): pl.pallas_call(forward_kernel, grid_spec=pltpu.PrefetchScalarGridSpec(num...]
  transfers between devices with their start and end apart: 2 -> 5, of which waited for: 2 -> 5; matrix products, arithmetic and copies ran while one was open for 0% -> 0% of each run, Pallas kernels for 0% -> 0%
where the time goes in v1:
time: 248 us; the launch traced here: 247 us
  blocking collectives  119 us (48%)
  waiting for transfers between devices  50.5 us (20%)
  starting transfers between devices  26.8 us (11%)
  Pallas kernels  24.7 us (10%)
  local copies, waits for them, and re-layouts  18.7 us (8%)
  other arithmetic  6.67 us (3%)
    all_to_all x5, blocking collectives, exchange(): return lax.all_to_all(x, axes, 0, 0, tiled=True)  119 us
    all_to_all x2, waiting for transfers between devices, exchange(): return lax.all_to_all(x, axes, 0, 0, tiled=True)  44.2 us
    ppermute x3, starting transfers between devices, to_other_core(): return lax.ppermute(x, 'core', [(0, 1), (1, 0)])  16.7 us
    pallas_call x1, Pallas kernels, forward(): pl.pallas_call(forward_kernel, grid_spec=pltpu.PrefetchScalarGridSpec(num...  14.7 us
    all_to_all x2, starting transfers between devices, exchange(): return lax.all_to_all(x, axes, 0, 0, tiled=True)  10.2 us
    pallas_call x1, Pallas kernels, backward(): pl.pallas_call(backward_kernel, grid_spec=pltpu.PrefetchScalarGridSpec(nu...  10 us
    unnamed x28, local copies, waits for them, and re-layouts  7.6 us
    ppermute x3, waiting for transfers between devices, to_other_core(): return lax.ppermute(x, 'core', [(0, 1), (1, 0)])  6.34 us
  transfers between devices with their start and end apart: 5, of which 5 were waited for; matrix products, arithmetic and copies ran while one was open for 0% of the time, Pallas kernels for 0%

profile of v1, /device:TPU:1, one launch (start us, length us, event | category | flops | bytes accessed | tf_op | source)
XLA Modules:
  0.0 247.0 jit_solution(15660437473302722114)
XLA Ops:
  0.6 0.0 copy-start
  0.7 1.4 copy-done
  2.1 0.0 copy-start.3
  2.2 0.0 copy-start.4
  2.2 0.0 copy-start.5
  2.2 0.0 copy-start.6
  2.2 0.3 reshape.60
  2.5 0.1 copy.65
  2.6 31.3 %all_to_all.35 = bf16[32,16,104]{2,1,0:T(8,128)(2,1)S(1)} all-to-all(bf16[32,16,104]{2,1,0:T(8,128)(2,1)S(1)} %copy.65), channel_id=1, replica_groups=mesh['y'=4,'x_hi'=2,'core'=2,'row'=32] {'row'}, dimensions={0} | all-to-all | bytes 212992 | tf_op jit(solution)/shard_map/all_to_all | solution.py:205
  33.9 0.1 copy.66
  34.0 0.1 broadcast_in_dim.10
  34.1 17.8 %all_to_all.36.own = bf16[8,104,512]{2,1,0:T(8,128)(2,1)S(1)} all-to-all(bf16[8,104,512]{2,1,0:T(8,128)(2,1)S(1)} %broadcast_in_dim.10), channel_id=1, replica_groups=mesh['y'=4,'x_hi'=2,'core'=2,'row'=32] {'y','x_hi'}, dimensions={0} | all-to-all | bytes 1703936 | tf_op jit(solution)/shard_map/all_to_all | solution.py:205
  51.9 6.4 %collective-permute-start = (bf16[8,104,512]{2,1,0:T(8,128)(2,1)S(1)}, bf16[8,104,512]{2,1,0:T(8,128)(2,1)}, u32[]{:S(2)}, u32[]{:S(2)}) collective-permute-start(bf16[8,104,512]{2,1,0:T(8,128)(2,1)S(1)} %all_to_all.36.own), channel_id=1, source_target_pairs={{0,32},{32,0},{1,33},{33,1},{2,34},{34,2},{3,35},{35,3},{4,36},{36... | collective-permute-start | bytes 2555912 | tf_op jit(solution)/shard_map/ppermute | solution.py:213
  58.3 0.1 pad_add_fusion.1.scalars
  58.4 2.0 collective-permute-done.other
  60.5 14.7 %bags_and_ranks.1 = (bf16[104,512]{1,0:T(8,128)(2,1)S(1)}, s32[2,16,64,512]{3,2,1,0:T(8,128)S(1)}, bf16[512,512]{1,0:T(8,128)(2,1)S(1)}) custom-call(s32[4]{0:T(128)S(1)} %pad_add_fusion.1.scalars, s32[26,8,512]{2,1,0:T(8,128)S(1)} %bitcast.58, s32[26,8,512]{2,1,0:T(8,128)S(1)} %bitcast.59, bf16[8,104,512]{2,1,0:T(8,128)(2,1)S(1)} %all_to_all.36.own, ...), custom_call_target="tpu_custom_call" | custom-call | tf_op jit(solution)/shard_map/bags_and_ranks/pallas_call | solution.py:87
  75.2 2.0 copy-done.1
  77.1 35.3 %all_to_all.37 = bf16[32,16,512]{2,1,0:T(8,128)(2,1)S(1)} all-to-all(bf16[32,16,512]{2,1,0:T(8,128)(2,1)S(1)} %bitcast.60), channel_id=1, replica_groups=mesh['y'=4,'x_hi'=2,'core'=2,'row'=32] {'row'}, dimensions={0} | all-to-all | bytes 1048576 | tf_op jit(solution)/shard_map/all_to_all | solution.py:205
  112.4 0.1 reduce_sum.30
  112.5 0.9 broadcast_in_dim.11
  113.3 5.5 %all-to-all-start.3 = ((bf16[32,16,512]{2,1,0:T(8,128)(2,1)}), bf16[32,16,512]{2,1,0:T(8,128)(2,1)S(1)}, u32[]{:S(2)}, u32[]{:S(2)}) async-start(bf16[32,16,512]{2,1,0:T(8,128)(2,1)} %broadcast_in_dim.11), calls=%async_computation.3 | async-start | bytes 1048576 | tf_op jit(solution)/shard_map/all_to_all | solution.py:205
  118.9 0.1 copy.67.bias
  119.0 0.1 pad_add_fusion.scalars
  119.0 30.1 %all-to-all-done.3 = bf16[32,16,512]{2,1,0:T(8,128)(2,1)S(1)} async-done(((bf16[32,16,512]{2,1,0:T(8,128)(2,1)}), bf16[32,16,512]{2,1,0:T(8,128)(2,1)S(1)}, u32[]{:S(2)}, u32[]{:S(2)}) %all-to-all-start.3) | async-done | bytes 524320 | tf_op jit(solution)/shard_map/all_to_all | solution.py:205
  149.1 2.2 copy-done.2
  151.3 10.0 %cross_and_row_grads.1 = (bf16[104,512]{1,0:T(8,128)(2,1)}, bf16[8,112,512]{2,1,0:T(8,128)(2,1)S(1)}, bf16[8,112,512]{2,1,0:T(8,128)(2,1)S(1)}) custom-call(s32[2]{0:T(128)S(1)} %pad_add_fusion.scalars, s32[2,16,64,512]{3,2,1,0:T(8,128)S(1)} %copy-done.2, bf16[512,512]{1,0:T(8,128)(2,1)S(1)} %bitcast.57, bf16[104,512]{1,0:T(8,128)(2,1)S(1)} %get-tuple-element.14.pooled_in, ...), custom_call_target="tpu_custom_call" | custom-call | tf_op jit(solution)/shard_map/cross_and_row_grads/pallas_call | solution.py:170
  161.3 4.1 %collective-permute-start.1 = (bf16[8,112,512]{2,1,0:T(8,128)(2,1)S(1)}, bf16[8,112,512]{2,1,0:T(8,128)(2,1)S(1)}, u32[]{:S(2)}, u32[]{:S(2)}) collective-permute-start(bf16[8,112,512]{2,1,0:T(8,128)(2,1)S(1)} %get-tuple-element.17), channel_id=1, source_target_pairs={{0,32},{32,0},{1,33},{33,1},{2,34},{34,2},{3,35},{35,3},{4,36},{36... | collective-permute-start | bytes 2752520 | tf_op jit(solution)/shard_map/ppermute | solution.py:213
  165.4 2.1 collective-permute-done.1
  167.5 0.3 add_convert_fusion
  167.7 0.0 copy-start.11
  167.8 17.9 %all_to_all.38 = bf16[8,112,512]{2,1,0:T(8,128)(2,1)S(1)} all-to-all(bf16[8,112,512]{2,1,0:T(8,128)(2,1)S(1)} %add_convert_fusion), channel_id=1, replica_groups=mesh['y'=4,'x_hi'=2,'core'=2,'row'=32] {'y','x_hi'}, dimensions={0} | all-to-all | bytes 1835008 | tf_op jit(solution)/shard_map/all_to_all | solution.py:205
  185.6 0.1 reduce.1
  185.8 0.8 copy.68
  186.5 4.7 %all-to-all-start.5 = ((bf16[32,16,104]{2,1,0:T(8,128)(2,1)}), bf16[32,16,104]{2,1,0:T(8,128)(2,1)S(1)}, u32[]{:S(2)}, u32[]{:S(2)}) async-start(bf16[32,16,104]{2,1,0:T(8,128)(2,1)} %bitcast.15), calls=%async_computation.5 | async-start | bytes 262144 | tf_op jit(solution)/shard_map/all_to_all | solution.py:205
  191.2 0.1 constant_dynamic-slice_fusion
  191.3 0.1 copy.80
  191.4 0.1 pad.8.clone
  191.5 14.1 %all-to-all-done.5 = bf16[32,16,104]{2,1,0:T(8,128)(2,1)S(1)} async-done(((bf16[32,16,104]{2,1,0:T(8,128)(2,1)}), bf16[32,16,104]{2,1,0:T(8,128)(2,1)S(1)}, u32[]{:S(2)}, u32[]{:S(2)}) %all-to-all-start.5) | async-done | bytes 106528 | tf_op jit(solution)/shard_map/all_to_all | solution.py:205
  205.6 0.1 copy.69
  205.7 0.2 reshape.74
  206.0 0.1 fusion.2
  206.1 0.1 fusion.4
  206.3 0.1 maximum_maximum_fusion
  206.4 0.1 copy.72
  206.5 0.1 reshape.67
  206.7 0.1 broadcast_in_dim.12
  206.8 16.4 %all_to_all.39 = bf16[8,461,128]{2,1,0:T(8,128)(2,1)S(1)} all-to-all(bf16[8,461,128]{2,1,0:T(8,128)(2,1)S(1)} %broadcast_in_dim.12), channel_id=1, replica_groups=mesh['y'=4,'x_hi'=2,'core'=2,'row'=32] {'y','x_hi'}, dimensions={0} | all-to-all | bytes 1888256 | tf_op jit(solution)/shard_map/all_to_all | solution.py:205
  223.1 0.9 copy-done.9
  224.1 0.2 copy.73
  224.3 6.1 %collective-permute-start.2 = (bf16[8,461,128]{2,0,1:T(8,128)(2,1)S(1)}, bf16[8,461,128]{2,0,1:T(8,128)(2,1)}, u32[]{:S(2)}, u32[]{:S(2)}) collective-permute-start(bf16[8,461,128]{2,0,1:T(8,128)(2,1)S(1)} %copy.73), channel_id=1, source_target_pairs={{0,32},{32,0},{1,33},{33,1},{2,34},{34,2},{3,35},{35,3},{4,36},{36... | collective-permute-start | bytes 2832392 | tf_op jit(solution)/shard_map/ppermute | solution.py:213
  230.5 2.2 collective-permute-done.2
  232.7 1.7 select_bitcast_fusion
  234.4 0.0 copy-start.7
  234.4 0.9 copy-done.7
  235.4 0.0 copy-start.8
  235.4 0.7 fusion.11
  236.1 0.5 slice_bitcast_fusion.1
  236.6 1.4 fusion.7
  238.0 1.3 fusion
  239.4 2.3 reshape.72
  241.7 1.2 fusion.1
  242.9 0.8 copy.78
  243.7 1.7 reshape.71
  245.3 1.7 copy.77
  (25 shorter events, 0.3 us)
Async XLA Ops:
  0.6 1.5 copy-start
  2.1 58.3 %copy-start.3 = (s32[512,26,8]{0,2,1:T(8,128)S(1)}, s32[512,26,8]{0,2,1:T(8,128)}, u32[]{:S(2)}) copy-start(s32[512,26,8]{0,2,1:T(8,128)} %param.9) | copy-start | bytes 1277956
  2.2 58.3 %copy-start.4 = (bf16[512,104]{0,1:T(8,128)(2,1)S(1)}, bf16[512,104]{0,1:T(8,128)(2,1)}, u32[]{:S(2)}) copy-start(bf16[512,104]{0,1:T(8,128)(2,1)} %param.13) | copy-start | bytes 319492
  2.2 58.3 %copy-start.5 = (bf16[104,256]{1,0:T(8,128)(2,1)S(1)}, bf16[104,256]{1,0:T(8,128)(2,1)}, u32[]{:S(2)}) copy-start(bf16[104,256]{1,0:T(8,128)(2,1)} %v.3) | copy-start | bytes 159748
  2.2 58.3 %copy-start.6 = (bf16[104,256]{1,0:T(8,128)(2,1)S(1)}, bf16[104,256]{1,0:T(8,128)(2,1)}, u32[]{:S(2)}) copy-start(bf16[104,256]{1,0:T(8,128)(2,1)} %u.3) | copy-start | bytes 159748
  51.9 8.6 %collective-permute-start = (bf16[8,104,512]{2,1,0:T(8,128)(2,1)S(1)}, bf16[8,104,512]{2,1,0:T(8,128)(2,1)}, u32[]{:S(2)}, u32[]{:S(2)}) collective-permute-start(bf16[8,104,512]{2,1,0:T(8,128)(2,1)S(1)} %all_to_all.36.own), channel_id=1, source_target_pairs={{0,32},{32,0},{1,33},{33,1},{2,34},{34,2},{3,35},{35,3},{4,36},{36... | collective-permute-start | bytes 2555912 | tf_op jit(solution)/shard_map/ppermute | solution.py:213
  75.2 2.0 copy-start.1
  77.1 41.7 %copy-start.12 = (f32[104]{0:T(128)S(1)}, f32[104]{0:T(128)}, u32[]{:S(2)}) copy-start(f32[104]{0:T(128)} %param.12) | copy-start | bytes 1252
  113.3 35.8 %all-to-all-start.3 = ((bf16[32,16,512]{2,1,0:T(8,128)(2,1)}), bf16[32,16,512]{2,1,0:T(8,128)(2,1)S(1)}, u32[]{:S(2)}, u32[]{:S(2)}) async-start(bf16[32,16,512]{2,1,0:T(8,128)(2,1)} %broadcast_in_dim.11), calls=%async_computation.3 | async-start | bytes 1048576 | tf_op jit(solution)/shard_map/all_to_all | solution.py:205
  149.1 2.2 copy-start.2
  161.3 6.2 %collective-permute-start.1 = (bf16[8,112,512]{2,1,0:T(8,128)(2,1)S(1)}, bf16[8,112,512]{2,1,0:T(8,128)(2,1)S(1)}, u32[]{:S(2)}, u32[]{:S(2)}) collective-permute-start(bf16[8,112,512]{2,1,0:T(8,128)(2,1)S(1)} %get-tuple-element.17), channel_id=1, source_target_pairs={{0,32},{32,0},{1,33},{33,1},{2,34},{34,2},{3,35},{35,3},{4,36},{36... | collective-permute-start | bytes 2752520 | tf_op jit(solution)/shard_map/ppermute | solution.py:213
  167.7 23.5 %copy-start.11 = (f32[26,256]{1,0:T(8,128)S(1)}, f32[26,256]{1,0:T(8,128)}, u32[]{:S(2)}) copy-start(f32[26,256]{1,0:T(8,128)} %param.8) | copy-start | bytes 79876
  186.5 19.1 %all-to-all-start.5 = ((bf16[32,16,104]{2,1,0:T(8,128)(2,1)}), bf16[32,16,104]{2,1,0:T(8,128)(2,1)S(1)}, u32[]{:S(2)}, u32[]{:S(2)}) async-start(bf16[32,16,104]{2,1,0:T(8,128)(2,1)} %bitcast.15), calls=%async_computation.5 | async-start | bytes 262144 | tf_op jit(solution)/shard_map/all_to_all | solution.py:205
  223.1 0.9 copy-start.9
  224.3 8.4 %collective-permute-start.2 = (bf16[8,461,128]{2,0,1:T(8,128)(2,1)S(1)}, bf16[8,461,128]{2,0,1:T(8,128)(2,1)}, u32[]{:S(2)}, u32[]{:S(2)}) collective-permute-start(bf16[8,461,128]{2,0,1:T(8,128)(2,1)S(1)} %copy.73), channel_id=1, source_target_pairs={{0,32},{32,0},{1,33},{33,1},{2,34},{34,2},{3,35},{35,3},{4,36},{36... | collective-permute-start | bytes 2832392 | tf_op jit(solution)/shard_map/ppermute | solution.py:213
  234.4 0.9 copy-start.7
  235.4 2.6 %copy-start.8 = (bf16[8,1,461,128]{3,2,1,0:T(8,128)(2,1)S(1)}, bf16[8,1,461,128]{3,2,1,0:T(8,128)(2,1)}, u32[]{:S(2)}) copy-start(bf16[8,1,461,128]{3,2,1,0:T(8,128)(2,1)} %copy-done.7) | copy-start | bytes 2832388
  239.4 6.0 %copy-start.10 = (bf16[8,2,416,128]{3,2,1,0:T(8,128)(2,1)S(1)}, bf16[8,2,416,128]{3,2,1,0:T(8,128)(2,1)}, u32[]{:S(2)}) copy-start(bf16[8,2,416,128]{3,2,1,0:T(8,128)(2,1)} %fusion) | copy-start | bytes 5111812

commit v2 on v1

--- a/solution.py
+++ b/solution.py
@@ -17,11 +17,145 @@
 WORDS = STEP_ROWS // 8
 GRAD_ROWS = 8
 OUT_ROWS = FEATS + GRAD_ROWS
-DP_OUTER = ("y", "x_hi")
+DP_OUTER = ("x_hi", "y")
+ROW_AXES = ("z", "x_lo")
+ROW_ALL = ("x_lo", "z")
+BLOCK_OF = [(i & 1) * 16 + (i >> 1) for i in range(N_ROW)]
+CHUNK = TABLES * PART + 16 + 32
 VMEM = 40 << 20
 
 NT_DIMS = (((1,), (1,)), ((), ()))
 TN_DIMS = (((0,), (0,)), ((), ()))
+
+
+def part_of(outer, core):
+    return (outer & 3) * 4 + (outer >> 2) * 2 + core
+
+
+def pieces(table):
+    found = []
+    for block in range(N_ROW):
+        low = max(table * WIDTH, block * FEATS)
+        high = min((table + 1) * WIDTH, (block + 1) * FEATS)
+        if low < high:
+            found.append((block, low - block * FEATS, high - block * FEATS))
+    return found
+
+
+def pack_kernel(scalars, rows, mine, packed):
+    mine[...] = rows[...]
+    for device, block in enumerate(BLOCK_OF):
+        first = block * FEATS // WIDTH
+        start = block * FEATS - first * WIDTH
+        cut = rows[first][:, start:].astype(f32)
+        if cut.shape[1] < FEATS:
+            cut = jnp.concatenate([cut, rows[first + 1][:, : FEATS - cut.shape[1]].astype(f32)], axis=1)
+        packed[device] = cut[:, :FEATS].astype(bf16)
+
+
+def pack(scalars, rows):
+    return pl.pallas_call(
+        pack_kernel,
+        grid_spec=pltpu.PrefetchScalarGridSpec(
+            num_scalar_prefetch=1,
+            grid=(1,),
+            in_specs=[pl.BlockSpec((TABLES, PART, WIDTH), lambda g, s: (0, s[0], 0))],
+            out_specs=[
+                pl.BlockSpec((TABLES, PART, WIDTH), lambda g, s: (0, 0, 0)),
+                pl.BlockSpec((N_ROW, PART, FEATS), lambda g, s: (0, 0, 0)),
+            ],
+        ),
+        out_shape=[
+            jax.ShapeDtypeStruct((TABLES, PART, WIDTH), bf16),
+            jax.ShapeDtypeStruct((N_ROW, PART, FEATS), bf16),
+        ],
+        compiler_params=pltpu.CompilerParams(vmem_limit_bytes=VMEM),
+        name="pack_rows",
+    )(scalars, rows)
+
+
+def adagrad_kernel(grads, rows, accum, cross_grads, out):
+    table_lane = lax.broadcasted_iota(jnp.int32, (PART, WIDTH), 1)
+    accum_in = accum[...]
+    accum_out = jnp.zeros((PART, WIDTH), f32)
+    device_of = {block: device for device, block in enumerate(BLOCK_OF)}
+    for table in range(TABLES):
+        cuts = [grads[device_of[block]].astype(f32)[:, low:high] for block, low, high in pieces(table)]
+        grad = jnp.concatenate(cuts, axis=1)
+        total = accum_in[:, table : table + 1] + jnp.mean(grad * grad, axis=1, keepdims=True)
+        step = learn_rate * grad * lax.rsqrt(total + epsilon)
+        new = (rows[table].astype(f32) - step).astype(bf16)
+        for copy in range(8):
+            out[copy, table * PART : (table + 1) * PART, :] = new
+        accum_out = jnp.where(table_lane == table, total, accum_out)
+    high = accum_out.astype(bf16).astype(f32)
+    rest = accum_out - high
+    middle = rest.astype(bf16).astype(f32)
+    low = rest - middle
+    terms = jnp.concatenate(
+        [high[:, :32], middle[:, :32], low[:, :32], jnp.zeros((PART, 32), f32)], axis=1
+    ).astype(bf16)
+    wide = cross_grads[...]
+    wide = jnp.concatenate([wide[:, lane : lane + WIDTH] for lane in range(0, 2 * RANK, WIDTH)], axis=0).astype(bf16)
+    for copy in range(8):
+        out[copy, TABLES * PART : TABLES * PART + PART, :] = terms
+        out[copy, TABLES * PART + PART :, :] = wide
+
+
+def adagrad(grads, rows, accum, cross_grads):
+    return pl.pallas_call(
+        adagrad_kernel,
+        out_shape=jax.ShapeDtypeStruct((8, CHUNK, WIDTH), bf16),
+        compiler_params=pltpu.CompilerParams(vmem_limit_bytes=VMEM),
+        name="adagrad",
+    )(grads, rows, accum, cross_grads)
+
+
+def unpack_kernel(scalars, own, other, rows_out, accum_out, grad_v, grad_u, grad_bias, accums, cross_grads):
+    for outer in range(8):
+        for turn, source in enumerate((own, other)):
+            part = part_of(outer, turn ^ scalars[0])
+            rows_out[:, pl.ds(part, 1)] = source[outer, : TABLES * PART].reshape(TABLES, 1, PART, WIDTH)
+            terms = source[outer, TABLES * PART : TABLES * PART + PART].astype(f32)
+            total = terms[:, :32] + terms[:, 32:64] + terms[:, 64:96]
+            accums[pl.ds(pl.multiple_of(part * PART, PART), PART), :] = jnp.concatenate(
+                [total, jnp.zeros((PART, WIDTH - 32), f32)], axis=1
+            )
+            wide = source[outer, TABLES * PART + PART :].astype(f32)
+            at = pl.multiple_of(part * GRAD_ROWS, GRAD_ROWS)
+            for i in range(4):
+                cross_grads[pl.ds(at, GRAD_ROWS), i * WIDTH : (i + 1) * WIDTH] = wide[i * 8 : (i + 1) * 8]
+    accum_out[...] = accums[...].T[:TABLES]
+    grad_u[...] = cross_grads[:FEATS, :RANK]
+    grad_v[...] = cross_grads[:FEATS, RANK:]
+    grad_bias[...] = cross_grads[FEATS : FEATS + 8, :WIDTH]
+
+
+def unpack(scalars, own, other):
+    whole = lambda *shape: pl.BlockSpec(shape, lambda g, s: (0,) * len(shape))
+    shapes = [
+        ((TABLES, N_DP, PART, WIDTH), bf16),
+        ((TABLES, ROWS), f32),
+        ((FEATS, RANK), f32),
+        ((FEATS, RANK), f32),
+        ((8, WIDTH), f32),
+    ]
+    return pl.pallas_call(
+        unpack_kernel,
+        grid_spec=pltpu.PrefetchScalarGridSpec(
+            num_scalar_prefetch=1,
+            grid=(1,),
+            in_specs=[whole(8, CHUNK, WIDTH), whole(8, CHUNK, WIDTH)],
+            out_specs=[whole(*shape) for shape, _ in shapes],
+            scratch_shapes=[
+                pltpu.VMEM((ROWS, WIDTH), f32),
+                pltpu.VMEM((N_DP * GRAD_ROWS, 2 * RANK), f32),
+            ],
+        ),
+        out_shape=[jax.ShapeDtypeStruct(shape, kind) for shape, kind in shapes],
+        compiler_params=pltpu.CompilerParams(vmem_limit_bytes=VMEM),
+        name="unpack",
+    )(scalars, own, other)
 
 
 def counts_of(words):
@@ -64,7 +198,9 @@
             row = ids[0]
             part = (row >> 4) & 15
             turn = (part & 1) ^ core
-            places[table] = turn * 4096 + (part >> 1) * 512 + (row >> 8) * 16 + (row & 15)
+            outer = (((part >> 1) & 1) << 2) | (part >> 2)
+            device = (((row >> 8) & 15) << 1) | (row >> 12)
+            places[table] = turn * 4096 + outer * 512 + device * 16 + (row & 15)
 
     rows = jnp.where(step < 8, own[0].astype(f32), other[0].astype(f32)).astype(bf16)
     for table in range(2):
@@ -110,7 +246,7 @@
         ),
         out_shape=[
             jax.ShapeDtypeStruct((FEATS, SAMPLES), bf16),
-            jax.ShapeDtypeStruct((2, N_DP, WORDS, SAMPLES), jnp.int32),
+            pltpu.HBM((2, N_DP, WORDS, SAMPLES), jnp.int32),
             jax.ShapeDtypeStruct((2 * RANK, SAMPLES), bf16),
         ],
         compiler_params=pltpu.CompilerParams(vmem_limit_bytes=VMEM),
@@ -150,7 +286,7 @@
         cross_grads[FEATS : FEATS + 8, :FEATS] = bias_sum[:8]
 
     turn = step // 8
-    part = 2 * (step - 8 * turn) + (turn ^ scalars[0])
+    part = part_of(step - 8 * turn, turn ^ scalars[0])
     result = lax.dot_general(grads[0], counts_of(words[0, 0]), NT_DIMS, preferred_element_type=f32)
     result = result + lax.dot_general(grads[1], counts_of(words[1, 0]), NT_DIMS, preferred_element_type=f32)
     extra = cross_grads[pl.ds(pl.multiple_of(part * GRAD_ROWS, GRAD_ROWS), GRAD_ROWS), :]
@@ -213,25 +349,16 @@
     return lax.ppermute(x, "core", [(0, 1), (1, 0)])
 
 
-def in_order(own, other, core):
-    first = jnp.where(core == 0, own, other)
-    second = jnp.where(core == 0, other, own)
-    return jnp.stack([first, second], axis=1)
-
-
 def body(rows_in, accum, bag_ids, cross_v, cross_u, cross_bias, upstream):
-    block = lax.axis_index("row")
+    block = lax.axis_index("x_lo") * 16 + lax.axis_index("z")
     core = lax.axis_index("core")
-    part = lax.axis_index(DP_OUTER) * 2 + core
+    part = part_of(lax.axis_index(DP_OUTER), core)
     table_a = (block * FEATS) // WIDTH
     table_b = jnp.minimum(table_a + 1, TABLES - 1)
     n_a = jnp.minimum(FEATS, WIDTH * (table_a + 1) - FEATS * block)
 
-    my_rows = lax.dynamic_slice(rows_in, (0, part * PART, 0), (TABLES, PART, WIDTH))
-    my_accum = lax.dynamic_slice(accum, (0, part * PART), (TABLES, PART))
-
-    packed = my_rows.transpose(1, 0, 2).reshape(PART, N_ROW, FEATS).transpose(1, 0, 2)
-    mine = exchange(packed, "row").reshape(STEP_ROWS, FEATS).T
+    my_rows, packed = pack(jnp.stack([part]).astype(jnp.int32), rows_in)
+    mine = exchange(packed, ROW_AXES).reshape(STEP_ROWS, FEATS).T
     own = spread(mine, DP_OUTER, 8)
     other = to_other_core(own)
 
@@ -241,8 +368,8 @@
         scalars, bag_ids.transpose(1, 2, 0), own, other, cross_v, cross_u, upstream_t
     )
 
-    gathered = exchange(rank_parts.reshape(N_ROW, 16, SAMPLES), "row")
-    ranks = spread(jnp.sum(gathered.astype(f32), axis=0).astype(bf16), "row", N_ROW).reshape(2 * RANK, SAMPLES)
+    gathered = exchange(rank_parts.reshape(N_ROW, 16, SAMPLES), ROW_ALL)
+    ranks = spread(jnp.sum(gathered.astype(f32), axis=0).astype(bf16), ROW_ALL, N_ROW).reshape(2 * RANK, SAMPLES)
 
     scalars = jnp.stack([core, n_a]).astype(jnp.int32)
     crossed, own, other = backward(
@@ -251,56 +378,39 @@
 
     chip_sum = (own.astype(f32) + to_other_core(other).astype(f32)).astype(bf16)
     sums = jnp.sum(exchange(chip_sum, DP_OUTER).astype(f32), axis=0)
-    row_grad = sums[:FEATS].astype(bf16).T.reshape(N_ROW, PART, FEATS)
-    row_grad = exchange(row_grad, "row").transpose(1, 0, 2).reshape(PART, TABLES, WIDTH)
-    row_grad = row_grad.transpose(1, 0, 2).astype(f32)
-
-    accum_out = my_accum + jnp.mean(row_grad * row_grad, axis=2)
-    scale = lax.rsqrt(accum_out + epsilon)
-    rows_out = (my_rows.astype(f32) - learn_rate * row_grad * scale[:, :, None]).astype(bf16)
-
-    high = accum_out.astype(bf16)
-    rest = accum_out - high.astype(f32)
-    middle = rest.astype(bf16)
-    low = (rest - middle.astype(f32)).astype(bf16)
-    accum_terms = jnp.stack([high, middle, low, jnp.zeros_like(low)]).reshape(13, WIDTH)
-    cross_grads = sums[FEATS:].astype(bf16).reshape(32, WIDTH)
-    result = jnp.concatenate([rows_out.reshape(TABLES * PART, WIDTH), accum_terms, cross_grads], axis=0)
-    own = spread(result, DP_OUTER, 8)
-    result = in_order(own, to_other_core(own), core)
-
-    new_rows = result[:, :, :416].reshape(N_DP, TABLES, PART, WIDTH).transpose(1, 0, 2, 3).reshape(TABLES, ROWS, WIDTH)
-    terms = result[:, :, 416:429].reshape(N_DP, 4, TABLES, PART).astype(f32)
-    new_accum = (terms[:, 0] + terms[:, 1] + terms[:, 2]).transpose(1, 0, 2).reshape(TABLES, ROWS)
-    cross_grads = result[:, :, 429:].reshape(N_DP * GRAD_ROWS, 2 * RANK).astype(f32)
-    grad_u = cross_grads[:FEATS, :RANK]
-    grad_v = cross_grads[:FEATS, RANK:]
-    grad_bias = cross_grads[FEATS, :FEATS]
-    return (crossed.T, new_rows, new_accum, grad_v, grad_u, grad_bias)
+    row_grad = exchange(sums[:FEATS].astype(bf16).T.reshape(N_ROW, PART, FEATS), ROW_AXES)
+    my_accum = lax.dynamic_slice(accum, (0, part * PART), (TABLES, PART)).T
+
+    own = exchange(adagrad(row_grad, my_rows, my_accum, sums[FEATS:]), DP_OUTER)
+    new_rows, new_accum, grad_v, grad_u, grad_bias = unpack(
+        jnp.stack([core]).astype(jnp.int32), own, to_other_core(own)
+    )
+    return (crossed.T, new_rows.reshape(TABLES, ROWS, WIDTH), new_accum, grad_v, grad_u, grad_bias[0, :FEATS])
 
 
 def solution(mesh):
-    inner = Mesh(mesh.devices.reshape(4, 2, 2, N_ROW), DP_OUTER + ("core", "row"))
-    dp = DP_OUTER + ("core",)
+    inner = Mesh(mesh.devices.reshape(4, 2, 2, 2, 16), ("y", "x_hi", "core", "x_lo", "z"))
+    dp = ("y", "x_hi", "core")
+    row = ROW_ALL
     return jax.shard_map(
         body,
         mesh=inner,
         in_specs=(
-            P(None, "row", None),
-            P(None, "row"),
+            P(None, row, None),
+            P(None, row),
             P(dp, None, None),
-            P("row", None),
-            P("row", None),
-            P("row"),
-            P(dp, "row"),
+            P(row, None),
+            P(row, None),
+            P(row),
+            P(dp, row),
         ),
         out_specs=(
-            P(dp, "row"),
-            P(None, "row", None),
-            P(None, "row"),
-            P("row", None),
-            P("row", None),
-            P("row"),
+            P(dp, row),
+            P(None, row, None),
+            P(None, row),
+            P(row, None),
+            P(row, None),
+            P(row),
         ),
         check_vma=False,
     )

time: 248 us -> 232 us (0.935)
  local copies, waits for them, and re-layouts: 18.7 us -> 6.25 us
  other arithmetic: 6.67 us -> 0.62 us
  Pallas kernels: 24.7 us -> 28.8 us
    pallas_call x0 -> x3, Pallas kernels: none -> 4.93 us  [the longest x1 3.23 us: adagrad(): pl.pallas_call(adagrad_kernel, out_shape=jax.ShapeDtypeStruct((8, CHUNK,...]
    unnamed x28 -> x17, local copies, waits for them, and re-layouts: 7.6 us -> 3.75 us
    another operation x4 -> x0, other arithmetic: 3.09 us -> none  [the longest x2 3.01 us: in_order(): return jnp.stack([first, second], axis=1)]
    convert_element_type x5 -> x0, local copies, waits for them, and re-layouts: 2.69 us -> none  [the longest x1 2.3 us: body(): terms = result[:, :, 416:429].reshape(N_DP, 4, TABLES, PART).astype(f32)]
    transpose x6 -> x2, local copies, waits for them, and re-layouts: 3.41 us -> 0.78 us  [body(): sums[:FEATS].astype(bf16).T.reshape(N_ROW, PART, FEATS)]
where the time goes in v2:
time: 232 us
  blocking collectives  118 us (51%)
  waiting for transfers between devices  49.8 us (21%)
  Pallas kernels  28.8 us (12%)
  starting transfers between devices  27.6 us (12%)
  local copies, waits for them, and re-layouts  6.25 us (3%)
    all_to_all x5, blocking collectives, exchange(): return lax.all_to_all(x, axes, 0, 0, tiled=True)  118 us
    all_to_all x2, waiting for transfers between devices, exchange(): return lax.all_to_all(x, axes, 0, 0, tiled=True)  43.7 us
    ppermute x3, starting transfers between devices, to_other_core(): return lax.ppermute(x, 'core', [(0, 1), (1, 0)])  17.4 us
    pallas_call x1, Pallas kernels, forward(): pl.pallas_call(forward_kernel, grid_spec=pltpu.PrefetchScalarGridSpec(num...  13.8 us
    all_to_all x2, starting transfers between devices, exchange(): return lax.all_to_all(x, axes, 0, 0, tiled=True)  10.1 us
    pallas_call x1, Pallas kernels, backward(): pl.pallas_call(backward_kernel, grid_spec=pltpu.PrefetchScalarGridSpec(nu...  10.1 us
    ppermute x3, waiting for transfers between devices, to_other_core(): return lax.ppermute(x, 'core', [(0, 1), (1, 0)])  6.08 us
  transfers between devices with their start and end apart: 5, of which 5 were waited for; matrix products, arithmetic and copies ran while one was open for 0% of the time, Pallas kernels for 0%

profile of v2, /device:TPU:1, one launch (start us, length us, event | category | flops | bytes accessed | tf_op | source)
XLA Modules:
  0.0 231.7 jit_solution(13938861213664336868)
XLA Ops:
  0.6 0.0 copy-start
  0.7 0.0 copy-start.2
  0.7 1.4 copy-done.2
  2.1 0.2 pack_rows.1
  2.3 0.0 copy-start.3
  2.3 0.0 copy-start.4
  2.3 0.0 copy-start.5
  2.3 0.0 copy-start.6
  2.3 31.0 %all_to_all.35 = bf16[32,16,104]{2,1,0:T(8,128)(2,1)S(1)} all-to-all(bf16[32,16,104]{2,1,0:T(8,128)(2,1)S(1)} %get-tuple-element.19), channel_id=1, replica_groups=mesh['y'=4,'x_hi'=2,'core'=2,'x_lo'=2,'z'=16] {'z','x_lo'}, dimensions={0} | all-to-all | bytes 212992 | tf_op jit(solution)/shard_map/all_to_all | solution.py:341
  33.3 0.1 copy.17
  33.4 0.1 broadcast_in_dim.6
  33.5 17.5 %all_to_all.36.own = bf16[8,104,512]{2,1,0:T(8,128)(2,1)S(1)} all-to-all(bf16[8,104,512]{2,1,0:T(8,128)(2,1)S(1)} %broadcast_in_dim.6), channel_id=1, replica_groups=mesh['y'=4,'x_hi'=2,'core'=2,'x_lo'=2,'z'=16] {'x_hi','y'}, dimensions={0} | all-to-all | bytes 1703936 | tf_op jit(solution)/shard_map/all_to_all | solution.py:341
  51.0 6.7 %collective-permute-start = (bf16[8,104,512]{2,1,0:T(8,128)(2,1)S(1)}, bf16[8,104,512]{2,1,0:T(8,128)(2,1)S(1)}, u32[]{:S(2)}, u32[]{:S(2)}) collective-permute-start(bf16[8,104,512]{2,1,0:T(8,128)(2,1)S(1)} %all_to_all.36.own), channel_id=1, source_target_pairs={{0,32},{32,0},{1,33},{33,1},{2,34},{34,2},{3,35},{35,3},{4,36},{36... | collective-permute-start | bytes 2555912 | tf_op jit(solution)/shard_map/ppermute | solution.py:349
  57.7 0.1 pad_add_fusion.1.scalars
  57.8 1.9 collective-permute-done.other
  59.7 0.0 copy-done.3
  59.7 0.0 copy-done.4
  59.7 0.0 copy-done.5
  59.7 0.0 copy-done.6
  59.7 13.8 %bags_and_ranks.1 = (bf16[104,512]{1,0:T(8,128)(2,1)S(1)}, s32[2,16,64,512]{3,2,1,0:T(8,128)}, bf16[512,512]{1,0:T(8,128)(2,1)S(1)}) custom-call(s32[4]{0:T(128)S(1)} %pad_add_fusion.1.scalars, s32[26,8,512]{2,1,0:T(8,128)S(1)} %bitcast.21, s32[26,8,512]{2,1,0:T(8,128)S(1)} %bitcast.22, bf16[8,104,512]{2,1,0:T(8,128)(2,1)S(1)} %all_to_all.36.own, ...), custom_call_target="tpu_custom_call" | custom-call | tf_op jit(solution)/shard_map/bags_and_ranks/pallas_call | solution.py:223
  73.5 0.0 copy-start.7
  73.5 35.0 %all_to_all.37 = bf16[32,16,512]{2,1,0:T(8,128)(2,1)S(1)} all-to-all(bf16[32,16,512]{2,1,0:T(8,128)(2,1)S(1)} %bitcast.23), channel_id=1, replica_groups=mesh['y'=4,'x_hi'=2,'core'=2,'x_lo'=2,'z'=16] {'x_lo','z'}, dimensions={0} | all-to-all | bytes 1048576 | tf_op jit(solution)/shard_map/all_to_all | solution.py:341
  108.6 0.1 reduce_sum.21
  108.7 0.9 broadcast_in_dim.7
  109.5 5.5 %all-to-all-start.3 = ((bf16[32,16,512]{2,1,0:T(8,128)(2,1)}), bf16[32,16,512]{2,1,0:T(8,128)(2,1)S(1)}, u32[]{:S(2)}, u32[]{:S(2)}) async-start(bf16[32,16,512]{2,1,0:T(8,128)(2,1)} %broadcast_in_dim.7), calls=%async_computation.3 | async-start | bytes 1048576 | tf_op jit(solution)/shard_map/all_to_all | solution.py:341
  115.0 0.0 copy-done.7
  115.1 0.1 copy.18.bias
  115.2 0.1 pad_add_fusion.scalars
  115.2 30.1 %all-to-all-done.3 = bf16[32,16,512]{2,1,0:T(8,128)(2,1)S(1)} async-done(((bf16[32,16,512]{2,1,0:T(8,128)(2,1)}), bf16[32,16,512]{2,1,0:T(8,128)(2,1)S(1)}, u32[]{:S(2)}, u32[]{:S(2)}) %all-to-all-start.3) | async-done | bytes 524320 | tf_op jit(solution)/shard_map/all_to_all | solution.py:341
  145.3 0.0 copy-start.1
  145.3 2.2 copy-done.1
  147.5 10.1 %cross_and_row_grads.1 = (bf16[104,512]{1,0:T(8,128)(2,1)}, bf16[8,112,512]{2,1,0:T(8,128)(2,1)S(1)}, bf16[8,112,512]{2,1,0:T(8,128)(2,1)S(1)}) custom-call(s32[2]{0:T(128)S(1)} %pad_add_fusion.scalars, s32[2,16,64,512]{3,2,1,0:T(8,128)S(1)} %copy-done.1, bf16[512,512]{1,0:T(8,128)(2,1)S(1)} %bitcast.20, bf16[104,512]{1,0:T(8,128)(2,1)S(1)} %get-tuple-element.22.pooled_in, ...), custom_call_target="tpu_custom_call" | custom-call | tf_op jit(solution)/shard_map/cross_and_row_grads/pallas_call | solution.py:306
  157.5 4.1 %collective-permute-start.1 = (bf16[8,112,512]{2,1,0:T(8,128)(2,1)S(1)}, bf16[8,112,512]{2,1,0:T(8,128)(2,1)S(1)}, u32[]{:S(2)}, u32[]{:S(2)}) collective-permute-start(bf16[8,112,512]{2,1,0:T(8,128)(2,1)S(1)} %get-tuple-element.25), channel_id=1, source_target_pairs={{0,32},{32,0},{1,33},{33,1},{2,34},{34,2},{3,35},{35,3},{4,36},{36... | collective-permute-start | bytes 2752520 | tf_op jit(solution)/shard_map/ppermute | solution.py:349
  161.7 2.1 collective-permute-done.1
  163.7 0.2 add_convert_fusion
  164.0 17.6 %all_to_all.38 = bf16[8,112,512]{2,1,0:T(8,128)(2,1)S(1)} all-to-all(bf16[8,112,512]{2,1,0:T(8,128)(2,1)S(1)} %add_convert_fusion), channel_id=1, replica_groups=mesh['y'=4,'x_hi'=2,'core'=2,'x_lo'=2,'z'=16] {'x_hi','y'}, dimensions={0} | all-to-all | bytes 1835008 | tf_op jit(solution)/shard_map/all_to_all | solution.py:341
  181.6 0.1 convert_reduce_fusion
  181.8 0.8 copy.19
  182.5 4.6 %all-to-all-start.5 = ((bf16[32,16,104]{2,1,0:T(8,128)(2,1)}), bf16[32,16,104]{2,1,0:T(8,128)(2,1)S(1)}, u32[]{:S(2)}, u32[]{:S(2)}) async-start(bf16[32,16,104]{2,1,0:T(8,128)(2,1)} %bitcast.14), calls=%async_computation.5 | async-start | bytes 262144 | tf_op jit(solution)/shard_map/all_to_all | solution.py:341
  187.1 0.0 copy-done
  187.2 0.1 constant_dynamic-slice_fusion
  187.2 0.1 copy.21
  187.3 13.6 %all-to-all-done.5.grads = bf16[32,16,104]{2,1,0:T(8,128)(2,1)S(1)} async-done(((bf16[32,16,104]{2,1,0:T(8,128)(2,1)}), bf16[32,16,104]{2,1,0:T(8,128)(2,1)S(1)}, u32[]{:S(2)}, u32[]{:S(2)}) %all-to-all-start.5) | async-done | bytes 106528 | tf_op jit(solution)/shard_map/all_to_all | solution.py:341
  201.0 3.2 %adagrad.1 = bf16[8,464,128]{2,1,0:T(8,128)(2,1)S(1)} custom-call(bf16[32,16,104]{2,1,0:T(8,128)(2,1)S(1)} %all-to-all-done.5.grads, bf16[26,16,128]{2,1,0:T(8,128)(2,1)S(1)} %get-tuple-element.26.rows, f32[16,26]{1,0:T(8,128)S(1)} %bitcast.26, f32[8,512]{1,0:T(8,128)S(1)} %slice.14.cross_grads), custom_call_target="tpu_custom_call" | custom-call | tf_op jit(solution)/shard_map/adagrad/pallas_call | solution.py:106
  204.2 16.7 %all_to_all.39.own = bf16[8,464,128]{2,1,0:T(8,128)(2,1)S(1)} all-to-all(bf16[8,464,128]{2,1,0:T(8,128)(2,1)S(1)} %adagrad.1), channel_id=1, replica_groups=mesh['y'=4,'x_hi'=2,'core'=2,'x_lo'=2,'z'=16] {'x_hi','y'}, dimensions={0} | all-to-all | bytes 1900544 | tf_op jit(solution)/shard_map/all_to_all | solution.py:341
  220.9 6.6 %collective-permute-start.2 = (bf16[8,464,128]{2,1,0:T(8,128)(2,1)S(1)}, bf16[8,464,128]{2,1,0:T(8,128)(2,1)S(1)}, u32[]{:S(2)}, u32[]{:S(2)}) collective-permute-start(bf16[8,464,128]{2,1,0:T(8,128)(2,1)S(1)} %all_to_all.39.own), channel_id=1, source_target_pairs={{0,32},{32,0},{1,33},{33,1},{2,34},{34,2},{3,35},{35,3},{4,36},{36... | collective-permute-start | bytes 2850824 | tf_op jit(solution)/shard_map/ppermute | solution.py:349
  227.6 2.1 collective-permute-done.2.other
  229.7 1.5 unpack.1
  231.2 0.5 slice_bitcast_fusion
  (2 shorter events, 0.0 us)
Async XLA Ops:
  0.6 186.5 %copy-start = (f32[26,256]{1,0:T(8,128)S(1)}, f32[26,256]{1,0:T(8,128)}, u32[]{:S(2)}) copy-start(f32[26,256]{1,0:T(8,128)} %param.8) | copy-start | bytes 79876
  0.7 1.5 copy-start.2
  2.3 57.4 %copy-start.3 = (s32[512,26,8]{0,2,1:T(8,128)S(1)}, s32[512,26,8]{0,2,1:T(8,128)}, u32[]{:S(2)}) copy-start(s32[512,26,8]{0,2,1:T(8,128)} %param.9) | copy-start | bytes 1277956
  2.3 57.4 %copy-start.4 = (bf16[512,104]{0,1:T(8,128)(2,1)S(1)}, bf16[512,104]{0,1:T(8,128)(2,1)}, u32[]{:S(2)}) copy-start(bf16[512,104]{0,1:T(8,128)(2,1)} %param.13) | copy-start | bytes 319492
  2.3 57.4 %copy-start.5 = (bf16[104,256]{1,0:T(8,128)(2,1)S(1)}, bf16[104,256]{1,0:T(8,128)(2,1)}, u32[]{:S(2)}) copy-start(bf16[104,256]{1,0:T(8,128)(2,1)} %v.3) | copy-start | bytes 159748
  2.3 57.4 %copy-start.6 = (bf16[104,256]{1,0:T(8,128)(2,1)S(1)}, bf16[104,256]{1,0:T(8,128)(2,1)}, u32[]{:S(2)}) copy-start(bf16[104,256]{1,0:T(8,128)(2,1)} %u.3) | copy-start | bytes 159748
  51.0 8.7 %collective-permute-start = (bf16[8,104,512]{2,1,0:T(8,128)(2,1)S(1)}, bf16[8,104,512]{2,1,0:T(8,128)(2,1)S(1)}, u32[]{:S(2)}, u32[]{:S(2)}) collective-permute-start(bf16[8,104,512]{2,1,0:T(8,128)(2,1)S(1)} %all_to_all.36.own), channel_id=1, source_target_pairs={{0,32},{32,0},{1,33},{33,1},{2,34},{34,2},{3,35},{35,3},{4,36},{36... | collective-permute-start | bytes 2555912 | tf_op jit(solution)/shard_map/ppermute | solution.py:349
  73.5 41.5 %copy-start.7 = (f32[104]{0:T(128)S(1)}, f32[104]{0:T(128)}, u32[]{:S(2)}) copy-start(f32[104]{0:T(128)} %param.12) | copy-start | bytes 1252
  109.5 35.8 %all-to-all-start.3 = ((bf16[32,16,512]{2,1,0:T(8,128)(2,1)}), bf16[32,16,512]{2,1,0:T(8,128)(2,1)S(1)}, u32[]{:S(2)}, u32[]{:S(2)}) async-start(bf16[32,16,512]{2,1,0:T(8,128)(2,1)} %broadcast_in_dim.7), calls=%async_computation.3 | async-start | bytes 1048576 | tf_op jit(solution)/shard_map/all_to_all | solution.py:341
  145.3 2.2 copy-start.1
  157.5 6.2 %collective-permute-start.1 = (bf16[8,112,512]{2,1,0:T(8,128)(2,1)S(1)}, bf16[8,112,512]{2,1,0:T(8,128)(2,1)S(1)}, u32[]{:S(2)}, u32[]{:S(2)}) collective-permute-start(bf16[8,112,512]{2,1,0:T(8,128)(2,1)S(1)} %get-tuple-element.25), channel_id=1, source_target_pairs={{0,32},{32,0},{1,33},{33,1},{2,34},{34,2},{3,35},{35,3},{4,36},{36... | collective-permute-start | bytes 2752520 | tf_op jit(solution)/shard_map/ppermute | solution.py:349
  182.5 18.4 %all-to-all-start.5 = ((bf16[32,16,104]{2,1,0:T(8,128)(2,1)}), bf16[32,16,104]{2,1,0:T(8,128)(2,1)S(1)}, u32[]{:S(2)}, u32[]{:S(2)}) async-start(bf16[32,16,104]{2,1,0:T(8,128)(2,1)} %bitcast.14), calls=%async_computation.5 | async-start | bytes 262144 | tf_op jit(solution)/shard_map/all_to_all | solution.py:341
  220.9 8.8 %collective-permute-start.2 = (bf16[8,464,128]{2,1,0:T(8,128)(2,1)S(1)}, bf16[8,464,128]{2,1,0:T(8,128)(2,1)S(1)}, u32[]{:S(2)}, u32[]{:S(2)}) collective-permute-start(bf16[8,464,128]{2,1,0:T(8,128)(2,1)S(1)} %all_to_all.39.own), channel_id=1, source_target_pairs={{0,32},{32,0},{1,33},{33,1},{2,34},{34,2},{3,35},{35,3},{4,36},{36... | collective-permute-start | bytes 2850824 | tf_op jit(solution)/shard_map/ppermute | solution.py:349

commit v3 on v2

--- a/solution.py
+++ b/solution.py
@@ -15,6 +15,7 @@
 N_ROW, N_DP, PART = 32, 16, 16
 STEP_ROWS = N_ROW * PART
 WORDS = STEP_ROWS // 8
+HALF = SAMPLES // 2
 GRAD_ROWS = 8
 OUT_ROWS = FEATS + GRAD_ROWS
 DP_OUTER = ("x_hi", "y")
@@ -69,7 +70,6 @@
             jax.ShapeDtypeStruct((TABLES, PART, WIDTH), bf16),
             jax.ShapeDtypeStruct((N_ROW, PART, FEATS), bf16),
         ],
-        compiler_params=pltpu.CompilerParams(vmem_limit_bytes=VMEM),
         name="pack_rows",
     )(scalars, rows)
 
@@ -160,7 +160,7 @@
 
 def counts_of(words):
     columns = []
-    for lane in range(0, SAMPLES, 128):
+    for lane in range(0, words.shape[1], 128):
         blocks = []
         for group in range(0, WORDS, 8):
             word = words[group : group + 8, lane : lane + 128]
@@ -185,78 +185,109 @@
     return jnp.concatenate(columns, axis=1)
 
 
-def forward_kernel(
-    scalars, ids_a, ids_b, own, other, v, u, upstream, pooled_out, words_out, ranks_out, places, total
-):
+def whole(*shape):
+    return pl.BlockSpec(shape, lambda g, s: (0,) * len(shape))
+
+
+def words_kernel(scalars, ids_a, ids_b, words, places):
     step = pl.program_id(0)
-    core = scalars[2]
+
+    @pl.when(step == 0)
+    def _():
+        for table, ids in enumerate((ids_a, ids_b)):
+            row = ids[0]
+            part = (row >> 4) & 15
+            turn = (part & 1) ^ scalars[2]
+            outer = (((part >> 1) & 1) << 2) | (part >> 2)
+            device = (((row >> 8) & 15) << 1) | (row >> 12)
+            places[table] = turn * 4096 + outer * 512 + device * 16 + (row & 15)
+
+    for table in range(2):
+        for turn in range(2):
+            words[table, turn, 0] = words_of(places[table] - (turn * 8 + step) * STEP_ROWS)
+
+
+def bag_words(scalars, ids):
+    return pl.pallas_call(
+        words_kernel,
+        grid_spec=pltpu.PrefetchScalarGridSpec(
+            num_scalar_prefetch=1,
+            grid=(8,),
+            in_specs=[
+                pl.BlockSpec((1, BAG, SAMPLES), lambda g, s: (s[0], 0, 0)),
+                pl.BlockSpec((1, BAG, SAMPLES), lambda g, s: (s[1], 0, 0)),
+            ],
+            out_specs=[pl.BlockSpec((2, 2, 1, WORDS, SAMPLES), lambda g, s: (0, 0, g, 0, 0))],
+            scratch_shapes=[pltpu.VMEM((2, BAG, SAMPLES), jnp.int32)],
+        ),
+        out_shape=[jax.ShapeDtypeStruct((2, 2, 8, WORDS, SAMPLES), jnp.int32)],
+        compiler_params=pltpu.CompilerParams(vmem_limit_bytes=VMEM),
+        cost_estimate=pl.CostEstimate(flops=1 << 28, bytes_accessed=5 << 20, transcendentals=0),
+        name="bag_words",
+    )(scalars, ids, ids)[0]
+
+
+WORD_BLOCK = pl.BlockSpec((2, 2, 1, WORDS, HALF), lambda g, s: (0, 0, g, 0, s[0]))
+HALF_BLOCK = pl.BlockSpec((FEATS, HALF), lambda g, s: (0, s[0]))
+KERNEL_COST = pl.CostEstimate(flops=1 << 32, bytes_accessed=5 << 20, transcendentals=0)
+
+
+def forward_kernel(scalars, words, own, other, v, u, upstream, pooled_out, ranks_out, total):
+    step = pl.program_id(0)
 
     @pl.when(step == 0)
     def _():
         total[...] = jnp.zeros_like(total)
-        for table, ids in enumerate((ids_a, ids_b)):
-            row = ids[0]
-            part = (row >> 4) & 15
-            turn = (part & 1) ^ core
-            outer = (((part >> 1) & 1) << 2) | (part >> 2)
-            device = (((row >> 8) & 15) << 1) | (row >> 12)
-            places[table] = turn * 4096 + outer * 512 + device * 16 + (row & 15)
-
-    rows = jnp.where(step < 8, own[0].astype(f32), other[0].astype(f32)).astype(bf16)
+
     for table in range(2):
-        words = words_of(places[table] - step * STEP_ROWS)
-        words_out[table, 0] = words
-        total[table] += jnp.dot(rows, counts_of(words), preferred_element_type=f32)
-
-    @pl.when(step == N_DP - 1)
+        total[table] += jnp.dot(own[0], counts_of(words[table, 0, 0]), preferred_element_type=f32) + jnp.dot(
+            other[0], counts_of(words[table, 1, 0]), preferred_element_type=f32
+        )
+
+    @pl.when(step == 7)
     def _():
-        feature = lax.broadcasted_iota(jnp.int32, (FEATS, SAMPLES), 0)
-        pooled = jnp.where(feature < scalars[3], total[0], total[1]).astype(bf16)
+        feature = lax.broadcasted_iota(jnp.int32, (FEATS, HALF), 0)
+        pooled = jnp.where(feature < scalars[1], total[0], total[1]).astype(bf16)
         pooled_out[...] = pooled
         gate_grad = (upstream[...].astype(f32) * pooled.astype(f32)).astype(bf16)
         ranks_out[:RANK] = lax.dot_general(v[...], pooled, TN_DIMS, preferred_element_type=f32).astype(bf16)
         ranks_out[RANK:] = lax.dot_general(u[...], gate_grad, TN_DIMS, preferred_element_type=f32).astype(bf16)
 
 
-def forward(scalars, ids, own, other, v, u, upstream):
-    whole = lambda *shape: pl.BlockSpec(shape, lambda g, s: (0,) * len(shape))
+def forward(scalars, words, own, other, v, u, upstream):
     return pl.pallas_call(
         forward_kernel,
         grid_spec=pltpu.PrefetchScalarGridSpec(
             num_scalar_prefetch=1,
-            grid=(N_DP,),
+            grid=(8,),
             in_specs=[
-                pl.BlockSpec((1, BAG, SAMPLES), lambda g, s: (s[0], 0, 0)),
-                pl.BlockSpec((1, BAG, SAMPLES), lambda g, s: (s[1], 0, 0)),
-                pl.BlockSpec((1, FEATS, STEP_ROWS), lambda g, s: (jnp.minimum(g, 7), 0, 0)),
-                pl.BlockSpec((1, FEATS, STEP_ROWS), lambda g, s: (jnp.maximum(g - 8, 0), 0, 0)),
+                WORD_BLOCK,
+                pl.BlockSpec((1, FEATS, STEP_ROWS), lambda g, s: (g, 0, 0)),
+                pl.BlockSpec((1, FEATS, STEP_ROWS), lambda g, s: (g, 0, 0)),
                 whole(FEATS, RANK),
                 whole(FEATS, RANK),
-                whole(FEATS, SAMPLES),
+                HALF_BLOCK,
             ],
-            out_specs=[
-                whole(FEATS, SAMPLES),
-                pl.BlockSpec((2, 1, WORDS, SAMPLES), lambda g, s: (0, g, 0, 0)),
-                whole(2 * RANK, SAMPLES),
-            ],
-            scratch_shapes=[
-                pltpu.VMEM((2, BAG, SAMPLES), jnp.int32),
-                pltpu.VMEM((2, FEATS, SAMPLES), f32),
-            ],
+            out_specs=[whole(FEATS, HALF), whole(2 * RANK, HALF)],
+            scratch_shapes=[pltpu.VMEM((2, FEATS, HALF), f32)],
         ),
         out_shape=[
-            jax.ShapeDtypeStruct((FEATS, SAMPLES), bf16),
-            pltpu.HBM((2, N_DP, WORDS, SAMPLES), jnp.int32),
-            jax.ShapeDtypeStruct((2 * RANK, SAMPLES), bf16),
+            jax.ShapeDtypeStruct((FEATS, HALF), bf16),
+            jax.ShapeDtypeStruct((2 * RANK, HALF), bf16),
         ],
         compiler_params=pltpu.CompilerParams(vmem_limit_bytes=VMEM),
+        cost_estimate=KERNEL_COST,
         name="bags_and_ranks",
-    )(scalars, ids, ids, own, other, v, u, upstream)
-
-
-def backward_kernel(
-    scalars, words, ranks, pooled_in, v, u, bias, upstream_in, crossed_out, own_out, other_out, grads, cross_grads
-):
+    )(scalars, words, own, other, v, u, upstream)
+
+
+def backward_kernel(scalars, words, ranks, pooled_in, v, u, bias, upstream_in, *refs):
+    if len(refs) == 5:
+        sums_in = None
+        crossed_out, own_out, other_out, grads, cross_grads = refs
+    else:
+        own_in, other_in, _, crossed_out, own_out, other_out, grads, cross_grads = refs
+        sums_in = (own_in, other_in)
     step = pl.program_id(0)
 
     @pl.when(step == 0)
@@ -270,7 +301,7 @@
         crossed_out[...] = (pooled * gate + pooled).astype(bf16)
         back = jnp.dot(v[...], rank_grad, preferred_element_type=f32)
         grad = (upstream * (gate + 1.0) + back).astype(bf16).astype(f32)
-        feature = lax.broadcasted_iota(jnp.int32, (FEATS, SAMPLES), 0)
+        feature = lax.broadcasted_iota(jnp.int32, (FEATS, HALF), 0)
         grads[0] = jnp.where(feature < scalars[1], grad, 0.0).astype(bf16)
         grads[1] = jnp.where(feature < scalars[1], 0.0, grad).astype(bf16)
         gate_grad = upstream * pooled
@@ -279,62 +310,66 @@
         cross_grads[...] = jnp.zeros_like(cross_grads)
         cross_grads[:FEATS, :RANK] = lax.dot_general(gate_bf, rank, NT_DIMS, preferred_element_type=f32)
         cross_grads[:FEATS, RANK:] = lax.dot_general(pooled_bf, rank_grad, NT_DIMS, preferred_element_type=f32)
-        ones = jnp.ones((16, SAMPLES), bf16)
+        ones = jnp.ones((16, HALF), bf16)
         bias_sum = lax.dot_general(ones, gate_bf, NT_DIMS, preferred_element_type=f32) + lax.dot_general(
             ones, gate_rest, NT_DIMS, preferred_element_type=f32
         )
         cross_grads[FEATS : FEATS + 8, :FEATS] = bias_sum[:8]
 
-    turn = step // 8
-    part = part_of(step - 8 * turn, turn ^ scalars[0])
-    result = lax.dot_general(grads[0], counts_of(words[0, 0]), NT_DIMS, preferred_element_type=f32)
-    result = result + lax.dot_general(grads[1], counts_of(words[1, 0]), NT_DIMS, preferred_element_type=f32)
-    extra = cross_grads[pl.ds(pl.multiple_of(part * GRAD_ROWS, GRAD_ROWS), GRAD_ROWS), :]
-    block = jnp.concatenate([result, extra], axis=0).astype(bf16)
-
-    @pl.when(turn == 0)
-    def _():
-        own_out[0] = block
-
-    @pl.when(turn == 1)
-    def _():
-        other_out[0] = block
-
-
-def backward(scalars, words, ranks, pooled, v, u, bias, upstream):
-    whole = lambda *shape: pl.BlockSpec(shape, lambda g, s: (0,) * len(shape))
+    for turn, out in enumerate((own_out, other_out)):
+        part = part_of(step, turn ^ scalars[2])
+        result = lax.dot_general(grads[0], counts_of(words[0, turn, 0]), NT_DIMS, preferred_element_type=f32)
+        result = result + lax.dot_general(
+            grads[1], counts_of(words[1, turn, 0]), NT_DIMS, preferred_element_type=f32
+        )
+        extra = cross_grads[pl.ds(pl.multiple_of(part * GRAD_ROWS, GRAD_ROWS), GRAD_ROWS), :]
+        block = jnp.concatenate([result, extra], axis=0)
+        if sums_in is not None:
+            block = block + sums_in[turn][0]
+        out[0] = block.astype(out.dtype)
+
+
+def backward(scalars, words, ranks, pooled, v, u, bias, upstream, before=None):
+    sums = pl.BlockSpec((1, OUT_ROWS, STEP_ROWS), lambda g, s: (g, 0, 0))
+    kind = f32 if before is None else bf16
+    operands = [scalars, words, ranks, pooled, v, u, bias, upstream]
+    in_specs = [
+        WORD_BLOCK,
+        whole(2 * RANK, HALF),
+        whole(FEATS, HALF),
+        whole(FEATS, RANK),
+        whole(FEATS, RANK),
+        whole(FEATS, 1),
+        HALF_BLOCK,
+    ]
+    aliases = {}
+    if before is not None:
+        crossed, own, other = before
+        operands += [own, other, crossed]
+        in_specs += [sums, sums, pl.BlockSpec(memory_space=pl.ANY)]
+        aliases = {len(operands) - 1: 0}
     return pl.pallas_call(
         backward_kernel,
         grid_spec=pltpu.PrefetchScalarGridSpec(
             num_scalar_prefetch=1,
-            grid=(N_DP,),
-            in_specs=[
-                pl.BlockSpec((2, 1, WORDS, SAMPLES), lambda g, s: (0, g, 0, 0)),
-                whole(2 * RANK, SAMPLES),
-                whole(FEATS, SAMPLES),
-                whole(FEATS, RANK),
-                whole(FEATS, RANK),
-                whole(FEATS, 1),
-                whole(FEATS, SAMPLES),
-            ],
-            out_specs=[
-                whole(FEATS, SAMPLES),
-                pl.BlockSpec((1, OUT_ROWS, STEP_ROWS), lambda g, s: (jnp.minimum(g, 7), 0, 0)),
-                pl.BlockSpec((1, OUT_ROWS, STEP_ROWS), lambda g, s: (jnp.maximum(g - 8, 0), 0, 0)),
-            ],
+            grid=(8,),
+            in_specs=in_specs,
+            out_specs=[HALF_BLOCK, sums, sums],
             scratch_shapes=[
-                pltpu.VMEM((2, FEATS, SAMPLES), bf16),
+                pltpu.VMEM((2, FEATS, HALF), bf16),
                 pltpu.VMEM((N_DP * GRAD_ROWS, 2 * RANK), f32),
             ],
         ),
         out_shape=[
             jax.ShapeDtypeStruct((FEATS, SAMPLES), bf16),
-            jax.ShapeDtypeStruct((8, OUT_ROWS, STEP_ROWS), bf16),
-            jax.ShapeDtypeStruct((8, OUT_ROWS, STEP_ROWS), bf16),
+            jax.ShapeDtypeStruct((8, OUT_ROWS, STEP_ROWS), kind),
+            jax.ShapeDtypeStruct((8, OUT_ROWS, STEP_ROWS), kind),
         ],
+        input_output_aliases=aliases,
         compiler_params=pltpu.CompilerParams(vmem_limit_bytes=VMEM),
+        cost_estimate=KERNEL_COST,
         name="cross_and_row_grads",
-    )(scalars, words, ranks, pooled, v, u, bias, upstream)
+    )(*operands)
 
 
 def exchange(x, axes):
@@ -345,8 +380,12 @@
     return exchange(jnp.broadcast_to(x, (count,) + x.shape), axes)
 
 
+def swap(x, axis):
+    return lax.ppermute(x, axis, [(0, 1), (1, 0)])
+
+
 def to_other_core(x):
-    return lax.ppermute(x, "core", [(0, 1), (1, 0)])
+    return swap(x, "core")
 
 
 def body(rows_in, accum, bag_ids, cross_v, cross_u, cross_bias, upstream):
@@ -363,17 +402,23 @@
     other = to_other_core(own)
 
     upstream_t = upstream.T
-    scalars = jnp.stack([table_a, table_b, core, n_a]).astype(jnp.int32)
-    pooled, words, rank_parts = forward(
-        scalars, bag_ids.transpose(1, 2, 0), own, other, cross_v, cross_u, upstream_t
-    )
-
-    gathered = exchange(rank_parts.reshape(N_ROW, 16, SAMPLES), ROW_ALL)
-    ranks = spread(jnp.sum(gathered.astype(f32), axis=0).astype(bf16), ROW_ALL, N_ROW).reshape(2 * RANK, SAMPLES)
-
-    scalars = jnp.stack([core, n_a]).astype(jnp.int32)
+    keep = lax.axis_index("x_lo")
+    scalars = jnp.stack([table_a, table_b, core]).astype(jnp.int32)
+    words = bag_words(scalars, bag_ids.transpose(1, 2, 0))
+    at_keep = jnp.stack([keep, n_a, core]).astype(jnp.int32)
+    at_sent = jnp.stack([1 - keep, n_a, core]).astype(jnp.int32)
+    sent_pooled, sent_ranks = forward(at_sent, words, own, other, cross_v, cross_u, upstream_t)
+    kept_pooled, kept_ranks = forward(at_keep, words, own, other, cross_v, cross_u, upstream_t)
+
+    kept_ranks = (kept_ranks.astype(f32) + swap(sent_ranks, "x_lo").astype(f32)).astype(bf16)
+    gathered = exchange(kept_ranks.reshape(16, 32, HALF), "z")
+    ranks = spread(jnp.sum(gathered.astype(f32), axis=0).astype(bf16), "z", 16).reshape(2 * RANK, HALF)
+    sent_ranks = swap(ranks, "x_lo")
+
+    bias = cross_bias.reshape(FEATS, 1)
+    half = backward(at_keep, words, ranks, kept_pooled, cross_v, cross_u, bias, upstream_t)
     crossed, own, other = backward(
-        scalars, words, ranks, pooled, cross_v, cross_u, cross_bias.reshape(FEATS, 1), upstream_t
+        at_sent, words, sent_ranks, sent_pooled, cross_v, cross_u, bias, upstream_t, half
     )
 
     chip_sum = (own.astype(f32) + to_other_core(other).astype(f32)).astype(bf16)

time: 232 us -> 217 us (0.935)
  blocking collectives: 118 us -> 100 us
  starting transfers between devices: 27.6 us -> 44.5 us
  waiting for transfers between devices: 49.8 us -> 32.9 us
  Pallas kernels: 28.8 us -> 32 us
    all_to_all x5, blocking collectives: 118 us -> 100 us  [exchange(): return lax.all_to_all(x, axes, 0, 0, tiled=True)]
    all_to_all x2, waiting for transfers between devices: 43.7 us -> 26.4 us  [exchange(): return lax.all_to_all(x, axes, 0, 0, tiled=True)]
    ppermute x3 -> x5, starting transfers between devices: 17.4 us -> 27.2 us  [swap(): return lax.ppermute(x, axis, [(0, 1), (1, 0)])]
    all_to_all x2, starting transfers between devices: 10.1 us -> 17.4 us  [exchange(): return lax.all_to_all(x, axes, 0, 0, tiled=True)]
    pallas_call x0 -> x1, Pallas kernels: none -> 5.58 us  [bag_words(): pl.pallas_call(words_kernel, grid_spec=pltpu.PrefetchScalarGridSpec(num_s...]
    pallas_call x1 -> x2, Pallas kernels: 13.8 us -> 8.94 us  [forward(): pl.pallas_call(forward_kernel, grid_spec=pltpu.PrefetchScalarGridSpec(num...]
    pallas_call x1 -> x2, Pallas kernels: 10.1 us -> 11 us  [backward(): pl.pallas_call(backward_kernel, grid_spec=pltpu.PrefetchScalarGridSpec(nu...]
    ppermute x3 -> x5, waiting for transfers between devices: 6.08 us -> 6.54 us  [swap(): return lax.ppermute(x, axis, [(0, 1), (1, 0)])]
  transfers between devices with their start and end apart: 5 -> 7, of which waited for: 5 -> 5; matrix products, arithmetic and copies ran while one was open for 0% -> 0% of each run, Pallas kernels for 0% -> 7%
where the time goes in v3:
time: 217 us; the launch traced here: 216 us
  blocking collectives  100 us (46%)
  starting transfers between devices  44.5 us (21%)
  waiting for transfers between devices  32.9 us (15%)
  Pallas kernels  32 us (15%)
  local copies, waits for them, and re-layouts  4.67 us (2%)
    all_to_all x5, blocking collectives, exchange(): return lax.all_to_all(x, axes, 0, 0, tiled=True)  100 us
    ppermute x5, starting transfers between devices, swap(): return lax.ppermute(x, axis, [(0, 1), (1, 0)])  27.2 us
    all_to_all x2, waiting for transfers between devices, exchange(): return lax.all_to_all(x, axes, 0, 0, tiled=True)  26.4 us
    all_to_all x2, starting transfers between devices, exchange(): return lax.all_to_all(x, axes, 0, 0, tiled=True)  17.4 us
    pallas_call x2, Pallas kernels, backward(): pl.pallas_call(backward_kernel, grid_spec=pltpu.PrefetchScalarGridSpec(nu...  11 us
    pallas_call x2, Pallas kernels, forward(): pl.pallas_call(forward_kernel, grid_spec=pltpu.PrefetchScalarGridSpec(num...  8.94 us
    ppermute x5, waiting for transfers between devices, swap(): return lax.ppermute(x, axis, [(0, 1), (1, 0)])  6.54 us
    pallas_call x1, Pallas kernels, bag_words(): pl.pallas_call(words_kernel, grid_spec=pltpu.PrefetchScalarGridSpec(num_s...  5.58 us
  transfers between devices with their start and end apart: 7, of which 5 were waited for; matrix products, arithmetic and copies ran while one was open for 0% of the time, Pallas kernels for 7%

profile of v3, /device:TPU:1, one launch (start us, length us, event | category | flops | bytes accessed | tf_op | source)
XLA Modules:
  0.0 216.2 jit_solution(10172881271709556304)
XLA Ops:
  0.6 0.0 copy-start
  0.7 1.7 pack_rows.1
  2.4 0.0 copy-start.3
  2.4 31.1 %all_to_all.35 = bf16[32,16,104]{2,1,0:T(8,128)(2,1)S(1)} all-to-all(bf16[32,16,104]{2,1,0:T(8,128)(2,1)} %get-tuple-element.23), channel_id=1, replica_groups=mesh['y'=4,'x_hi'=2,'core'=2,'x_lo'=2,'z'=16] {'z','x_lo'}, dimensions={0} | all-to-all | bytes 212992 | tf_op jit(solution)/shard_map/all_to_all | solution.py:376
  33.5 0.1 copy.19
  33.6 0.1 broadcast_in_dim.6
  33.7 17.5 %all_to_all.36.own = bf16[8,104,512]{2,1,0:T(8,128)(2,1)S(1)} all-to-all(bf16[8,104,512]{2,1,0:T(8,128)(2,1)S(1)} %broadcast_in_dim.6), channel_id=1, replica_groups=mesh['y'=4,'x_hi'=2,'core'=2,'x_lo'=2,'z'=16] {'x_hi','y'}, dimensions={0} | all-to-all | bytes 1703936 | tf_op jit(solution)/shard_map/all_to_all | solution.py:376
  51.2 6.7 %collective-permute-start = (bf16[8,104,512]{2,1,0:T(8,128)(2,1)S(1)}, bf16[8,104,512]{2,1,0:T(8,128)(2,1)S(1)}, u32[]{:S(2)}, u32[]{:S(2)}) collective-permute-start(bf16[8,104,512]{2,1,0:T(8,128)(2,1)S(1)} %all_to_all.36.own), channel_id=1, source_target_pairs={{0,32},{32,0},{1,33},{33,1},{2,34},{34,2},{3,35},{35,3},{4,36},{36... | collective-permute-start | bytes 2555912 | tf_op jit(solution)/shard_map/ppermute | solution.py:384
  57.9 0.1 add_add_fusion
  58.0 0.0 copy-done.3
  58.0 0.0 copy-start.5
  58.0 0.0 copy-start.6
  58.0 0.0 copy-start.7
  58.0 5.6 %bag_words.1.words = s32[2,2,8,64,512]{4,3,2,1,0:T(8,128)S(1)} custom-call(s32[3]{0:T(128)S(1)} %get-tuple-element.41.scalars, s32[26,8,512]{2,1,0:T(8,128)S(1)} %bitcast.22, s32[26,8,512]{2,1,0:T(8,128)S(1)} %bitcast.23), custom_call_target="tpu_custom_call" | custom-call | flops 268435456 | bytes 5242880 | tf_op jit(solution)/shard_map/bag_words/pallas_call | solution.py:211
  63.6 0.0 copy-start.1
  63.6 0.1 add_add_fusion.2.scalars
  63.7 0.0 collective-permute-done.other
  63.7 0.0 copy-done.5
  63.7 0.0 copy-done.6
  63.7 0.0 copy-done.7
  63.7 4.5 %bags_and_ranks.3 = (bf16[104,256]{1,0:T(8,128)(2,1)S(1)}, bf16[512,256]{1,0:T(8,128)(2,1)S(1)}) custom-call(s32[3]{0:T(128)S(1)} %get-tuple-element.40.scalars, s32[2,2,8,64,512]{4,3,2,1,0:T(8,128)S(1)} %bag_words.1.words, bf16[8,104,512]{2,1,0:T(8,128)(2,1)S(1)} %all_to_all.36.own, bf16[8,104,512]{2,1,0:T(8,128)(2,1)S(1)} %collective-permute-done.other, ...), custom_call_target="tpu_custom_call" | custom-call | flops 4294967296 | bytes 5242880 | tf_op jit(solution)/shard_map/bags_and_ranks/pallas_call | solution.py:258
  68.2 3.0 %collective-permute-start.1 = (bf16[512,256]{1,0:T(8,128)(2,1)S(1)}, bf16[512,256]{1,0:T(8,128)(2,1)S(1)}, u32[]{:S(2)}, u32[]{:S(2)}) collective-permute-start(bf16[512,256]{1,0:T(8,128)(2,1)S(1)} %get-tuple-element.25), channel_id=1, source_target_pairs={{0,16},{16,0},{1,17},{17,1},{2,18},{18,2},{3,19},{19,3},{4,20},{20... | collective-permute-start | bytes 786440 | tf_op jit(solution)/shard_map/ppermute | solution.py:384
  71.2 0.0 copy-done.1
  71.2 4.5 %bags_and_ranks.2 = (bf16[104,256]{1,0:T(8,128)(2,1)S(1)}, bf16[512,256]{1,0:T(8,128)(2,1)S(1)}) custom-call(s32[3]{0:T(128)S(1)} %add_add_fusion.2.scalars, s32[2,2,8,64,512]{4,3,2,1,0:T(8,128)S(1)} %bag_words.1.words, bf16[8,104,512]{2,1,0:T(8,128)(2,1)S(1)} %all_to_all.36.own, bf16[8,104,512]{2,1,0:T(8,128)(2,1)S(1)} %collective-permute-done.other, ...), custom_call_target="tpu_custom_call" | custom-call | flops 4294967296 | bytes 5242880 | tf_op jit(solution)/shard_map/bags_and_ranks/pallas_call | solution.py:258
  75.7 0.0 copy-start.8
  75.7 2.3 %collective-permute-done.1 = bf16[512,256]{1,0:T(8,128)(2,1)S(1)} collective-permute-done((bf16[512,256]{1,0:T(8,128)(2,1)S(1)}, bf16[512,256]{1,0:T(8,128)(2,1)S(1)}, u32[]{:S(2)}, u32[]{:S(2)}) %collective-permute-start.1) | collective-permute-done | bytes 262176 | tf_op jit(solution)/shard_map/ppermute | solution.py:384
  78.0 0.1 add_convert_fusion.1
  78.1 16.9 %all_to_all.37 = bf16[16,32,256]{2,1,0:T(8,128)(2,1)S(1)} all-to-all(bf16[16,32,256]{2,1,0:T(8,128)(2,1)S(1)} %bitcast.31), channel_id=1, replica_groups=mesh['y'=4,'x_hi'=2,'core'=2,'x_lo'=2,'z'=16] {'z'}, dimensions={0} | all-to-all | bytes 524288 | tf_op jit(solution)/shard_map/all_to_all | solution.py:376
  95.1 0.7 broadcast_in_dim.7
  95.8 11.0 %all-to-all-start.3 = ((bf16[16,32,256]{2,1,0:T(8,128)(2,1)}), bf16[16,32,256]{2,1,0:T(8,128)(2,1)S(1)}, u32[]{:S(2)}, u32[]{:S(2)}) async-start(bf16[16,32,256]{2,1,0:T(8,128)(2,1)} %broadcast_in_dim.7), calls=%async_computation.3 | async-start | bytes 524288 | tf_op jit(solution)/shard_map/all_to_all | solution.py:376
  106.9 0.0 copy-done.8
  106.9 0.1 copy.21.bias
  107.0 12.9 %all-to-all-done.3 = bf16[16,32,256]{2,1,0:T(8,128)(2,1)S(1)} async-done(((bf16[16,32,256]{2,1,0:T(8,128)(2,1)}), bf16[16,32,256]{2,1,0:T(8,128)(2,1)S(1)}, u32[]{:S(2)}, u32[]{:S(2)}) %all-to-all-start.3) | async-done | bytes 262176 | tf_op jit(solution)/shard_map/all_to_all | solution.py:376
  119.9 2.3 %collective-permute-start.2 = (bf16[512,256]{1,0:T(8,128)(2,1)S(1)}, bf16[512,256]{1,0:T(8,128)(2,1)S(1)}, u32[]{:S(2)}, u32[]{:S(2)}) collective-permute-start(bf16[512,256]{1,0:T(8,128)(2,1)S(1)} %bitcast.24), channel_id=1, source_target_pairs={{0,16},{16,0},{1,17},{17,1},{2,18},{18,2},{3,19},{19,3},{4,20},{20... | collective-permute-start | bytes 786440 | tf_op jit(solution)/shard_map/ppermute | solution.py:384
  122.2 0.0 copy-start.2
  122.2 2.2 %copy-done.2 = s32[2,2,8,64,512]{4,3,2,1,0:T(8,128)S(1)} copy-done((s32[2,2,8,64,512]{4,3,2,1,0:T(8,128)S(1)}, s32[2,2,8,64,512]{4,3,2,1,0:T(8,128)}, u32[]{:S(2)}) %copy-start.2) | copy-done | bytes 4194328
  124.4 5.5 %cross_and_row_grads.2 = (bf16[104,512]{1,0:T(8,128)(2,1)}, f32[8,112,512]{2,1,0:T(8,128)S(1)}, f32[8,112,512]{2,1,0:T(8,128)S(1)}) custom-call(s32[3]{0:T(128)S(1)} %add_add_fusion.2.scalars, s32[2,2,8,64,512]{4,3,2,1,0:T(8,128)S(1)} %copy-done.2, bf16[512,256]{1,0:T(8,128)(2,1)S(1)} %bitcast.25, bf16[104,256]{1,0:T(8,128)(2,1)S(1)} %get-tuple-element.27.pooled_in, ...), custom_call_target="tpu_custom_call" | custom-call | flops 4294967296 | bytes 5242880 | tf_op jit(solution)/shard_map/cross_and_row_grads/pallas_call | solution.py:351
  129.9 0.0 collective-permute-done.2.ranks
  129.9 5.5 %cross_and_row_grads.3 = (bf16[104,512]{1,0:T(8,128)(2,1)}, bf16[8,112,512]{2,1,0:T(8,128)(2,1)S(1)}, bf16[8,112,512]{2,1,0:T(8,128)(2,1)S(1)}) custom-call(s32[3]{0:T(128)S(1)} %get-tuple-element.40.scalars, s32[2,2,8,64,512]{4,3,2,1,0:T(8,128)S(1)} %copy-done.2, ...), custom_call_target="tpu_custom_call", output_to_operand_aliasing={{0}: (10, {})} | custom-call | flops 4294967296 | bytes 5242880 | tf_op jit(solution)/shard_map/cross_and_row_grads/pallas_call | solution.py:351
  135.4 8.5 %collective-permute-start.3 = (bf16[8,112,512]{2,1,0:T(8,128)(2,1)S(1)}, bf16[8,112,512]{2,1,0:T(8,128)(2,1)S(1)}, u32[]{:S(2)}, u32[]{:S(2)}) collective-permute-start(bf16[8,112,512]{2,1,0:T(8,128)(2,1)S(1)} %get-tuple-element.33), channel_id=1, source_target_pairs={{0,32},{32,0},{1,33},{33,1},{2,34},{34,2},{3,35},{35,3},{4,36},{36... | collective-permute-start | bytes 2752520 | tf_op jit(solution)/shard_map/ppermute | solution.py:384
  144.0 2.1 collective-permute-done.3
  146.1 0.3 add_convert_fusion
  146.3 0.0 copy-start.4
  146.4 17.7 %all_to_all.38 = bf16[8,112,512]{2,1,0:T(8,128)(2,1)S(1)} all-to-all(bf16[8,112,512]{2,1,0:T(8,128)(2,1)S(1)} %add_convert_fusion), channel_id=1, replica_groups=mesh['y'=4,'x_hi'=2,'core'=2,'x_lo'=2,'z'=16] {'x_hi','y'}, dimensions={0} | all-to-all | bytes 1835008 | tf_op jit(solution)/shard_map/all_to_all | solution.py:376
  164.1 0.1 convert_reduce_fusion
  164.3 0.8 copy.22
  165.0 6.3 %all-to-all-start.5 = ((bf16[32,16,104]{2,1,0:T(8,128)(2,1)}), bf16[32,16,104]{2,1,0:T(8,128)(2,1)S(1)}, u32[]{:S(2)}, u32[]{:S(2)}) async-start(bf16[32,16,104]{2,1,0:T(8,128)(2,1)} %bitcast.16), calls=%async_computation.5 | async-start | bytes 262144 | tf_op jit(solution)/shard_map/all_to_all | solution.py:376
  171.3 0.0 copy-done
  171.4 0.1 constant_dynamic-slice_fusion
  171.4 0.1 copy.24
  171.5 13.4 %all-to-all-done.5.grads = bf16[32,16,104]{2,1,0:T(8,128)(2,1)S(1)} async-done(((bf16[32,16,104]{2,1,0:T(8,128)(2,1)}), bf16[32,16,104]{2,1,0:T(8,128)(2,1)S(1)}, u32[]{:S(2)}, u32[]{:S(2)}) %all-to-all-start.5) | async-done | bytes 106528 | tf_op jit(solution)/shard_map/all_to_all | solution.py:376
  185.0 0.0 copy-done.4
  185.0 3.2 %adagrad.1 = bf16[8,464,128]{2,1,0:T(8,128)(2,1)S(1)} custom-call(bf16[32,16,104]{2,1,0:T(8,128)(2,1)S(1)} %all-to-all-done.5.grads, bf16[26,16,128]{2,1,0:T(8,128)(2,1)S(1)} %copy-done.4, f32[16,26]{1,0:T(8,128)S(1)} %bitcast.26, f32[8,512]{1,0:T(8,128)S(1)} %slice.14.cross_grads), custom_call_target="tpu_custom_call" | custom-call | tf_op jit(solution)/shard_map/adagrad/pallas_call | solution.py:106
  188.2 17.2 %all_to_all.39.own = bf16[8,464,128]{2,1,0:T(8,128)(2,1)S(1)} all-to-all(bf16[8,464,128]{2,1,0:T(8,128)(2,1)S(1)} %adagrad.1), channel_id=1, replica_groups=mesh['y'=4,'x_hi'=2,'core'=2,'x_lo'=2,'z'=16] {'x_hi','y'}, dimensions={0} | all-to-all | bytes 1900544 | tf_op jit(solution)/shard_map/all_to_all | solution.py:376
  205.4 6.6 %collective-permute-start.4 = (bf16[8,464,128]{2,1,0:T(8,128)(2,1)S(1)}, bf16[8,464,128]{2,1,0:T(8,128)(2,1)S(1)}, u32[]{:S(2)}, u32[]{:S(2)}) collective-permute-start(bf16[8,464,128]{2,1,0:T(8,128)(2,1)S(1)} %all_to_all.39.own), channel_id=1, source_target_pairs={{0,32},{32,0},{1,33},{33,1},{2,34},{34,2},{3,35},{35,3},{4,36},{36... | collective-permute-start | bytes 2850824 | tf_op jit(solution)/shard_map/ppermute | solution.py:384
  212.0 2.1 collective-permute-done.4.other
  214.1 1.5 unpack.1
  215.7 0.5 slice_bitcast_fusion
  (3 shorter events, 0.1 us)
Async XLA Ops:
  0.6 170.7 %copy-start = (f32[26,256]{1,0:T(8,128)S(1)}, f32[26,256]{1,0:T(8,128)}, u32[]{:S(2)}) copy-start(f32[26,256]{1,0:T(8,128)} %param.8) | copy-start | bytes 79876
  2.4 55.6 %copy-start.3 = (s32[512,26,8]{0,2,1:T(8,128)S(1)}, s32[512,26,8]{0,2,1:T(8,128)}, u32[]{:S(2)}) copy-start(s32[512,26,8]{0,2,1:T(8,128)} %param.9) | copy-start | bytes 1277956
  51.2 12.5 %collective-permute-start = (bf16[8,104,512]{2,1,0:T(8,128)(2,1)S(1)}, bf16[8,104,512]{2,1,0:T(8,128)(2,1)S(1)}, u32[]{:S(2)}, u32[]{:S(2)}) collective-permute-start(bf16[8,104,512]{2,1,0:T(8,128)(2,1)S(1)} %all_to_all.36.own), channel_id=1, source_target_pairs={{0,32},{32,0},{1,33},{33,1},{2,34},{34,2},{3,35},{35,3},{4,36},{36... | collective-permute-start | bytes 2555912 | tf_op jit(solution)/shard_map/ppermute | solution.py:384
  58.0 5.7 %copy-start.5 = (bf16[512,104]{0,1:T(8,128)(2,1)S(1)}, bf16[512,104]{0,1:T(8,128)(2,1)}, u32[]{:S(2)}) copy-start(bf16[512,104]{0,1:T(8,128)(2,1)} %param.13) | copy-start | bytes 319492
  58.0 5.7 %copy-start.6 = (bf16[104,256]{1,0:T(8,128)(2,1)S(1)}, bf16[104,256]{1,0:T(8,128)(2,1)}, u32[]{:S(2)}) copy-start(bf16[104,256]{1,0:T(8,128)(2,1)} %v.7) | copy-start | bytes 159748
  58.0 5.7 %copy-start.7 = (bf16[104,256]{1,0:T(8,128)(2,1)S(1)}, bf16[104,256]{1,0:T(8,128)(2,1)}, u32[]{:S(2)}) copy-start(bf16[104,256]{1,0:T(8,128)(2,1)} %u.7) | copy-start | bytes 159748
  63.6 7.6 %copy-start.1 = (s32[2,2,8,64,512]{4,3,2,1,0:T(8,128)}, s32[2,2,8,64,512]{4,3,2,1,0:T(8,128)S(1)}, u32[]{:S(2)}) copy-start(s32[2,2,8,64,512]{4,3,2,1,0:T(8,128)S(1)} %bag_words.1.words) | copy-start | bytes 12582916
  68.2 9.8 %collective-permute-start.1 = (bf16[512,256]{1,0:T(8,128)(2,1)S(1)}, bf16[512,256]{1,0:T(8,128)(2,1)S(1)}, u32[]{:S(2)}, u32[]{:S(2)}) collective-permute-start(bf16[512,256]{1,0:T(8,128)(2,1)S(1)} %get-tuple-element.25), channel_id=1, source_target_pairs={{0,16},{16,0},{1,17},{17,1},{2,18},{18,2},{3,19},{19,3},{4,20},{20... | collective-permute-start | bytes 786440 | tf_op jit(solution)/shard_map/ppermute | solution.py:384
  75.7 31.2 %copy-start.8 = (f32[104]{0:T(128)S(1)}, f32[104]{0:T(128)}, u32[]{:S(2)}) copy-start(f32[104]{0:T(128)} %param.12) | copy-start | bytes 1252
  95.8 24.1 %all-to-all-start.3 = ((bf16[16,32,256]{2,1,0:T(8,128)(2,1)}), bf16[16,32,256]{2,1,0:T(8,128)(2,1)S(1)}, u32[]{:S(2)}, u32[]{:S(2)}) async-start(bf16[16,32,256]{2,1,0:T(8,128)(2,1)} %broadcast_in_dim.7), calls=%async_computation.3 | async-start | bytes 524288 | tf_op jit(solution)/shard_map/all_to_all | solution.py:376
  119.9 10.0 %collective-permute-start.2 = (bf16[512,256]{1,0:T(8,128)(2,1)S(1)}, bf16[512,256]{1,0:T(8,128)(2,1)S(1)}, u32[]{:S(2)}, u32[]{:S(2)}) collective-permute-start(bf16[512,256]{1,0:T(8,128)(2,1)S(1)} %bitcast.24), channel_id=1, source_target_pairs={{0,16},{16,0},{1,17},{17,1},{2,18},{18,2},{3,19},{19,3},{4,20},{20... | collective-permute-start | bytes 786440 | tf_op jit(solution)/shard_map/ppermute | solution.py:384
  122.2 2.2 %copy-start.2 = (s32[2,2,8,64,512]{4,3,2,1,0:T(8,128)S(1)}, s32[2,2,8,64,512]{4,3,2,1,0:T(8,128)}, u32[]{:S(2)}) copy-start(s32[2,2,8,64,512]{4,3,2,1,0:T(8,128)} %copy-done.1) | copy-start | bytes 12582916
  135.4 10.6 %collective-permute-start.3 = (bf16[8,112,512]{2,1,0:T(8,128)(2,1)S(1)}, bf16[8,112,512]{2,1,0:T(8,128)(2,1)S(1)}, u32[]{:S(2)}, u32[]{:S(2)}) collective-permute-start(bf16[8,112,512]{2,1,0:T(8,128)(2,1)S(1)} %get-tuple-element.33), channel_id=1, source_target_pairs={{0,32},{32,0},{1,33},{33,1},{2,34},{34,2},{3,35},{35,3},{4,36},{36... | collective-permute-start | bytes 2752520 | tf_op jit(solution)/shard_map/ppermute | solution.py:384
  146.3 38.6 %copy-start.4 = (bf16[26,16,128]{2,1,0:T(8,128)(2,1)S(1)}, bf16[26,16,128]{2,1,0:T(8,128)(2,1)}, u32[]{:S(2)}) copy-start(bf16[26,16,128]{2,1,0:T(8,128)(2,1)} %get-tuple-element.34.rows) | copy-start | bytes 319492
  165.0 19.9 %all-to-all-start.5 = ((bf16[32,16,104]{2,1,0:T(8,128)(2,1)}), bf16[32,16,104]{2,1,0:T(8,128)(2,1)S(1)}, u32[]{:S(2)}, u32[]{:S(2)}) async-start(bf16[32,16,104]{2,1,0:T(8,128)(2,1)} %bitcast.16), calls=%async_computation.5 | async-start | bytes 262144 | tf_op jit(solution)/shard_map/all_to_all | solution.py:376
  205.4 8.8 %collective-permute-start.4 = (bf16[8,464,128]{2,1,0:T(8,128)(2,1)S(1)}, bf16[8,464,128]{2,1,0:T(8,128)(2,1)S(1)}, u32[]{:S(2)}, u32[]{:S(2)}) collective-permute-start(bf16[8,464,128]{2,1,0:T(8,128)(2,1)S(1)} %all_to_all.39.own), channel_id=1, source_target_pairs={{0,32},{32,0},{1,33},{33,1},{2,34},{34,2},{3,35},{35,3},{4,36},{36... | collective-permute-start | bytes 2850824 | tf_op jit(solution)/shard_map/ppermute | solution.py:384

commit v4 on v3

v4 whole, which is shorter than its diff:
```python
import functools

import jax
import jax.numpy as jnp
from jax import lax
from jax.experimental import pallas as pl
from jax.experimental.pallas import tpu as pltpu
from jax.sharding import Mesh
from jax.sharding import PartitionSpec as P

bf16 = jnp.bfloat16
f32 = jnp.float32
learn_rate = 0.3
epsilon = 1e-06

SAMPLES, TABLES, BAG, ROWS, WIDTH, FEATS, RANK = 512, 26, 8, 256, 128, 104, 256
N_ROW, N_DP, PART = 32, 16, 16
STEP_ROWS = N_ROW * PART
WORDS = STEP_ROWS // 8
HALF = SAMPLES // 2
GRAD_ROWS = 8
OUT_ROWS = FEATS + GRAD_ROWS
DP_OUTER = ("x_hi", "y")
ROW_AXES = ("z", "x_lo")
ROW_ALL = ("x_lo", "z")
BLOCK_OF = [(i & 1) * 16 + (i >> 1) for i in range(N_ROW)]
CHUNK = TABLES * PART + 16 + 32
UNROLL = 2
VMEM = 16 << 20

NT_DIMS = (((1,), (1,)), ((), ()))
TN_DIMS = (((0,), (0,)), ((), ()))


def part_of(outer, core):
    return (outer & 3) * 4 + (outer >> 2) * 2 + core


def pieces(table):
    found = []
    for block in range(N_ROW):
        low = max(table * WIDTH, block * FEATS)
        high = min((table + 1) * WIDTH, (block + 1) * FEATS)
        if low < high:
            found.append((block, low - block * FEATS, high - block * FEATS))
    return found


def pack_kernel(scalars, rows, mine, packed):
    mine[...] = rows[...]
    for device, block in enumerate(BLOCK_OF):
        first = block * FEATS // WIDTH
        start = block * FEATS - first * WIDTH
        cut = rows[first][:, start:].astype(f32)
        if cut.shape[1] < FEATS:
            cut = jnp.concatenate([cut, rows[first + 1][:, : FEATS - cut.shape[1]].astype(f32)], axis=1)
        packed[device] = cut[:, :FEATS].astype(bf16)


def pack(scalars, rows):
    return pl.pallas_call(
        pack_kernel,
        grid_spec=pltpu.PrefetchScalarGridSpec(
            num_scalar_prefetch=1,
            grid=(1,),
            in_specs=[pl.BlockSpec((TABLES, PART, WIDTH), lambda g, s: (0, s[0], 0))],
            out_specs=[
                pl.BlockSpec((TABLES, PART, WIDTH), lambda g, s: (0, 0, 0)),
                pl.BlockSpec((N_ROW, PART, FEATS), lambda g, s: (0, 0, 0)),
            ],
        ),
        out_shape=[
            jax.ShapeDtypeStruct((TABLES, PART, WIDTH), bf16),
            jax.ShapeDtypeStruct((N_ROW, PART, FEATS), bf16),
        ],
        name="pack_rows",
    )(scalars, rows)


def adagrad_kernel(grads, rows, accum, cross_grads, out):
    table_lane = lax.broadcasted_iota(jnp.int32, (PART, WIDTH), 1)
    accum_in = accum[...]
    accum_out = jnp.zeros((PART, WIDTH), f32)
    device_of = {block: device for device, block in enumerate(BLOCK_OF)}
    for table in range(TABLES):
        cuts = [grads[device_of[block]].astype(f32)[:, low:high] for block, low, high in pieces(table)]
        grad = jnp.concatenate(cuts, axis=1)
        total = accum_in[:, table : table + 1] + jnp.mean(grad * grad, axis=1, keepdims=True)
        step = learn_rate * grad * lax.rsqrt(total + epsilon)
        new = (rows[table].astype(f32) - step).astype(bf16)
        for copy in range(8):
            out[copy, table * PART : (table + 1) * PART, :] = new
        accum_out = jnp.where(table_lane == table, total, accum_out)
    high = accum_out.astype(bf16).astype(f32)
    rest = accum_out - high
    middle = rest.astype(bf16).astype(f32)
    low = rest - middle
    terms = jnp.concatenate(
        [high[:, :32], middle[:, :32], low[:, :32], jnp.zeros((PART, 32), f32)], axis=1
    ).astype(bf16)
    wide = cross_grads[...]
    wide = jnp.concatenate([wide[:, lane : lane + WIDTH] for lane in range(0, 2 * RANK, WIDTH)], axis=0).astype(bf16)
    for copy in range(8):
        out[copy, TABLES * PART : TABLES * PART + PART, :] = terms
        out[copy, TABLES * PART + PART :, :] = wide


def adagrad(grads, rows, accum, cross_grads):
    return pl.pallas_call(
        adagrad_kernel,
        out_shape=jax.ShapeDtypeStruct((8, CHUNK, WIDTH), bf16),
        compiler_params=pltpu.CompilerParams(vmem_limit_bytes=VMEM),
        name="adagrad",
    )(grads, rows, accum, cross_grads)


def unpack_kernel(scalars, own, other, rows_out, accum_out, grad_v, grad_u, grad_bias, accums, cross_grads):
    for outer in range(8):
        for turn, source in enumerate((own, other)):
            part = part_of(outer, turn ^ scalars[0])
            rows_out[:, pl.ds(part, 1)] = source[outer, : TABLES * PART].reshape(TABLES, 1, PART, WIDTH)
            terms = source[outer, TABLES * PART : TABLES * PART + PART].astype(f32)
            total = terms[:, :32] + terms[:, 32:64] + terms[:, 64:96]
            accums[pl.ds(pl.multiple_of(part * PART, PART), PART), :] = jnp.concatenate(
                [total, jnp.zeros((PART, WIDTH - 32), f32)], axis=1
            )
            wide = source[outer, TABLES * PART + PART :].astype(f32)
            at = pl.multiple_of(part * GRAD_ROWS, GRAD_ROWS)
            for i in range(4):
                cross_grads[pl.ds(at, GRAD_ROWS), i * WIDTH : (i + 1) * WIDTH] = wide[i * 8 : (i + 1) * 8]
    accum_out[...] = accums[...].T[:TABLES]
    grad_u[...] = cross_grads[:FEATS, :RANK]
    grad_v[...] = cross_grads[:FEATS, RANK:]
    grad_bias[...] = cross_grads[FEATS, :FEATS]


def unpack(scalars, own, other):
    whole = lambda *shape: pl.BlockSpec(shape, lambda g, s: (0,) * len(shape))
    shapes = [
        ((TABLES, N_DP, PART, WIDTH), bf16),
        ((TABLES, ROWS), f32),
        ((FEATS, RANK), f32),
        ((FEATS, RANK), f32),
        ((FEATS,), f32),
    ]
    return pl.pallas_call(
        unpack_kernel,
        grid_spec=pltpu.PrefetchScalarGridSpec(
            num_scalar_prefetch=1,
            grid=(1,),
            in_specs=[whole(8, CHUNK, WIDTH), whole(8, CHUNK, WIDTH)],
            out_specs=[whole(*shape) for shape, _ in shapes],
            scratch_shapes=[
                pltpu.VMEM((ROWS, WIDTH), f32),
                pltpu.VMEM((N_DP * GRAD_ROWS, 2 * RANK), f32),
            ],
        ),
        out_shape=[jax.ShapeDtypeStruct(shape, kind) for shape, kind in shapes],
        compiler_params=pltpu.CompilerParams(vmem_limit_bytes=VMEM),
        name="unpack",
    )(scalars, own, other)


def counts_of(words, scaled=False):
    columns = []
    for lane in range(0, words.shape[1], 128):
        blocks = []
        for group in range(0, WORDS, 8):
            word = words[group : group + 8, lane : lane + 128]
            if scaled:
                digits = [word & jnp.int32(15 << (4 * j)) for j in range(7)]
            else:
                digits = [lax.shift_right_logical(word, jnp.int32(4 * j)) & 15 for j in range(7)]
            digits.append(lax.shift_right_logical(word, jnp.int32(28)))
            blocks.append(jnp.concatenate(digits, axis=0).astype(f32).astype(bf16))
        columns.append(jnp.concatenate(blocks, axis=0))
    return jnp.concatenate(columns, axis=1)


def words_of(place):
    inside = (place >= 0) & (place < STEP_ROWS)
    word = jnp.where(inside, ((place >> 6) << 3) | (place & 7), -1)
    unit = jnp.left_shift(jnp.int32(1), ((place >> 3) & 7) * 4)
    columns = []
    for lane in range(0, place.shape[1], 128):
        slots = lax.broadcasted_iota(jnp.int32, (WORDS, 128), 0)
        total = jnp.zeros((WORDS, 128), jnp.int32)
        for k in range(BAG):
            here = word[k : k + 1, lane : lane + 128] == slots
            total = total + jnp.where(here, unit[k : k + 1, lane : lane + 128], 0)
        columns.append(total)
    return jnp.concatenate(columns, axis=1)


def whole(*shape):
    return pl.BlockSpec(shape, lambda g, s: (0,) * len(shape))


def words_kernel(scalars, *refs):
    ids, outs, places = refs[:4], refs[4:6], refs[6]
    step = pl.program_id(0)

    @pl.when(step == 0)
    def _():
        for i in range(4):
            row = ids[i][0]
            part = (row >> 4) & 15
            turn = (part & 1) ^ scalars[2]
            outer = (((part >> 1) & 1) << 2) | (part >> 2)
            device = (((row >> 8) & 15) << 1) | (row >> 12)
            places[i] = turn * 4096 + outer * 512 + device * 16 + (row & 15)

    for half, words in enumerate(outs):
        for table in range(2):
            for turn in range(2):
                words[table, turn, 0] = words_of(places[2 * half + table] - (turn * 8 + step) * STEP_ROWS)


def bag_words(scalars, ids):
    return pl.pallas_call(
        words_kernel,
        grid_spec=pltpu.PrefetchScalarGridSpec(
            num_scalar_prefetch=1,
            grid=(8,),
            in_specs=[
                pl.BlockSpec((1, BAG, HALF), lambda g, s: (s[0], 0, s[3])),
                pl.BlockSpec((1, BAG, HALF), lambda g, s: (s[1], 0, s[3])),
                pl.BlockSpec((1, BAG, HALF), lambda g, s: (s[0], 0, 1 - s[3])),
                pl.BlockSpec((1, BAG, HALF), lambda g, s: (s[1], 0, 1 - s[3])),
            ],
            out_specs=[pl.BlockSpec((2, 2, 1, WORDS, HALF), lambda g, s: (0, 0, g, 0, 0))] * 2,
            scratch_shapes=[pltpu.VMEM((4, BAG, HALF), jnp.int32)],
        ),
        out_shape=[jax.ShapeDtypeStruct((2, 2, 8, WORDS, HALF), jnp.int32)] * 2,
        compiler_params=pltpu.CompilerParams(vmem_limit_bytes=VMEM),
        cost_estimate=pl.CostEstimate(flops=1 << 28, bytes_accessed=5 << 20, transcendentals=0),
        name="bag_words",
    )(scalars, ids, ids, ids, ids)


HALF_BLOCK = pl.BlockSpec((FEATS, HALF), lambda g, s: (0, s[0]))
KERNEL_COST = pl.CostEstimate(flops=1 << 32, bytes_accessed=5 << 20, transcendentals=0)


def words_block(first_turn, turns):
    block = first_turn if turns == 1 else 0
    return pl.BlockSpec((2, turns, UNROLL, WORDS, HALF), lambda g, s: (0, block, g, 0, 0))


def call(kernel, name, steps, operands, in_specs, out_specs, out_shape, scratch_shapes=(), aliases=None):
    return pl.pallas_call(
        kernel,
        grid_spec=pltpu.PrefetchScalarGridSpec(
            num_scalar_prefetch=1,
            grid=(steps,),
            in_specs=in_specs,
            out_specs=out_specs,
            scratch_shapes=list(scratch_shapes),
        ),
        out_shape=out_shape,
        input_output_aliases=aliases or {},
        compiler_params=pltpu.CompilerParams(vmem_limit_bytes=VMEM),
        cost_estimate=KERNEL_COST,
        name=name,
    )(*operands)


def forward_kernel(turns, last, scalars, words, *refs):
    step = pl.program_id(0)
    rows, refs = refs[:turns], refs[turns:]
    if last:
        *before, pooled_out, total = refs
    else:
        before, total = refs[:-1], refs[-1]

    @pl.when(step == 0)
    def _():
        total[...] = before[0][...] if before else jnp.zeros_like(total)

    for i in range(UNROLL):
        for table in range(2):
            for turn, source in enumerate(rows):
                counts = counts_of(words[table, turn, i], scaled=True)
                total[table] += jnp.dot(source[i], counts, preferred_element_type=f32)

    if last:

        @pl.when(step == 8 // UNROLL - 1)
        def _():
            feature = lax.broadcasted_iota(jnp.int32, (FEATS, HALF), 0)
            pooled_out[...] = jnp.where(feature < scalars[1], total[0], total[1]).astype(bf16)


def forward(scalars, words, rows, first_turn, before=None, last=True):
    turns = len(rows)
    operands = [scalars, words, *rows]
    in_specs = [words_block(first_turn, turns)]
    in_specs += [pl.BlockSpec((UNROLL, FEATS, STEP_ROWS), lambda g, s: (g, 0, 0))] * turns
    if before is not None:
        operands.append(before)
        in_specs.append(whole(2, FEATS, HALF))
    if last:
        out_specs, out_shape = whole(FEATS, HALF), jax.ShapeDtypeStruct((FEATS, HALF), bf16)
        scratch = [pltpu.VMEM((2, FEATS, HALF), f32)]
    else:
        out_specs, out_shape, scratch = whole(2, FEATS, HALF), jax.ShapeDtypeStruct((2, FEATS, HALF), f32), []
    kernel = functools.partial(forward_kernel, turns, last)
    return call(kernel, "bags", 8 // UNROLL, operands, in_specs, out_specs, out_shape, scratch)


def ranks_kernel(scalars, pooled_a, pooled_b, v_a, u_a, upstream_a, v_b, u_b, upstream_b, ranks):
    rank = jnp.zeros((RANK, HALF), f32)
    rank_grad = jnp.zeros((RANK, HALF), f32)
    for pooled_in, v, u, upstream in ((pooled_a, v_a, u_a, upstream_a), (pooled_b, v_b, u_b, upstream_b)):
        pooled = pooled_in[...]
        gate_grad = (upstream[...].astype(f32) * pooled.astype(f32)).astype(bf16)
        rank += lax.dot_general(v[...], pooled, TN_DIMS, preferred_element_type=f32)
        rank_grad += lax.dot_general(u[...], gate_grad, TN_DIMS, preferred_element_type=f32)
    ranks[:RANK] = rank.astype(bf16)
    ranks[RANK:] = rank_grad.astype(bf16)


def rank_terms(scalars, pooled, partner_pooled, v, u, upstream, partner):
    side = [pl.BlockSpec((FEATS, HALF), lambda g, s, i=i: (0, i)) for i in range(3)]
    return call(
        ranks_kernel,
        "rank_terms",
        1,
        [scalars, pooled, partner_pooled, v, u, upstream, partner, partner, partner],
        [whole(FEATS, HALF), whole(FEATS, HALF), whole(FEATS, RANK), whole(FEATS, RANK), HALF_BLOCK, *side],
        whole(2 * RANK, HALF),
        jax.ShapeDtypeStruct((2 * RANK, HALF), bf16),
    )


def cross_layer(scalars, ranks, pooled_in, v, u, bias, upstream_in, crossed_out, grads, cross_grads):
    rank = ranks[:RANK]
    rank_grad = ranks[RANK:]
    pooled_bf = pooled_in[...]
    pooled = pooled_bf.astype(f32)
    upstream = upstream_in[...].astype(f32)
    gate = jnp.dot(u[...], rank, preferred_element_type=f32) + bias[...]
    crossed_out[...] = (pooled * gate + pooled).astype(bf16)
    back = jnp.dot(v[...], rank_grad, preferred_element_type=f32)
    grad = (upstream * (gate + 1.0) + back).astype(bf16).astype(f32)
    feature = lax.broadcasted_iota(jnp.int32, (FEATS, HALF), 0)
    grads[0] = jnp.where(feature < scalars[1], grad, 0.0).astype(bf16)
    grads[1] = jnp.where(feature < scalars[1], 0.0, grad).astype(bf16)
    gate_grad = upstream * pooled
    gate_bf = gate_grad.astype(bf16)
    gate_rest = (gate_grad - gate_bf.astype(f32)).astype(bf16)
    cross_grads[...] = jnp.zeros_like(cross_grads)
    cross_grads[:FEATS, :RANK] = lax.dot_general(gate_bf, rank, NT_DIMS, preferred_element_type=f32)
    cross_grads[:FEATS, RANK:] = lax.dot_general(pooled_bf, rank_grad, NT_DIMS, preferred_element_type=f32)
    ones = jnp.ones((16, HALF), bf16)
    bias_sum = lax.dot_general(ones, gate_bf, NT_DIMS, preferred_element_type=f32) + lax.dot_general(
        ones, gate_rest, NT_DIMS, preferred_element_type=f32
    )
    cross_grads[FEATS : FEATS + 8, :FEATS] = bias_sum[:8]


def row_grads(scalars, turns, words, grads, cross_grads, before, outs):
    step = pl.program_id(0)
    for i in range(UNROLL):
        for n, turn in enumerate(turns):
            part = part_of(step * UNROLL + i, turn ^ scalars[2])
            result = lax.dot_general(grads[0], counts_of(words[0, n, i]), NT_DIMS, preferred_element_type=f32)
            result += lax.dot_general(grads[1], counts_of(words[1, n, i]), NT_DIMS, preferred_element_type=f32)
            extra = cross_grads[pl.ds(pl.multiple_of(part * GRAD_ROWS, GRAD_ROWS), GRAD_ROWS), :]
            block = jnp.concatenate([result, extra], axis=0)
            if before is not None:
                block = block + before[i]
            outs[n][i] = block.astype(outs[n].dtype)


def backward_kernel(turns, scalars, words, ranks, pooled, v, u, bias, upstream, *refs):
    if len(turns) == 2:
        before = None
        crossed, own, other, grads, cross_grads = refs
        outs = (own, other)
    else:
        before, _, crossed, grads, cross_grads, other = refs
        outs = (other,)

    @pl.when(pl.program_id(0) == 0)
    def _():
        cross_layer(scalars, ranks, pooled, v, u, bias, upstream, crossed, grads, cross_grads)

    row_grads(scalars, turns, words, grads, cross_grads, before, outs)


def rest_kernel(scalars, words, grads, cross_grads, before, own):
    row_grads(scalars, (0,), words, grads, cross_grads, before, (own,))


SUMS_BLOCK = pl.BlockSpec((UNROLL, OUT_ROWS, STEP_ROWS), lambda g, s: (g, 0, 0))
SUMS_SHAPE = (8, OUT_ROWS, STEP_ROWS)
CROSS_SPECS = [whole(2 * RANK, HALF), whole(FEATS, HALF), whole(FEATS, RANK), whole(FEATS, RANK), whole(FEATS, 1), HALF_BLOCK]
CROSSED = jax.ShapeDtypeStruct((FEATS, SAMPLES), bf16)
GRADS = (2, FEATS, HALF)
CROSS_GRADS = (N_DP * GRAD_ROWS, 2 * RANK)


def first_backward(scalars, words, *operands):
    return call(
        functools.partial(backward_kernel, (0, 1)),
        "cross_and_row_grads",
        8 // UNROLL,
        [scalars, words, *operands],
        [words_block(0, 2), *CROSS_SPECS],
        [HALF_BLOCK, SUMS_BLOCK, SUMS_BLOCK],
        [CROSSED, jax.ShapeDtypeStruct(SUMS_SHAPE, f32), jax.ShapeDtypeStruct(SUMS_SHAPE, f32)],
        [pltpu.VMEM(GRADS, bf16), pltpu.VMEM(CROSS_GRADS, f32)],
    )


def second_backward(scalars, words, *operands):
    return call(
        functools.partial(backward_kernel, (1,)),
        "cross_and_row_grads",
        8 // UNROLL,
        [scalars, words, *operands],
        [words_block(1, 1), *CROSS_SPECS, SUMS_BLOCK, pl.BlockSpec(memory_space=pl.ANY)],
        [HALF_BLOCK, whole(*GRADS), whole(*CROSS_GRADS), SUMS_BLOCK],
        [
            CROSSED,
            jax.ShapeDtypeStruct(GRADS, bf16),
            jax.ShapeDtypeStruct(CROSS_GRADS, f32),
            jax.ShapeDtypeStruct(SUMS_SHAPE, bf16),
        ],
        aliases={len(operands) + 1: 0},
    )


def rest_of_backward(scalars, words, grads, cross_grads, before):
    return call(
        rest_kernel,
        "row_grads",
        8 // UNROLL,
        [scalars, words, grads, cross_grads, before],
        [words_block(0, 1), whole(*GRADS), whole(*CROSS_GRADS), SUMS_BLOCK],
        SUMS_BLOCK,
        jax.ShapeDtypeStruct(SUMS_SHAPE, bf16),
    )


def exchange(x, axes):
    return lax.all_to_all(x, axes, 0, 0, tiled=True)


def spread(x, axes, count):
    return exchange(jnp.broadcast_to(x, (count,) + x.shape), axes)


def swap(x, axis):
    return lax.ppermute(x, axis, [(0, 1), (1, 0)])


def to_other_core(x):
    return swap(x, "core")


def body(rows_in, accum, bag_ids, cross_v, cross_u, cross_bias, upstream):
    block = lax.axis_index("x_lo") * 16 + lax.axis_index("z")
    core = lax.axis_index("core")
    part = part_of(lax.axis_index(DP_OUTER), core)
    table_a = (block * FEATS) // WIDTH
    table_b = jnp.minimum(table_a + 1, TABLES - 1)
    n_a = jnp.minimum(FEATS, WIDTH * (table_a + 1) - FEATS * block)

    upstream_t = upstream.T
    sent_upstream = lax.dynamic_slice(upstream_t, (0, (1 - lax.axis_index("x_lo")) * HALF), (FEATS, HALF))
    partner = swap(jnp.concatenate([cross_v, cross_u, sent_upstream], axis=1), "x_lo")

    my_rows, packed = pack(jnp.stack([part]).astype(jnp.int32), rows_in)
    mine = exchange(packed, ROW_AXES).reshape(STEP_ROWS, FEATS).T
    nibble = (jnp.arange(STEP_ROWS) >> 3) & 7
    mine = mine * jnp.where(nibble == 7, 1.0, jnp.exp2(-4.0 * nibble)).astype(bf16)
    mine, partner = lax.optimization_barrier((mine, partner))
    own = spread(mine, DP_OUTER, 8)
    keep = lax.axis_index("x_lo")
    scalars = jnp.stack([table_a, table_b, core, keep]).astype(jnp.int32)
    at_keep = jnp.stack([keep, n_a, core]).astype(jnp.int32)
    at_sent = jnp.stack([1 - keep, n_a, core]).astype(jnp.int32)
    kept_words, sent_words = bag_words(scalars, bag_ids.transpose(1, 2, 0))
    own, kept_words, sent_words = lax.optimization_barrier((own, kept_words, sent_words))
    other = to_other_core(own)

    sent_sums = forward(at_sent, sent_words, [own], 0, last=False)
    sent_pooled = forward(at_sent, sent_words, [other], 1, before=sent_sums)
    partner_pooled = swap(sent_pooled, "x_lo")
    kept_pooled = forward(at_keep, kept_words, [own, other], 0)

    terms = rank_terms(at_keep, kept_pooled, partner_pooled, cross_v, cross_u, upstream_t, partner)
    gathered = exchange(terms.reshape(16, 32, HALF), "z")
    ranks = spread(jnp.sum(gathered.astype(f32), axis=0).astype(bf16), "z", 16).reshape(2 * RANK, HALF)
    sent_ranks = swap(ranks, "x_lo")

    cross = (cross_v, cross_u, cross_bias.reshape(FEATS, 1), upstream_t)
    crossed, own, other = first_backward(at_keep, kept_words, ranks, kept_pooled, *cross)
    crossed, grads, cross_grads, other = second_backward(
        at_sent, sent_words, sent_ranks, sent_pooled, *cross, other, crossed
    )
    from_other = to_other_core(other)
    own = rest_of_backward(at_sent, sent_words, grads, cross_grads, own)

    chip_sum = (own.astype(f32) + from_other.astype(f32)).astype(bf16)
    sums = jnp.sum(exchange(chip_sum, DP_OUTER).astype(f32), axis=0)
    row_grad = exchange(sums[:FEATS].astype(bf16).T.reshape(N_ROW, PART, FEATS), ROW_AXES)
    my_accum = lax.dynamic_slice(accum, (0, part * PART), (TABLES, PART)).T

    own = exchange(adagrad(row_grad, my_rows, my_accum, sums[FEATS:]), DP_OUTER)
    new_rows, new_accum, grad_v, grad_u, grad_bias = unpack(
        jnp.stack([core]).astype(jnp.int32), own, to_other_core(own)
    )
    return (crossed.T, new_rows.reshape(TABLES, ROWS, WIDTH), new_accum, grad_v, grad_u, grad_bias)


def solution(mesh):
    inner = Mesh(mesh.devices.reshape(4, 2, 2, 2, 16), ("y", "x_hi", "core", "x_lo", "z"))
    dp = ("y", "x_hi", "core")
    row = ROW_ALL
    return jax.shard_map(
        body,
        mesh=inner,
        in_specs=(
            P(None, row, None),
            P(None, row),
            P(dp, None, None),
            P(row, None),
            P(row, None),
            P(row),
            P(dp, row),
        ),
        out_specs=(
            P(dp, row),
            P(None, row, None),
            P(None, row),
            P(row, None),
            P(row, None),
            P(row),
        ),
        check_vma=False,
    )
```

time: 217 us -> 208 us (0.959)
  blocking collectives: 100 us -> 52.4 us
  starting transfers between devices: 44.5 us -> 72.3 us
  waiting for transfers between devices: 32.9 us -> 41.8 us
  local copies, waits for them, and re-layouts: 4.67 us -> 8.7 us
    all_to_all x5 -> x3, blocking collectives: 100 us -> 52.4 us  [exchange(): return lax.all_to_all(x, axes, 0, 0, tiled=True)]
    all_to_all x2 -> x4, starting transfers between devices: 17.4 us -> 40.9 us  [exchange(): return lax.all_to_all(x, axes, 0, 0, tiled=True)]
    all_to_all x2 -> x4, waiting for transfers between devices: 26.4 us -> 39.6 us  [exchange(): return lax.all_to_all(x, axes, 0, 0, tiled=True)]
    ppermute x5 -> x6, waiting for transfers between devices: 6.54 us -> 2.14 us  [swap(): return lax.ppermute(x, axis, [(0, 1), (1, 0)])]
    ppermute x5 -> x6, starting transfers between devices: 27.2 us -> 31.4 us  [swap(): return lax.ppermute(x, axis, [(0, 1), (1, 0)])]
    unnamed x19 -> x27, local copies, waits for them, and re-layouts: 2.31 us -> 5.93 us
    pallas_call x4 -> x7, Pallas kernels: 20 us -> 18.9 us  [call(): pl.pallas_call(kernel, grid_spec=pltpu.PrefetchScalarGridSpec(num_scalar_...]
  transfers between devices with their start and end apart: 7 -> 10, of which waited for: 5 -> 5; matrix products, arithmetic and copies ran while one was open for 0% -> 0% of each run, Pallas kernels for 7% -> 8%
where the time goes in v4:
time: 208 us; the launch traced here: 207 us
  starting transfers between devices  72.3 us (35%)
  blocking collectives  52.4 us (25%)
  waiting for transfers between devices  41.8 us (20%)
  Pallas kernels  30.3 us (15%)
  local copies, waits for them, and re-layouts  8.7 us (4%)
    all_to_all x3, blocking collectives, exchange(): return lax.all_to_all(x, axes, 0, 0, tiled=True)  52.4 us
    all_to_all x4, starting transfers between devices, exchange(): return lax.all_to_all(x, axes, 0, 0, tiled=True)  40.9 us
    all_to_all x4, waiting for transfers between devices, exchange(): return lax.all_to_all(x, axes, 0, 0, tiled=True)  39.6 us
    ppermute x6, starting transfers between devices, swap(): return lax.ppermute(x, axis, [(0, 1), (1, 0)])  31.4 us
    pallas_call x7, Pallas kernels, call(): pl.pallas_call(kernel, grid_spec=pltpu.PrefetchScalarGridSpec(num_scalar_...  18.9 us
    unnamed x27, local copies, waits for them, and re-layouts  5.93 us
    pallas_call x1, Pallas kernels, bag_words(): pl.pallas_call(words_kernel, grid_spec=pltpu.PrefetchScalarGridSpec(num_s...  4.83 us
  transfers between devices with their start and end apart: 10, of which 5 were waited for; matrix products, arithmetic and copies ran while one was open for 0% of the time, Pallas kernels for 8%

profile of v4, /device:TPU:1, one launch (start us, length us, event | category | flops | bytes accessed | tf_op | source)
XLA Modules:
  0.0 207.2 jit_solution(5396835577251599289)
XLA Ops:
  0.6 0.0 copy-start
  0.6 0.0 copy-start.5
  0.7 0.0 copy-start.3
  0.7 0.0 copy-start.4
  0.7 1.7 pack_rows.1
  2.4 17.0 %all-to-all-start = ((bf16[32,16,104]{2,1,0:T(8,128)(2,1)}), bf16[32,16,104]{2,1,0:T(8,128)(2,1)S(1)}, u32[]{:S(2)}, u32[]{:S(2)}) async-start(bf16[32,16,104]{2,1,0:T(8,128)(2,1)} %get-tuple-element.27), calls=%async_computation | async-start | bytes 262144 | tf_op jit(solution)/shard_map/all_to_all | solution.py:448
  19.4 0.0 copy-start.1
  19.4 0.0 copy-done.5
  19.5 0.0 copy-done.3
  19.5 0.0 copy-done.4
  19.5 3.3 %collective-permute-start = (bf16[104,768]{1,0:T(8,128)(2,1)S(1)}, bf16[104,768]{1,0:T(8,128)(2,1)S(1)}, u32[]{:S(2)}, u32[]{:S(2)}) collective-permute-start(bf16[104,768]{1,0:T(8,128)(2,1)S(1)} %pad_maximum_fusion), channel_id=1, source_target_pairs={{0,16},{16,0},{1,17},{17,1},{2,18},{18,2},{3,19},{19,3},{4,20},{20... | collective-permute-start | bytes 479240 | tf_op jit(solution)/shard_map/ppermute | solution.py:456
  22.8 10.7 %all-to-all-done = bf16[32,16,104]{2,1,0:T(8,128)(2,1)S(1)} async-done(((bf16[32,16,104]{2,1,0:T(8,128)(2,1)}), bf16[32,16,104]{2,1,0:T(8,128)(2,1)S(1)}, u32[]{:S(2)}, u32[]{:S(2)}) %all-to-all-start) | async-done | bytes 106528 | tf_op jit(solution)/shard_map/all_to_all | solution.py:448
  33.4 0.1 copy.19
  33.6 0.0 collective-permute-done.v_b.u_b.upstream_b
  33.6 1.0 broadcast_in_dim.12
  34.6 6.4 %all-to-all-start.1 = ((bf16[8,104,512]{2,1,0:T(8,128)(2,1)}), bf16[8,104,512]{2,1,0:T(8,128)(2,1)S(1)}, u32[]{:S(2)}, u32[]{:S(2)}) async-start(bf16[8,104,512]{2,1,0:T(8,128)(2,1)} %broadcast_in_dim.12), calls=%async_computation.1 | async-start | bytes 1703936 | tf_op jit(solution)/shard_map/all_to_all | solution.py:448
  40.9 0.1 pad_add_fusion.scalars
  41.0 0.0 copy-done.1
  41.0 4.8 %bag_words.1 = (s32[2,2,8,64,256]{4,3,2,1,0:T(8,128)S(1)}, s32[2,2,8,64,256]{4,3,2,1,0:T(8,128)S(1)}) custom-call(s32[4]{0:T(128)S(1)} %pad_add_fusion.scalars, s32[26,8,512]{2,1,0:T(8,128)S(1)} %bitcast.23, s32[26,8,512]{2,1,0:T(8,128)S(1)} %bitcast.24, s32[26,8,512]{2,1,0:T(8,128)S(1)} %bitcast.25, s32[26,8,512]{2,1,0:T(8,128)S(1)} %bitcast.26), custom_call_target="tpu_custom_call" | custom-call | flops 268435456 | bytes 5242880 | tf_op jit(solution)/shard_map/bag_words/pallas_call | solution.py:220
  45.8 0.0 copy-start.6
  45.8 1.3 copy-done.6
  47.2 1.3 copy-done.9
  48.5 2.6 %all-to-all-done.1.refs_0_ = bf16[8,104,512]{2,1,0:T(8,128)(2,1)S(1)} async-done(((bf16[8,104,512]{2,1,0:T(8,128)(2,1)}), bf16[8,104,512]{2,1,0:T(8,128)(2,1)S(1)}, u32[]{:S(2)}, u32[]{:S(2)}) %all-to-all-start.1) | async-done | bytes 852000 | tf_op jit(solution)/shard_map/all_to_all | solution.py:448
  51.1 7.0 %collective-permute-start.1 = (bf16[8,104,512]{2,1,0:T(8,128)(2,1)S(1)}, bf16[8,104,512]{2,1,0:T(8,128)(2,1)S(1)}, u32[]{:S(2)}, u32[]{:S(2)}) collective-permute-start(bf16[8,104,512]{2,1,0:T(8,128)(2,1)S(1)} %all-to-all-done.1.refs_0_), channel_id=1, source_target_pairs={{0,32},{32,0},{1,33},{33,1},{2,34},{34,2},{3,35},{35,3},{4,36},{36... | collective-permute-start | bytes 2555912 | tf_op jit(solution)/shard_map/ppermute | solution.py:456
  58.1 0.1 add_add_fusion.1.scalars
  58.2 0.1 add_add_fusion.scalars
  58.2 1.6 copy-done.7
  59.8 2.1 %bags.4.refs_1_ = f32[2,104,256]{2,1,0:T(8,128)S(1)} custom-call(s32[3]{0:T(128)S(1)} %add_add_fusion.scalars, s32[2,2,8,64,256]{4,3,2,1,0:T(8,128)S(1)} %copy-done.7, bf16[8,104,512]{2,1,0:T(8,128)(2,1)S(1)} %all-to-all-done.1.refs_0_), custom_call_target="tpu_custom_call" | custom-call | flops 4294967296 | bytes 5242880 | tf_op jit(solution)/shard_map/bags/pallas_call | solution.py:251
  62.0 0.0 collective-permute-done.1.refs_1_.refs_0_
  62.0 2.1 %bags.5.pooled = bf16[104,256]{1,0:T(8,128)(2,1)S(1)} custom-call(s32[3]{0:T(128)S(1)} %add_add_fusion.scalars, s32[2,2,8,64,256]{4,3,2,1,0:T(8,128)S(1)} %copy-done.7, bf16[8,104,512]{2,1,0:T(8,128)(2,1)S(1)} %collective-permute-done.1.refs_1_.refs_0_, f32[2,104,256]{2,1,0:T(8,128)S(1)} %bags.4.refs_1_), custom_call_target="tpu_custom_call" | custom-call | flops 4294967296 | bytes 5242880 | tf_op jit(solution)/shard_map/bags/pallas_call | solution.py:251
  64.1 3.2 %collective-permute-start.2 = (bf16[104,256]{1,0:T(8,128)(2,1)S(1)}, bf16[104,256]{1,0:T(8,128)(2,1)S(1)}, u32[]{:S(2)}, u32[]{:S(2)}) collective-permute-start(bf16[104,256]{1,0:T(8,128)(2,1)S(1)} %bags.5.pooled), channel_id=1, source_target_pairs={{0,16},{16,0},{1,17},{17,1},{2,18},{18,2},{3,19},{19,3},{4,20},{20... | collective-permute-start | bytes 159752 | tf_op jit(solution)/shard_map/ppermute | solution.py:456
  67.3 3.0 %bags.3.pooled_a.pooled = bf16[104,256]{1,0:T(8,128)(2,1)S(1)} custom-call(s32[3]{0:T(128)S(1)} %add_add_fusion.1.scalars, s32[2,2,8,64,256]{4,3,2,1,0:T(8,128)S(1)} %copy-done.10, bf16[8,104,512]{2,1,0:T(8,128)(2,1)S(1)} %all-to-all-done.1.refs_0_, bf16[8,104,512]{2,1,0:T(8,128)(2,1)S(1)} %collective-permute-done.1.refs_1_.refs_0_), custom_call_target="tpu_custom_call" | custom-call | flops 4294967296 | bytes 5242880 | tf_op jit(solution)/shard_map/bags/pallas_call | solution.py:251
  70.3 0.0 collective-permute-done.2.pooled_b
  70.3 0.0 copy-start.12
  70.3 0.9 rank_terms.1
  71.2 16.7 %all_to_all.35 = bf16[16,32,256]{2,1,0:T(8,128)(2,1)S(1)} all-to-all(bf16[16,32,256]{2,1,0:T(8,128)(2,1)S(1)} %bitcast.29), channel_id=1, replica_groups=mesh['y'=4,'x_hi'=2,'core'=2,'x_lo'=2,'z'=16] {'z'}, dimensions={0} | all-to-all | bytes 524288 | tf_op jit(solution)/shard_map/all_to_all | solution.py:448
  88.0 0.7 broadcast_in_dim.13
  88.7 11.0 %all-to-all-start.3 = ((bf16[16,32,256]{2,1,0:T(8,128)(2,1)}), bf16[16,32,256]{2,1,0:T(8,128)(2,1)S(1)}, u32[]{:S(2)}, u32[]{:S(2)}) async-start(bf16[16,32,256]{2,1,0:T(8,128)(2,1)} %broadcast_in_dim.13), calls=%async_computation.3 | async-start | bytes 524288 | tf_op jit(solution)/shard_map/all_to_all | solution.py:448
  99.7 0.1 copy.21.bias
  99.9 12.9 %all-to-all-done.3 = bf16[16,32,256]{2,1,0:T(8,128)(2,1)S(1)} async-done(((bf16[16,32,256]{2,1,0:T(8,128)(2,1)}), bf16[16,32,256]{2,1,0:T(8,128)(2,1)S(1)}, u32[]{:S(2)}, u32[]{:S(2)}) %all-to-all-start.3) | async-done | bytes 262176 | tf_op jit(solution)/shard_map/all_to_all | solution.py:448
  112.8 3.6 %collective-permute-start.3 = (bf16[512,256]{1,0:T(8,128)(2,1)S(1)}, bf16[512,256]{1,0:T(8,128)(2,1)S(1)}, u32[]{:S(2)}, u32[]{:S(2)}) collective-permute-start(bf16[512,256]{1,0:T(8,128)(2,1)S(1)} %bitcast.27), channel_id=1, source_target_pairs={{0,16},{16,0},{1,17},{17,1},{2,18},{18,2},{3,19},{19,3},{4,20},{20... | collective-permute-start | bytes 786440 | tf_op jit(solution)/shard_map/ppermute | solution.py:456
  116.4 0.0 copy-start.11
  116.4 1.6 copy-done.11
  118.0 4.8 %cross_and_row_grads.2 = (bf16[104,512]{1,0:T(8,128)(2,1)}, f32[8,112,512]{2,1,0:T(8,128)S(1)}, f32[8,112,512]{2,1,0:T(8,128)S(1)}) custom-call(s32[3]{0:T(128)S(1)} %add_add_fusion.1.scalars, s32[2,2,8,64,256]{4,3,2,1,0:T(8,128)S(1)} %copy-done.11, bf16[512,256]{1,0:T(8,128)(2,1)S(1)} %bitcast.28, bf16[104,256]{1,0:T(8,128)(2,1)S(1)} %bags.3.pooled_a.pooled, ...), custom_call_target="tpu_custom_call" | custom-call | flops 4294967296 | bytes 5242880 | tf_op jit(solution)/shard_map/cross_and_row_grads/pallas_call | solution.py:251
  122.8 0.0 collective-permute-done.3.ranks
  122.8 0.0 copy-done.8
  122.8 3.4 %cross_and_row_grads.3 = (bf16[104,512]{1,0:T(8,128)(2,1)}, bf16[2,104,256]{2,1,0:T(8,128)(2,1)S(1)}, f32[128,512]{1,0:T(8,128)S(1)}, bf16[8,112,512]{2,1,0:T(8,128)(2,1)S(1)}) custom-call(s32[3]{0:T(128)S(1)} %add_add_fusion.scalars, s32[2,2,8,64,256]{4,3,2,1,0:T(8,128)S(1)} %copy-done.8, ...), custom_call_target="tpu_custom_call", output_to_operand_aliasing={{0}: (9, {})} | custom-call | flops 4294967296 | bytes 5242880 | tf_op jit(solution)/shard_map/cross_and_row_grads/pallas_call | solution.py:251
  126.2 7.9 %collective-permute-start.4 = (bf16[8,112,512]{2,1,0:T(8,128)(2,1)S(1)}, bf16[8,112,512]{2,1,0:T(8,128)(2,1)S(1)}, u32[]{:S(2)}, u32[]{:S(2)}) collective-permute-start(bf16[8,112,512]{2,1,0:T(8,128)(2,1)S(1)} %get-tuple-element.41), channel_id=1, source_target_pairs={{0,32},{32,0},{1,33},{33,1},{2,34},{34,2},{3,35},{35,3},{4,36},{36... | collective-permute-start | bytes 2752520 | tf_op jit(solution)/shard_map/ppermute | solution.py:456
  134.1 2.6 %row_grads.1 = bf16[8,112,512]{2,1,0:T(8,128)(2,1)S(1)} custom-call(s32[3]{0:T(128)S(1)} %add_add_fusion.scalars, s32[2,2,8,64,256]{4,3,2,1,0:T(8,128)S(1)} %copy-done.8, bf16[2,104,256]{2,1,0:T(8,128)(2,1)S(1)} %get-tuple-element.38.grads, f32[128,512]{1,0:T(8,128)S(1)} %get-tuple-element.39.cross_grads, f32[8,112,512]{2,1,0:T(8,128)S(1)} %get-tuple-element.40.before), custom_call_target="tpu_custom_call" | custom-call | flops 4294967296 | bytes 5242880 | tf_op jit(solution)/shard_map/row_grads/pallas_call | solution.py:251
  136.7 0.0 collective-permute-done.4
  136.8 0.3 add_convert_fusion
  137.0 0.0 copy-start.2
  137.0 18.3 %all_to_all.36 = bf16[8,112,512]{2,1,0:T(8,128)(2,1)S(1)} all-to-all(bf16[8,112,512]{2,1,0:T(8,128)(2,1)S(1)} %add_convert_fusion), channel_id=1, replica_groups=mesh['y'=4,'x_hi'=2,'core'=2,'x_lo'=2,'z'=16] {'x_hi','y'}, dimensions={0} | all-to-all | bytes 1835008 | tf_op jit(solution)/shard_map/all_to_all | solution.py:448
  155.3 0.1 convert_reduce_fusion
  155.5 0.8 copy.22
  156.2 6.6 %all-to-all-start.5 = ((bf16[32,16,104]{2,1,0:T(8,128)(2,1)}), bf16[32,16,104]{2,1,0:T(8,128)(2,1)S(1)}, u32[]{:S(2)}, u32[]{:S(2)}) async-start(bf16[32,16,104]{2,1,0:T(8,128)(2,1)} %bitcast.17), calls=%async_computation.5 | async-start | bytes 262144 | tf_op jit(solution)/shard_map/all_to_all | solution.py:448
  162.9 0.1 constant_dynamic-slice_fusion
  162.9 0.1 copy.24
  163.0 13.4 %all-to-all-done.5.grads = bf16[32,16,104]{2,1,0:T(8,128)(2,1)S(1)} async-done(((bf16[32,16,104]{2,1,0:T(8,128)(2,1)}), bf16[32,16,104]{2,1,0:T(8,128)(2,1)S(1)}, u32[]{:S(2)}, u32[]{:S(2)}) %all-to-all-start.5) | async-done | bytes 106528 | tf_op jit(solution)/shard_map/all_to_all | solution.py:448
  176.5 3.2 %adagrad.1 = bf16[8,464,128]{2,1,0:T(8,128)(2,1)S(1)} custom-call(bf16[32,16,104]{2,1,0:T(8,128)(2,1)S(1)} %all-to-all-done.5.grads, bf16[26,16,128]{2,1,0:T(8,128)(2,1)S(1)} %copy-done.2, f32[16,26]{1,0:T(8,128)S(1)} %bitcast.30, f32[8,512]{1,0:T(8,128)S(1)} %slice.10.cross_grads), custom_call_target="tpu_custom_call" | custom-call | tf_op jit(solution)/shard_map/adagrad/pallas_call | solution.py:109
  179.7 17.4 %all_to_all.37.own = bf16[8,464,128]{2,1,0:T(8,128)(2,1)S(1)} all-to-all(bf16[8,464,128]{2,1,0:T(8,128)(2,1)S(1)} %adagrad.1), channel_id=1, replica_groups=mesh['y'=4,'x_hi'=2,'core'=2,'x_lo'=2,'z'=16] {'x_hi','y'}, dimensions={0} | all-to-all | bytes 1900544 | tf_op jit(solution)/shard_map/all_to_all | solution.py:448
  197.1 6.4 %collective-permute-start.5 = (bf16[8,464,128]{2,1,0:T(8,128)(2,1)S(1)}, bf16[8,464,128]{2,1,0:T(8,128)(2,1)S(1)}, u32[]{:S(2)}, u32[]{:S(2)}) collective-permute-start(bf16[8,464,128]{2,1,0:T(8,128)(2,1)S(1)} %all_to_all.37.own), channel_id=1, source_target_pairs={{0,32},{32,0},{1,33},{33,1},{2,34},{34,2},{3,35},{35,3},{4,36},{36... | collective-permute-start | bytes 2850824 | tf_op jit(solution)/shard_map/ppermute | solution.py:456
  203.6 2.1 %collective-permute-done.5.other = bf16[8,464,128]{2,1,0:T(8,128)(2,1)S(1)} collective-permute-done((bf16[8,464,128]{2,1,0:T(8,128)(2,1)S(1)}, bf16[8,464,128]{2,1,0:T(8,128)(2,1)S(1)}, u32[]{:S(2)}, u32[]{:S(2)}) %collective-permute-start.5) | collective-permute-done | bytes 950304 | tf_op jit(solution)/shard_map/ppermute | solution.py:456
  205.7 1.5 unpack.1
  (15 shorter events, 0.1 us)
Async XLA Ops:
  0.6 162.2 %copy-start = (f32[26,256]{1,0:T(8,128)S(1)}, f32[26,256]{1,0:T(8,128)}, u32[]{:S(2)}) copy-start(f32[26,256]{1,0:T(8,128)} %param.8) | copy-start | bytes 79876
  0.6 18.8 %copy-start.5 = (bf16[512,104]{0,1:T(8,128)(2,1)S(1)}, bf16[512,104]{0,1:T(8,128)(2,1)}, u32[]{:S(2)}) copy-start(bf16[512,104]{0,1:T(8,128)(2,1)} %param.13) | copy-start | bytes 319492
  0.7 18.8 %copy-start.3 = (bf16[104,256]{1,0:T(8,128)(2,1)S(1)}, bf16[104,256]{1,0:T(8,128)(2,1)}, u32[]{:S(2)}) copy-start(bf16[104,256]{1,0:T(8,128)(2,1)} %v.3) | copy-start | bytes 159748
  0.7 18.8 %copy-start.4 = (bf16[104,256]{1,0:T(8,128)(2,1)S(1)}, bf16[104,256]{1,0:T(8,128)(2,1)}, u32[]{:S(2)}) copy-start(bf16[104,256]{1,0:T(8,128)(2,1)} %u.3) | copy-start | bytes 159748
  2.4 31.0 %all-to-all-start = ((bf16[32,16,104]{2,1,0:T(8,128)(2,1)}), bf16[32,16,104]{2,1,0:T(8,128)(2,1)S(1)}, u32[]{:S(2)}, u32[]{:S(2)}) async-start(bf16[32,16,104]{2,1,0:T(8,128)(2,1)} %get-tuple-element.27), calls=%async_computation | async-start | bytes 262144 | tf_op jit(solution)/shard_map/all_to_all | solution.py:448
  19.4 21.6 %copy-start.1 = (s32[512,26,8]{0,2,1:T(8,128)S(1)}, s32[512,26,8]{0,2,1:T(8,128)}, u32[]{:S(2)}) copy-start(s32[512,26,8]{0,2,1:T(8,128)} %param.9) | copy-start | bytes 1277956
  19.5 14.1 %collective-permute-start = (bf16[104,768]{1,0:T(8,128)(2,1)S(1)}, bf16[104,768]{1,0:T(8,128)(2,1)S(1)}, u32[]{:S(2)}, u32[]{:S(2)}) collective-permute-start(bf16[104,768]{1,0:T(8,128)(2,1)S(1)} %pad_maximum_fusion), channel_id=1, source_target_pairs={{0,16},{16,0},{1,17},{17,1},{2,18},{18,2},{3,19},{19,3},{4,20},{20... | collective-permute-start | bytes 479240 | tf_op jit(solution)/shard_map/ppermute | solution.py:456
  34.6 16.5 %all-to-all-start.1 = ((bf16[8,104,512]{2,1,0:T(8,128)(2,1)}), bf16[8,104,512]{2,1,0:T(8,128)(2,1)S(1)}, u32[]{:S(2)}, u32[]{:S(2)}) async-start(bf16[8,104,512]{2,1,0:T(8,128)(2,1)} %broadcast_in_dim.12), calls=%async_computation.1 | async-start | bytes 1703936 | tf_op jit(solution)/shard_map/all_to_all | solution.py:448
  45.8 1.3 copy-start.6
  47.2 1.3 copy-start.9
  51.1 10.9 %collective-permute-start.1 = (bf16[8,104,512]{2,1,0:T(8,128)(2,1)S(1)}, bf16[8,104,512]{2,1,0:T(8,128)(2,1)S(1)}, u32[]{:S(2)}, u32[]{:S(2)}) collective-permute-start(bf16[8,104,512]{2,1,0:T(8,128)(2,1)S(1)} %all-to-all-done.1.refs_0_), channel_id=1, source_target_pairs={{0,32},{32,0},{1,33},{33,1},{2,34},{34,2},{3,35},{35,3},{4,36},{36... | collective-permute-start | bytes 2555912 | tf_op jit(solution)/shard_map/ppermute | solution.py:456
  58.2 1.6 copy-start.7
  62.0 5.3 %copy-start.10 = (s32[2,2,8,64,256]{4,3,2,1,0:T(8,128)S(1)}, s32[2,2,8,64,256]{4,3,2,1,0:T(8,128)}, u32[]{:S(2)}) copy-start(s32[2,2,8,64,256]{4,3,2,1,0:T(8,128)} %copy-done.9) | copy-start | bytes 6291460
  64.1 6.2 %collective-permute-start.2 = (bf16[104,256]{1,0:T(8,128)(2,1)S(1)}, bf16[104,256]{1,0:T(8,128)(2,1)S(1)}, u32[]{:S(2)}, u32[]{:S(2)}) collective-permute-start(bf16[104,256]{1,0:T(8,128)(2,1)S(1)} %bags.5.pooled), channel_id=1, source_target_pairs={{0,16},{16,0},{1,17},{17,1},{2,18},{18,2},{3,19},{19,3},{4,20},{20... | collective-permute-start | bytes 159752 | tf_op jit(solution)/shard_map/ppermute | solution.py:456
  70.3 29.4 %copy-start.12 = (f32[104]{0:T(128)S(1)}, f32[104]{0:T(128)}, u32[]{:S(2)}) copy-start(f32[104]{0:T(128)} %param.12) | copy-start | bytes 1252
  88.7 24.1 %all-to-all-start.3 = ((bf16[16,32,256]{2,1,0:T(8,128)(2,1)}), bf16[16,32,256]{2,1,0:T(8,128)(2,1)S(1)}, u32[]{:S(2)}, u32[]{:S(2)}) async-start(bf16[16,32,256]{2,1,0:T(8,128)(2,1)} %broadcast_in_dim.13), calls=%async_computation.3 | async-start | bytes 524288 | tf_op jit(solution)/shard_map/all_to_all | solution.py:448
  112.8 10.0 %copy-start.8 = (s32[2,2,8,64,256]{4,3,2,1,0:T(8,128)S(1)}, s32[2,2,8,64,256]{4,3,2,1,0:T(8,128)}, u32[]{:S(2)}) copy-start(s32[2,2,8,64,256]{4,3,2,1,0:T(8,128)} %copy-done.6) | copy-start | bytes 6291460
  112.8 10.0 %collective-permute-start.3 = (bf16[512,256]{1,0:T(8,128)(2,1)S(1)}, bf16[512,256]{1,0:T(8,128)(2,1)S(1)}, u32[]{:S(2)}, u32[]{:S(2)}) collective-permute-start(bf16[512,256]{1,0:T(8,128)(2,1)S(1)} %bitcast.27), channel_id=1, source_target_pairs={{0,16},{16,0},{1,17},{17,1},{2,18},{18,2},{3,19},{19,3},{4,20},{20... | collective-permute-start | bytes 786440 | tf_op jit(solution)/shard_map/ppermute | solution.py:456
  116.4 1.6 copy-start.11
  126.2 10.5 %collective-permute-start.4 = (bf16[8,112,512]{2,1,0:T(8,128)(2,1)S(1)}, bf16[8,112,512]{2,1,0:T(8,128)(2,1)S(1)}, u32[]{:S(2)}, u32[]{:S(2)}) collective-permute-start(bf16[8,112,512]{2,1,0:T(8,128)(2,1)S(1)} %get-tuple-element.41), channel_id=1, source_target_pairs={{0,32},{32,0},{1,33},{33,1},{2,34},{34,2},{3,35},{35,3},{4,36},{36... | collective-permute-start | bytes 2752520 | tf_op jit(solution)/shard_map/ppermute | solution.py:456
  137.0 39.5 %copy-start.2 = (bf16[26,16,128]{2,1,0:T(8,128)(2,1)S(1)}, bf16[26,16,128]{2,1,0:T(8,128)(2,1)}, u32[]{:S(2)}) copy-start(bf16[26,16,128]{2,1,0:T(8,128)(2,1)} %get-tuple-element.42.rows) | copy-start | bytes 319492
  156.2 20.2 %all-to-all-start.5 = ((bf16[32,16,104]{2,1,0:T(8,128)(2,1)}), bf16[32,16,104]{2,1,0:T(8,128)(2,1)S(1)}, u32[]{:S(2)}, u32[]{:S(2)}) async-start(bf16[32,16,104]{2,1,0:T(8,128)(2,1)} %bitcast.17), calls=%async_computation.5 | async-start | bytes 262144 | tf_op jit(solution)/shard_map/all_to_all | solution.py:448
  197.1 8.6 %collective-permute-start.5 = (bf16[8,464,128]{2,1,0:T(8,128)(2,1)S(1)}, bf16[8,464,128]{2,1,0:T(8,128)(2,1)S(1)}, u32[]{:S(2)}, u32[]{:S(2)}) collective-permute-start(bf16[8,464,128]{2,1,0:T(8,128)(2,1)S(1)} %all_to_all.37.own), channel_id=1, source_target_pairs={{0,32},{32,0},{1,33},{33,1},{2,34},{34,2},{3,35},{35,3},{4,36},{36... | collective-permute-start | bytes 2850824 | tf_op jit(solution)/shard_map/ppermute | solution.py:456

commit v5 on v4

v5 whole, which is shorter than its diff:
```python
import functools

import jax
import jax.numpy as jnp
from jax import lax
from jax.experimental import pallas as pl
from jax.experimental.pallas import tpu as pltpu
from jax.sharding import Mesh
from jax.sharding import PartitionSpec as P

bf16 = jnp.bfloat16
f32 = jnp.float32
learn_rate = 0.3
epsilon = 1e-06

SAMPLES, TABLES, BAG, ROWS, WIDTH, FEATS, RANK = 512, 26, 8, 256, 128, 104, 256
N_ROW, N_DP, PART = 32, 16, 16
STEP_ROWS = N_ROW * PART
WORDS = STEP_ROWS // 8
HALF = SAMPLES // 2
GRAD_ROWS = 8
OUT_ROWS = FEATS + GRAD_ROWS
DP_OUTER = ("x_hi", "y")
ROW_AXES = ("z", "x_lo")
ROW_ALL = ("x_lo", "z")
BLOCK_OF = [(i & 1) * 16 + (i >> 1) for i in range(N_ROW)]
CHUNK = TABLES * PART + 16 + 32
UNROLL = 2
VMEM = 16 << 20

NT_DIMS = (((1,), (1,)), ((), ()))
TN_DIMS = (((0,), (0,)), ((), ()))


def part_of(outer, core):
    return (outer & 3) * 4 + (outer >> 2) * 2 + core


def pieces(table):
    found = []
    for block in range(N_ROW):
        low = max(table * WIDTH, block * FEATS)
        high = min((table + 1) * WIDTH, (block + 1) * FEATS)
        if low < high:
            found.append((block, low - block * FEATS, high - block * FEATS))
    return found


def pack_kernel(scalars, rows, mine, packed):
    mine[...] = rows[...]
    for device, block in enumerate(BLOCK_OF):
        first = block * FEATS // WIDTH
        start = block * FEATS - first * WIDTH
        cut = rows[first][:, start:].astype(f32)
        if cut.shape[1] < FEATS:
            cut = jnp.concatenate([cut, rows[first + 1][:, : FEATS - cut.shape[1]].astype(f32)], axis=1)
        packed[device] = cut[:, :FEATS].astype(bf16)


def pack(scalars, rows):
    return pl.pallas_call(
        pack_kernel,
        grid_spec=pltpu.PrefetchScalarGridSpec(
            num_scalar_prefetch=1,
            grid=(1,),
            in_specs=[pl.BlockSpec((TABLES, PART, WIDTH), lambda g, s: (0, s[0], 0))],
            out_specs=[
                pl.BlockSpec((TABLES, PART, WIDTH), lambda g, s: (0, 0, 0)),
                pl.BlockSpec((N_ROW, PART, FEATS), lambda g, s: (0, 0, 0)),
            ],
        ),
        out_shape=[
            jax.ShapeDtypeStruct((TABLES, PART, WIDTH), bf16),
            jax.ShapeDtypeStruct((N_ROW, PART, FEATS), bf16),
        ],
        name="pack_rows",
    )(scalars, rows)


def adagrad_kernel(grads_in, rows, accum, cross_grads, out):
    device_of = {block: device for device, block in enumerate(BLOCK_OF)}
    grads = [
        jnp.concatenate([grads_in[device_of[block]].astype(f32)[:, low:high] for block, low, high in pieces(table)], axis=1)
        for table in range(TABLES)
    ]
    grad = jnp.concatenate(grads, axis=0)
    square = grad * grad
    high = square.astype(bf16)
    rest = (square - high.astype(f32)).astype(bf16)
    ones = jnp.ones((WIDTH, WIDTH), bf16)
    sums = jnp.dot(high, ones, preferred_element_type=f32) + jnp.dot(rest, ones, preferred_element_type=f32)
    total = accum[...] + sums * (1.0 / WIDTH)
    new = (rows[...].astype(f32) - learn_rate * grad * lax.rsqrt(total + epsilon)).astype(bf16)
    lane = lax.broadcasted_iota(jnp.int32, (PART, WIDTH), 1)
    accum_out = jnp.zeros((PART, WIDTH), f32)
    for table in range(TABLES):
        mine = total[table * PART : (table + 1) * PART]
        high = mine.astype(bf16).astype(f32)
        rest = mine - high
        middle = rest.astype(bf16).astype(f32)
        accum_out = jnp.where(lane == table, high, accum_out)
        accum_out = jnp.where(lane == table + 32, middle, accum_out)
        accum_out = jnp.where(lane == table + 64, rest - middle, accum_out)
    terms = accum_out.astype(bf16)
    wide = cross_grads[...]
    wide = jnp.concatenate([wide[:, at : at + WIDTH] for at in range(0, 2 * RANK, WIDTH)], axis=0).astype(bf16)
    for copy in range(8):
        out[copy, : TABLES * PART, :] = new
        out[copy, TABLES * PART : TABLES * PART + PART, :] = terms
        out[copy, TABLES * PART + PART :, :] = wide


def adagrad(grads, rows, accum, cross_grads):
    return pl.pallas_call(
        adagrad_kernel,
        out_shape=jax.ShapeDtypeStruct((8, CHUNK, WIDTH), bf16),
        compiler_params=pltpu.CompilerParams(vmem_limit_bytes=VMEM),
        name="adagrad",
    )(grads, rows, accum, cross_grads)


def unpack_kernel(scalars, own, other, rows_out, accum_out, grad_v, grad_u, grad_bias, accums, cross_grads):
    for outer in range(8):
        for turn, source in enumerate((own, other)):
            part = part_of(outer, turn ^ scalars[0])
            rows_out[:, pl.ds(part, 1)] = source[outer, : TABLES * PART].reshape(TABLES, 1, PART, WIDTH)
            terms = source[outer, TABLES * PART : TABLES * PART + PART].astype(f32)
            total = terms[:, :32] + terms[:, 32:64] + terms[:, 64:96]
            accums[pl.ds(pl.multiple_of(part * PART, PART), PART), :] = jnp.concatenate(
                [total, jnp.zeros((PART, WIDTH - 32), f32)], axis=1
            )
            wide = source[outer, TABLES * PART + PART :].astype(f32)
            at = pl.multiple_of(part * GRAD_ROWS, GRAD_ROWS)
            for i in range(4):
                cross_grads[pl.ds(at, GRAD_ROWS), i * WIDTH : (i + 1) * WIDTH] = wide[i * 8 : (i + 1) * 8]
    accum_out[...] = accums[...].T[:TABLES]
    grad_u[...] = cross_grads[:FEATS, :RANK]
    grad_v[...] = cross_grads[:FEATS, RANK:]
    grad_bias[...] = cross_grads[FEATS, :FEATS]


def unpack(scalars, own, other):
    shapes = [
        ((TABLES, N_DP, PART, WIDTH), bf16),
        ((TABLES, ROWS), f32),
        ((FEATS, RANK), f32),
        ((FEATS, RANK), f32),
        ((FEATS,), f32),
    ]
    return call(
        unpack_kernel,
        "unpack",
        scalars,
        (own, other),
        [jax.ShapeDtypeStruct(shape, kind) for shape, kind in shapes],
        [pltpu.VMEM((ROWS, WIDTH), f32), pltpu.VMEM((N_DP * GRAD_ROWS, 2 * RANK), f32)],
    )


def counts_of(words, scaled=False):
    columns = []
    for lane in range(0, words.shape[1], 128):
        blocks = []
        for group in range(0, WORDS, 8):
            word = words[group : group + 8, lane : lane + 128]
            if scaled:
                digits = [word & jnp.int32(15 << (4 * j)) for j in range(7)]
            else:
                digits = [lax.shift_right_logical(word, jnp.int32(4 * j)) & 15 for j in range(7)]
            digits.append(lax.shift_right_logical(word, jnp.int32(28)))
            blocks.append(jnp.concatenate(digits, axis=0).astype(f32).astype(bf16))
        columns.append(jnp.concatenate(blocks, axis=0))
    return jnp.concatenate(columns, axis=1)


def words_of(place):
    inside = (place >= 0) & (place < STEP_ROWS)
    word = jnp.where(inside, ((place >> 6) << 3) | (place & 7), -1)
    unit = jnp.left_shift(jnp.int32(1), ((place >> 3) & 7) * 4)
    columns = []
    for lane in range(0, place.shape[1], 128):
        slots = lax.broadcasted_iota(jnp.int32, (WORDS, 128), 0)
        total = jnp.zeros((WORDS, 128), jnp.int32)
        for k in range(BAG):
            here = word[k : k + 1, lane : lane + 128] == slots
            total = total + jnp.where(here, unit[k : k + 1, lane : lane + 128], 0)
        columns.append(total)
    return jnp.concatenate(columns, axis=1)


def whole(*shape):
    return pl.BlockSpec(shape, lambda g, s: (0,) * len(shape))


def words_kernel(scalars, *refs):
    ids, kept, sent, places = refs[:4], refs[4], refs[5:7], refs[7]
    step = pl.program_id(0)

    @pl.when(step == 0)
    def _():
        for i in range(4):
            row = ids[i][0]
            part = (row >> 4) & 15
            turn = (part & 1) ^ scalars[2]
            outer = (((part >> 1) & 1) << 2) | (part >> 2)
            device = (((row >> 8) & 15) << 1) | (row >> 12)
            places[i] = turn * 4096 + outer * 512 + device * 16 + (row & 15)

    for table in range(2):
        for turn in range(2):
            first = (turn * 8 + step) * STEP_ROWS
            kept[table, turn, 0] = words_of(places[table] - first)
            sent[turn][table, 0, 0] = words_of(places[2 + table] - first)


def bag_words(scalars, ids):
    return pl.pallas_call(
        words_kernel,
        grid_spec=pltpu.PrefetchScalarGridSpec(
            num_scalar_prefetch=1,
            grid=(8,),
            in_specs=[
                pl.BlockSpec((1, BAG, HALF), lambda g, s: (s[0], 0, s[3])),
                pl.BlockSpec((1, BAG, HALF), lambda g, s: (s[1], 0, s[3])),
                pl.BlockSpec((1, BAG, HALF), lambda g, s: (s[0], 0, 1 - s[3])),
                pl.BlockSpec((1, BAG, HALF), lambda g, s: (s[1], 0, 1 - s[3])),
            ],
            out_specs=[pl.BlockSpec((2, turns, 1, WORDS, HALF), lambda g, s: (0, 0, g, 0, 0)) for turns in (2, 1, 1)],
            scratch_shapes=[pltpu.VMEM((4, BAG, HALF), jnp.int32)],
        ),
        out_shape=[jax.ShapeDtypeStruct((2, turns, 8, WORDS, HALF), jnp.int32) for turns in (2, 1, 1)],
        compiler_params=pltpu.CompilerParams(vmem_limit_bytes=VMEM),
        cost_estimate=pl.CostEstimate(flops=1 << 28, bytes_accessed=5 << 20, transcendentals=0),
        name="bag_words",
    )(scalars, ids, ids, ids, ids)


KERNEL_COST = pl.CostEstimate(flops=1 << 32, bytes_accessed=5 << 20, transcendentals=0)


def call(kernel, name, scalars, operands, out_shape, scratch_shapes=()):
    return pl.pallas_call(
        kernel,
        in_specs=[pl.BlockSpec(memory_space=pltpu.SMEM)] + [pl.BlockSpec(memory_space=pltpu.VMEM)] * len(operands),
        out_shape=out_shape,
        scratch_shapes=list(scratch_shapes),
        compiler_params=pltpu.CompilerParams(vmem_limit_bytes=VMEM),
        cost_estimate=KERNEL_COST,
        name=name,
    )(scalars, *operands)


def half_of(scalars):
    return pl.ds(pl.multiple_of(scalars[0] * HALF, HALF), HALF)


def forward_kernel(turns, last, scalars, words, *refs):
    rows, refs = refs[:turns], refs[turns:]
    if last:
        *before, pooled_out, total = refs
    else:
        before, total = refs[:-1], refs[-1]
    total[...] = before[0][...] if before else jnp.zeros_like(total)

    @pl.loop(0, 8 // UNROLL)
    def _(step):
        for table in range(2):
            added = None
            for i in range(UNROLL):
                for turn, source in enumerate(rows):
                    counts = counts_of(words[table, turn, step * UNROLL + i], scaled=True)
                    term = jnp.dot(source[step * UNROLL + i], counts, preferred_element_type=f32)
                    added = term if added is None else added + term
            total[table] += added

    if last:
        feature = lax.broadcasted_iota(jnp.int32, (FEATS, HALF), 0)
        pooled_out[...] = jnp.where(feature < scalars[1], total[0], total[1]).astype(bf16)


def forward(scalars, words, rows, before=None, last=True):
    operands = [words, *rows] if before is None else [words, *rows, before]
    if last:
        out_shape, scratch = jax.ShapeDtypeStruct((FEATS, HALF), bf16), [pltpu.VMEM((2, FEATS, HALF), f32)]
    else:
        out_shape, scratch = jax.ShapeDtypeStruct((2, FEATS, HALF), f32), []
    return call(functools.partial(forward_kernel, len(rows), last), "bags", scalars, operands, out_shape, scratch)


def ranks_kernel(scalars, pooled_a, pooled_b, v_a, u_a, upstream_a, partner, ranks):
    rank = jnp.zeros((RANK, HALF), f32)
    rank_grad = jnp.zeros((RANK, HALF), f32)
    sides = (
        (pooled_a[...], v_a[...], u_a[...], upstream_a[:, half_of(scalars)]),
        (pooled_b[...], partner[:, :RANK], partner[:, RANK : 2 * RANK], partner[:, 2 * RANK :]),
    )
    for pooled, v, u, upstream in sides:
        gate_grad = (upstream.astype(f32) * pooled.astype(f32)).astype(bf16)
        rank += lax.dot_general(v, pooled, TN_DIMS, preferred_element_type=f32)
        rank_grad += lax.dot_general(u, gate_grad, TN_DIMS, preferred_element_type=f32)
    ranks[:RANK] = rank.astype(bf16)
    ranks[RANK:] = rank_grad.astype(bf16)


def rank_terms(scalars, *operands):
    return call(ranks_kernel, "rank_terms", scalars, operands, jax.ShapeDtypeStruct((2 * RANK, HALF), bf16))


def cross_layer(scalars, ranks, pooled_in, v, u, bias, upstream_in, grads, cross_grads):
    rank = ranks[:RANK]
    rank_grad = ranks[RANK:]
    pooled_bf = pooled_in[...]
    pooled = pooled_bf.astype(f32)
    upstream = upstream_in[:, half_of(scalars)].astype(f32)
    gate = jnp.dot(u[...], rank, preferred_element_type=f32) + bias[...]
    crossed = (pooled * gate + pooled).astype(bf16)
    back = jnp.dot(v[...], rank_grad, preferred_element_type=f32)
    grad = (upstream * (gate + 1.0) + back).astype(bf16).astype(f32)
    feature = lax.broadcasted_iota(jnp.int32, (FEATS, HALF), 0)
    grads[0] = jnp.where(feature < scalars[1], grad, 0.0).astype(bf16)
    grads[1] = jnp.where(feature < scalars[1], 0.0, grad).astype(bf16)
    gate_grad = upstream * pooled
    gate_bf = gate_grad.astype(bf16)
    gate_rest = (gate_grad - gate_bf.astype(f32)).astype(bf16)
    cross_grads[...] = jnp.zeros_like(cross_grads)
    cross_grads[:FEATS, :RANK] = lax.dot_general(gate_bf, rank, NT_DIMS, preferred_element_type=f32)
    cross_grads[:FEATS, RANK:] = lax.dot_general(pooled_bf, rank_grad, NT_DIMS, preferred_element_type=f32)
    ones = jnp.ones((16, HALF), bf16)
    bias_sum = lax.dot_general(ones, gate_bf, NT_DIMS, preferred_element_type=f32) + lax.dot_general(
        ones, gate_rest, NT_DIMS, preferred_element_type=f32
    )
    cross_grads[FEATS : FEATS + 8, :FEATS] = bias_sum[:8]
    return crossed


def row_grads(scalars, turns, words, grads, cross_grads, before, outs):
    @pl.loop(0, 8 // UNROLL)
    def _(step):
        for i in range(UNROLL):
            at = step * UNROLL + i
            for n, turn in enumerate(turns):
                part = part_of(at, turn ^ scalars[2])
                result = lax.dot_general(grads[0], counts_of(words[0, n, at]), NT_DIMS, preferred_element_type=f32)
                result += lax.dot_general(grads[1], counts_of(words[1, n, at]), NT_DIMS, preferred_element_type=f32)
                extra = cross_grads[pl.ds(pl.multiple_of(part * GRAD_ROWS, GRAD_ROWS), GRAD_ROWS), :]
                block = jnp.concatenate([result, extra], axis=0)
                if before is not None:
                    block = block + before[at]
                outs[n][at] = block.astype(outs[n].dtype)


def first_kernel(scalars, words, ranks, pooled, v, u, bias, upstream, crossed, own, other, grads, cross_grads):
    crossed[...] = cross_layer(scalars, ranks, pooled, v, u, bias, upstream, grads, cross_grads)
    row_grads(scalars, (0, 1), words, grads, cross_grads, None, (own, other))


def second_kernel(
    scalars, words, ranks, pooled, v, u, bias, upstream, before, first, crossed, grads, cross_grads, other
):
    mine = cross_layer(scalars, ranks, pooled, v, u, bias, upstream, grads, cross_grads)
    crossed[:, half_of(scalars)] = mine
    crossed[:, pl.ds(pl.multiple_of((1 - scalars[0]) * HALF, HALF), HALF)] = first[...]
    row_grads(scalars, (1,), words, grads, cross_grads, before, (other,))


def rest_kernel(scalars, words, grads, cross_grads, before, own):
    row_grads(scalars, (0,), words, grads, cross_grads, before, (own,))


SUMS = (8, OUT_ROWS, STEP_ROWS)
GRADS = (2, FEATS, HALF)
CROSS_GRADS = (N_DP * GRAD_ROWS, 2 * RANK)


def first_backward(scalars, *operands):
    return call(
        first_kernel,
        "cross_and_row_grads",
        scalars,
        operands,
        [jax.ShapeDtypeStruct((FEATS, HALF), bf16), jax.ShapeDtypeStruct(SUMS, f32), jax.ShapeDtypeStruct(SUMS, f32)],
        [pltpu.VMEM(GRADS, bf16), pltpu.VMEM(CROSS_GRADS, f32)],
    )


def second_backward(scalars, *operands):
    return call(
        second_kernel,
        "cross_and_row_grads",
        scalars,
        operands,
        [
            jax.ShapeDtypeStruct((FEATS, SAMPLES), bf16),
            jax.ShapeDtypeStruct(GRADS, bf16),
            jax.ShapeDtypeStruct(CROSS_GRADS, f32),
            jax.ShapeDtypeStruct(SUMS, bf16),
        ],
    )


def rest_of_backward(scalars, *operands):
    return call(rest_kernel, "row_grads", scalars, operands, jax.ShapeDtypeStruct(SUMS, bf16))


def exchange(x, axes):
    return lax.all_to_all(x, axes, 0, 0, tiled=True)


def spread(x, axes, count):
    return exchange(jnp.broadcast_to(x, (count,) + x.shape), axes)


def swap(x, axis):
    return lax.ppermute(x, axis, [(0, 1), (1, 0)])


def to_other_core(x):
    return swap(x, "core")


def body(rows_in, accum, bag_ids, cross_v, cross_u, cross_bias, upstream):
    block = lax.axis_index("x_lo") * 16 + lax.axis_index("z")
    core = lax.axis_index("core")
    part = part_of(lax.axis_index(DP_OUTER), core)
    table_a = (block * FEATS) // WIDTH
    table_b = jnp.minimum(table_a + 1, TABLES - 1)
    n_a = jnp.minimum(FEATS, WIDTH * (table_a + 1) - FEATS * block)

    upstream_t = upstream.T
    sent_upstream = lax.dynamic_slice(upstream_t, (0, (1 - lax.axis_index("x_lo")) * HALF), (FEATS, HALF))
    partner = swap(jnp.concatenate([cross_v, cross_u, sent_upstream], axis=1), "x_lo")

    my_rows, packed = pack(jnp.stack([part]).astype(jnp.int32), rows_in)
    mine = exchange(packed, ROW_AXES).reshape(STEP_ROWS, FEATS).T
    nibble = (jnp.arange(STEP_ROWS) >> 3) & 7
    mine = mine * jnp.where(nibble == 7, 1.0, jnp.exp2(-4.0 * nibble)).astype(bf16)
    mine, partner = lax.optimization_barrier((mine, partner))
    own = spread(mine, DP_OUTER, 8)
    keep = lax.axis_index("x_lo")
    scalars = jnp.stack([table_a, table_b, core, keep]).astype(jnp.int32)
    at_keep = jnp.stack([keep, n_a, core]).astype(jnp.int32)
    at_sent = jnp.stack([1 - keep, n_a, core]).astype(jnp.int32)
    words = bag_words(scalars, bag_ids.transpose(1, 2, 0))
    own, kept_words, own_words, other_words = lax.optimization_barrier((own, *words))
    other = to_other_core(own)

    sent_sums = forward(at_sent, own_words, [own], last=False)
    sent_pooled = forward(at_sent, other_words, [other], before=sent_sums)
    partner_pooled = swap(sent_pooled, "x_lo")
    kept_pooled = forward(at_keep, kept_words, [own, other])

    terms = rank_terms(at_keep, kept_pooled, partner_pooled, cross_v, cross_u, upstream_t, partner)
    gathered = exchange(terms.reshape(16, 32, HALF), "z")
    ranks = spread(jnp.sum(gathered.astype(f32), axis=0).astype(bf16), "z", 16).reshape(2 * RANK, HALF)
    sent_ranks = swap(ranks, "x_lo")

    cross = (cross_v, cross_u, cross_bias.reshape(FEATS, 1), upstream_t)
    crossed, own, other = first_backward(at_keep, kept_words, ranks, kept_pooled, *cross)
    crossed, grads, cross_grads, other = second_backward(
        at_sent, other_words, sent_ranks, sent_pooled, *cross, other, crossed
    )
    from_other = to_other_core(other)
    own = rest_of_backward(at_sent, own_words, grads, cross_grads, own)

    chip_sum = (own.astype(f32) + from_other.astype(f32)).astype(bf16)
    sums = jnp.sum(exchange(chip_sum, DP_OUTER).astype(f32), axis=0)
    row_grad = exchange(sums[:FEATS].astype(bf16).T.reshape(N_ROW, PART, FEATS), ROW_AXES)
    my_accum = lax.dynamic_slice(accum, (0, part * PART), (TABLES, PART))
    my_accum = jnp.broadcast_to(my_accum[:, :, None], (TABLES, PART, WIDTH)).reshape(TABLES * PART, WIDTH)

    own = exchange(
        adagrad(row_grad, my_rows.reshape(TABLES * PART, WIDTH), my_accum, sums[FEATS:]), DP_OUTER
    )
    new_rows, new_accum, grad_v, grad_u, grad_bias = unpack(
        jnp.stack([core]).astype(jnp.int32), own, to_other_core(own)
    )
    return (crossed.T, new_rows.reshape(TABLES, ROWS, WIDTH), new_accum, grad_v, grad_u, grad_bias)


def solution(mesh):
    inner = Mesh(mesh.devices.reshape(4, 2, 2, 2, 16), ("y", "x_hi", "core", "x_lo", "z"))
    dp = ("y", "x_hi", "core")
    row = ROW_ALL
    return jax.shard_map(
        body,
        mesh=inner,
        in_specs=(
            P(None, row, None),
            P(None, row),
            P(dp, None, None),
            P(row, None),
            P(row, None),
            P(row),
            P(dp, row),
        ),
        out_specs=(
            P(dp, row),
            P(None, row, None),
            P(None, row),
            P(row, None),
            P(row, None),
            P(row),
        ),
        check_vma=False,
    )
```

time: 208 us -> 203 us (0.976)
  Pallas kernels: 30.3 us -> 25.9 us
    pallas_call x1, Pallas kernels: 3.23 us -> 0.35 us  [adagrad(): pl.pallas_call(adagrad_kernel, out_shape=jax.ShapeDtypeStruct((8, CHUNK,...]
    unnamed x27 -> x30, local copies, waits for them, and re-layouts: 5.93 us -> 3.95 us
where the time goes in v5:
time: 203 us; the launch traced here: 202 us
  starting transfers between devices  73 us (36%)
  blocking collectives  52.3 us (26%)
  waiting for transfers between devices  42.2 us (21%)
  Pallas kernels  25.9 us (13%)
  local copies, waits for them, and re-layouts  6.91 us (3%)
    all_to_all x3, blocking collectives, exchange(): return lax.all_to_all(x, axes, 0, 0, tiled=True)  52.3 us
    all_to_all x4, starting transfers between devices, exchange(): return lax.all_to_all(x, axes, 0, 0, tiled=True)  41.6 us
    all_to_all x4, waiting for transfers between devices, exchange(): return lax.all_to_all(x, axes, 0, 0, tiled=True)  40.1 us
    ppermute x6, starting transfers between devices, swap(): return lax.ppermute(x, axis, [(0, 1), (1, 0)])  31.4 us
    pallas_call x8, Pallas kernels, call(): pl.pallas_call(kernel, in_specs=[pl.BlockSpec(memory_space=pltpu.SMEM)] +...  19.1 us
    pallas_call x1, Pallas kernels, bag_words(): pl.pallas_call(words_kernel, grid_spec=pltpu.PrefetchScalarGridSpec(num_s...  4.7 us
  transfers between devices with their start and end apart: 10, of which 5 were waited for; matrix products, arithmetic and copies ran while one was open for 0% of the time, Pallas kernels for 8%

profile of v5, /device:TPU:1, one launch (start us, length us, event | category | flops | bytes accessed | tf_op | source)
XLA Modules:
  0.0 202.1 jit_solution(11748768687614398549)
XLA Ops:
  0.6 0.0 copy-start
  0.6 0.0 copy-start.5
  0.7 0.0 copy-start.3
  0.7 0.0 copy-start.4
  0.7 1.7 pack_rows.1
  2.4 17.0 %all-to-all-start = ((bf16[32,16,104]{2,1,0:T(8,128)(2,1)}), bf16[32,16,104]{2,1,0:T(8,128)(2,1)S(1)}, u32[]{:S(2)}, u32[]{:S(2)}) async-start(bf16[32,16,104]{2,1,0:T(8,128)(2,1)} %get-tuple-element.29), calls=%async_computation | async-start | bytes 262144 | tf_op jit(solution)/shard_map/all_to_all | solution.py:406
  19.4 0.0 copy-start.1
  19.4 0.0 copy-done.5
  19.5 0.0 copy-done.3
  19.5 0.0 copy-done.4
  19.5 3.3 %collective-permute-start = (bf16[104,768]{1,0:T(8,128)(2,1)S(1)}, bf16[104,768]{1,0:T(8,128)(2,1)S(1)}, u32[]{:S(2)}, u32[]{:S(2)}) collective-permute-start(bf16[104,768]{1,0:T(8,128)(2,1)S(1)} %pad_maximum_fusion), channel_id=1, source_target_pairs={{0,16},{16,0},{1,17},{17,1},{2,18},{18,2},{3,19},{19,3},{4,20},{20... | collective-permute-start | bytes 479240 | tf_op jit(solution)/shard_map/ppermute | solution.py:414
  22.8 10.7 %all-to-all-done = bf16[32,16,104]{2,1,0:T(8,128)(2,1)S(1)} async-done(((bf16[32,16,104]{2,1,0:T(8,128)(2,1)}), bf16[32,16,104]{2,1,0:T(8,128)(2,1)S(1)}, u32[]{:S(2)}, u32[]{:S(2)}) %all-to-all-start) | async-done | bytes 106528 | tf_op jit(solution)/shard_map/all_to_all | solution.py:406
  33.4 0.1 copy.17
  33.6 0.0 collective-permute-done.partner
  33.6 0.0 copy-start.12
  33.6 1.0 broadcast_in_dim.20
  34.6 0.0 copy-done.12
  34.6 6.4 %all-to-all-start.1 = ((bf16[8,104,512]{2,1,0:T(8,128)(2,1)}), bf16[8,104,512]{2,1,0:T(8,128)(2,1)S(1)}, u32[]{:S(2)}, u32[]{:S(2)}) async-start(bf16[8,104,512]{2,1,0:T(8,128)(2,1)} %broadcast_in_dim.20), calls=%async_computation.1 | async-start | bytes 1703936 | tf_op jit(solution)/shard_map/all_to_all | solution.py:406
  40.9 0.1 pad_add_fusion.scalars
  41.0 4.7 %bag_words.1 = (s32[2,2,8,64,256]{4,3,2,1,0:T(8,128)S(1)}, s32[2,1,8,64,256]{4,3,2,1,0:T(8,128)S(1)}, s32[2,1,8,64,256]{4,3,2,1,0:T(8,128)S(1)}) custom-call(s32[4]{0:T(128)S(1)} %pad_add_fusion.scalars, s32[26,8,512]{2,1,0:T(8,128)S(1)} %bitcast.23, s32[26,8,512]{2,1,0:T(8,128)S(1)} %bitcast.24, s32[26,8,512]{2,1,0:T(8,128)S(1)} %bitcast.25, ...), custom_call_target="tpu_custom_call" | custom-call | flops 268435456 | bytes 5242880 | tf_op jit(solution)/shard_map/bag_words/pallas_call | solution.py:217
  45.7 1.3 copy-done.6
  47.1 1.0 copy-done.9
  48.0 3.0 %all-to-all-done.1.refs_0_ = bf16[8,104,512]{2,1,0:T(8,128)(2,1)S(1)} async-done(((bf16[8,104,512]{2,1,0:T(8,128)(2,1)}), bf16[8,104,512]{2,1,0:T(8,128)(2,1)S(1)}, u32[]{:S(2)}, u32[]{:S(2)}) %all-to-all-start.1) | async-done | bytes 852000 | tf_op jit(solution)/shard_map/all_to_all | solution.py:406
  51.1 7.0 %collective-permute-start.1 = (bf16[8,104,512]{2,1,0:T(8,128)(2,1)S(1)}, bf16[8,104,512]{2,1,0:T(8,128)(2,1)S(1)}, u32[]{:S(2)}, u32[]{:S(2)}) collective-permute-start(bf16[8,104,512]{2,1,0:T(8,128)(2,1)S(1)} %all-to-all-done.1.refs_0_), channel_id=1, source_target_pairs={{0,32},{32,0},{1,33},{33,1},{2,34},{34,2},{3,35},{35,3},{4,36},{36... | collective-permute-start | bytes 2555912 | tf_op jit(solution)/shard_map/ppermute | solution.py:414
  58.1 0.1 add_add_fusion.1.scalars
  58.2 0.1 add_add_fusion.scalars
  58.2 2.0 bags.4.refs_1_
  60.2 0.0 collective-permute-done.1.refs_1_.refs_0_
  60.2 2.0 bags.5.pooled
  62.2 3.3 %collective-permute-start.2 = (bf16[104,256]{1,0:T(8,128)(2,1)S(1)}, bf16[104,256]{1,0:T(8,128)(2,1)S(1)}, u32[]{:S(2)}, u32[]{:S(2)}) collective-permute-start(bf16[104,256]{1,0:T(8,128)(2,1)S(1)} %bags.5.pooled), channel_id=1, source_target_pairs={{0,16},{16,0},{1,17},{17,1},{2,18},{18,2},{3,19},{19,3},{4,20},{20... | collective-permute-start | bytes 159752 | tf_op jit(solution)/shard_map/ppermute | solution.py:414
  65.6 2.8 %bags.3.pooled_a.pooled = bf16[104,256]{1,0:T(8,128)(2,1)S(1)} custom-call(s32[3]{0:T(128)S(1)} %add_add_fusion.1.scalars, s32[2,2,8,64,256]{4,3,2,1,0:T(8,128)S(1)} %copy-done.7, bf16[8,104,512]{2,1,0:T(8,128)(2,1)S(1)} %all-to-all-done.1.refs_0_, bf16[8,104,512]{2,1,0:T(8,128)(2,1)S(1)} %collective-permute-done.1.refs_1_.refs_0_), custom_call_target="tpu_custom_call" | custom-call | flops 4294967296 | bytes 5242880 | tf_op jit(solution)/shard_map/bags/pallas_call | solution.py:242
  68.3 0.0 collective-permute-done.2.pooled_b
  68.4 0.0 copy-start.14
  68.4 0.9 rank_terms.1
  69.3 16.6 %all_to_all.35 = bf16[16,32,256]{2,1,0:T(8,128)(2,1)S(1)} all-to-all(bf16[16,32,256]{2,1,0:T(8,128)(2,1)S(1)} %bitcast.29), channel_id=1, replica_groups=mesh['y'=4,'x_hi'=2,'core'=2,'x_lo'=2,'z'=16] {'z'}, dimensions={0} | all-to-all | bytes 524288 | tf_op jit(solution)/shard_map/all_to_all | solution.py:406
  85.9 0.7 broadcast_in_dim.21
  86.7 11.1 %all-to-all-start.3 = ((bf16[16,32,256]{2,1,0:T(8,128)(2,1)}), bf16[16,32,256]{2,1,0:T(8,128)(2,1)S(1)}, u32[]{:S(2)}, u32[]{:S(2)}) async-start(bf16[16,32,256]{2,1,0:T(8,128)(2,1)} %broadcast_in_dim.21), calls=%async_computation.3 | async-start | bytes 524288 | tf_op jit(solution)/shard_map/all_to_all | solution.py:406
  97.8 0.0 copy-done.14
  97.8 0.1 copy.19.bias
  97.9 12.9 %all-to-all-done.3 = bf16[16,32,256]{2,1,0:T(8,128)(2,1)S(1)} async-done(((bf16[16,32,256]{2,1,0:T(8,128)(2,1)}), bf16[16,32,256]{2,1,0:T(8,128)(2,1)S(1)}, u32[]{:S(2)}, u32[]{:S(2)}) %all-to-all-start.3) | async-done | bytes 262176 | tf_op jit(solution)/shard_map/all_to_all | solution.py:406
  110.9 2.9 %collective-permute-start.3 = (bf16[512,256]{1,0:T(8,128)(2,1)S(1)}, bf16[512,256]{1,0:T(8,128)(2,1)S(1)}, u32[]{:S(2)}, u32[]{:S(2)}) collective-permute-start(bf16[512,256]{1,0:T(8,128)(2,1)S(1)} %bitcast.27), channel_id=1, source_target_pairs={{0,16},{16,0},{1,17},{17,1},{2,18},{18,2},{3,19},{19,3},{4,20},{20... | collective-permute-start | bytes 786440 | tf_op jit(solution)/shard_map/ppermute | solution.py:414
  113.8 1.6 copy-done.8
  115.3 4.1 %cross_and_row_grads.2 = (bf16[104,256]{1,0:T(8,128)(2,1)S(1)}, f32[8,112,512]{2,1,0:T(8,128)S(1)}, f32[8,112,512]{2,1,0:T(8,128)S(1)}) custom-call(s32[3]{0:T(128)S(1)} %add_add_fusion.1.scalars, s32[2,2,8,64,256]{4,3,2,1,0:T(8,128)S(1)} %copy-done.8, bf16[512,256]{1,0:T(8,128)(2,1)S(1)} %bitcast.28, bf16[104,256]{1,0:T(8,128)(2,1)S(1)} %bags.3.pooled_a.pooled, ...), custom_call_target="tpu_custom_call" | custom-call | flops 4294967296 | bytes 5242880 | tf_op jit(solution)/shard_map/cross_and_row_grads/pallas_call | solution.py:242
  119.4 0.0 collective-permute-done.3.ranks
  119.4 3.4 %cross_and_row_grads.3 = (bf16[104,512]{1,0:T(8,128)(2,1)}, bf16[2,104,256]{2,1,0:T(8,128)(2,1)S(1)}, f32[128,512]{1,0:T(8,128)S(1)}, bf16[8,112,512]{2,1,0:T(8,128)(2,1)S(1)}) custom-call(s32[3]{0:T(128)S(1)} %add_add_fusion.scalars, s32[2,1,8,64,256]{4,3,2,1,0:T(8,128)S(1)} %copy-done.11, bf16[512,256]{1,0:T(8,128)(2,1)S(1)} %collective-permute-done.3.ranks, ...), custom_call_target="tpu_custom_call" | custom-call | flops 4294967296 | bytes 5242880 | tf_op jit(solution)/shard_map/cross_and_row_grads/pallas_call | solution.py:242
  122.8 8.5 %collective-permute-start.4 = (bf16[8,112,512]{2,1,0:T(8,128)(2,1)S(1)}, bf16[8,112,512]{2,1,0:T(8,128)(2,1)S(1)}, u32[]{:S(2)}, u32[]{:S(2)}) collective-permute-start(bf16[8,112,512]{2,1,0:T(8,128)(2,1)S(1)} %get-tuple-element.45), channel_id=1, source_target_pairs={{0,32},{32,0},{1,33},{33,1},{2,34},{34,2},{3,35},{35,3},{4,36},{36... | collective-permute-start | bytes 2752520 | tf_op jit(solution)/shard_map/ppermute | solution.py:414
  131.4 2.5 %row_grads.1 = bf16[8,112,512]{2,1,0:T(8,128)(2,1)S(1)} custom-call(s32[3]{0:T(128)S(1)} %add_add_fusion.scalars, s32[2,1,8,64,256]{4,3,2,1,0:T(8,128)S(1)} %get-tuple-element.37.words, bf16[2,104,256]{2,1,0:T(8,128)(2,1)S(1)} %get-tuple-element.42.grads, f32[128,512]{1,0:T(8,128)S(1)} %get-tuple-element.43.cross_grads, ...), custom_call_target="tpu_custom_call" | custom-call | flops 4294967296 | bytes 5242880 | tf_op jit(solution)/shard_map/row_grads/pallas_call | solution.py:242
  133.9 0.0 collective-permute-done.4
  133.9 0.3 add_convert_fusion
  134.1 0.0 copy-start.2
  134.1 18.2 %all_to_all.36 = bf16[8,112,512]{2,1,0:T(8,128)(2,1)S(1)} all-to-all(bf16[8,112,512]{2,1,0:T(8,128)(2,1)S(1)} %add_convert_fusion), channel_id=1, replica_groups=mesh['y'=4,'x_hi'=2,'core'=2,'x_lo'=2,'z'=16] {'x_hi','y'}, dimensions={0} | all-to-all | bytes 1835008 | tf_op jit(solution)/shard_map/all_to_all | solution.py:406
  152.4 0.1 convert_reduce_fusion
  152.5 0.8 copy.20
  153.3 7.2 %all-to-all-start.5 = ((bf16[32,16,104]{2,1,0:T(8,128)(2,1)}), bf16[32,16,104]{2,1,0:T(8,128)(2,1)S(1)}, u32[]{:S(2)}, u32[]{:S(2)}) async-start(bf16[32,16,104]{2,1,0:T(8,128)(2,1)} %bitcast.17), calls=%async_computation.5 | async-start | bytes 262144 | tf_op jit(solution)/shard_map/all_to_all | solution.py:406
  160.5 0.0 copy-done
  160.5 0.1 constant_dynamic-slice_fusion
  160.6 0.1 broadcast_in_dim.22
  160.7 13.4 %all-to-all-done.5.grads_in = bf16[32,16,104]{2,1,0:T(8,128)(2,1)S(1)} async-done(((bf16[32,16,104]{2,1,0:T(8,128)(2,1)}), bf16[32,16,104]{2,1,0:T(8,128)(2,1)S(1)}, u32[]{:S(2)}, u32[]{:S(2)}) %all-to-all-start.5) | async-done | bytes 106528 | tf_op jit(solution)/shard_map/all_to_all | solution.py:406
  174.1 0.1 broadcast_in_dim.23.accum
  174.2 0.3 adagrad.1
  174.6 17.4 %all_to_all.37.own = bf16[8,464,128]{2,1,0:T(8,128)(2,1)S(1)} all-to-all(bf16[8,464,128]{2,1,0:T(8,128)(2,1)S(1)} %adagrad.1), channel_id=1, replica_groups=mesh['y'=4,'x_hi'=2,'core'=2,'x_lo'=2,'z'=16] {'x_hi','y'}, dimensions={0} | all-to-all | bytes 1900544 | tf_op jit(solution)/shard_map/all_to_all | solution.py:406
  192.0 6.4 %collective-permute-start.5 = (bf16[8,464,128]{2,1,0:T(8,128)(2,1)S(1)}, bf16[8,464,128]{2,1,0:T(8,128)(2,1)S(1)}, u32[]{:S(2)}, u32[]{:S(2)}) collective-permute-start(bf16[8,464,128]{2,1,0:T(8,128)(2,1)S(1)} %all_to_all.37.own), channel_id=1, source_target_pairs={{0,32},{32,0},{1,33},{33,1},{2,34},{34,2},{3,35},{35,3},{4,36},{36... | collective-permute-start | bytes 2850824 | tf_op jit(solution)/shard_map/ppermute | solution.py:414
  198.4 2.1 %collective-permute-done.5.other = bf16[8,464,128]{2,1,0:T(8,128)(2,1)S(1)} collective-permute-done((bf16[8,464,128]{2,1,0:T(8,128)(2,1)S(1)}, bf16[8,464,128]{2,1,0:T(8,128)(2,1)S(1)}, u32[]{:S(2)}, u32[]{:S(2)}) %collective-permute-start.5) | collective-permute-done | bytes 950304 | tf_op jit(solution)/shard_map/ppermute | solution.py:414
  200.6 1.5 unpack.1
  (20 shorter events, 0.1 us)
Async XLA Ops:
  0.6 159.9 %copy-start = (f32[26,256]{1,0:T(8,128)S(1)}, f32[26,256]{1,0:T(8,128)}, u32[]{:S(2)}) copy-start(f32[26,256]{1,0:T(8,128)} %param.8) | copy-start | bytes 79876
  0.6 18.8 %copy-start.5 = (bf16[512,104]{0,1:T(8,128)(2,1)S(1)}, bf16[512,104]{0,1:T(8,128)(2,1)}, u32[]{:S(2)}) copy-start(bf16[512,104]{0,1:T(8,128)(2,1)} %param.13) | copy-start | bytes 319492
  0.7 18.8 %copy-start.3 = (bf16[104,256]{1,0:T(8,128)(2,1)S(1)}, bf16[104,256]{1,0:T(8,128)(2,1)}, u32[]{:S(2)}) copy-start(bf16[104,256]{1,0:T(8,128)(2,1)} %v.3) | copy-start | bytes 159748
  0.7 18.8 %copy-start.4 = (bf16[104,256]{1,0:T(8,128)(2,1)S(1)}, bf16[104,256]{1,0:T(8,128)(2,1)}, u32[]{:S(2)}) copy-start(bf16[104,256]{1,0:T(8,128)(2,1)} %u.3) | copy-start | bytes 159748
  2.4 31.0 %all-to-all-start = ((bf16[32,16,104]{2,1,0:T(8,128)(2,1)}), bf16[32,16,104]{2,1,0:T(8,128)(2,1)S(1)}, u32[]{:S(2)}, u32[]{:S(2)}) async-start(bf16[32,16,104]{2,1,0:T(8,128)(2,1)} %get-tuple-element.29), calls=%async_computation | async-start | bytes 262144 | tf_op jit(solution)/shard_map/all_to_all | solution.py:406
  19.4 21.6 %copy-start.1 = (s32[512,26,8]{0,2,1:T(8,128)S(1)}, s32[512,26,8]{0,2,1:T(8,128)}, u32[]{:S(2)}) copy-start(s32[512,26,8]{0,2,1:T(8,128)} %param.9) | copy-start | bytes 1277956
  19.5 14.1 %collective-permute-start = (bf16[104,768]{1,0:T(8,128)(2,1)S(1)}, bf16[104,768]{1,0:T(8,128)(2,1)S(1)}, u32[]{:S(2)}, u32[]{:S(2)}) collective-permute-start(bf16[104,768]{1,0:T(8,128)(2,1)S(1)} %pad_maximum_fusion), channel_id=1, source_target_pairs={{0,16},{16,0},{1,17},{17,1},{2,18},{18,2},{3,19},{19,3},{4,20},{20... | collective-permute-start | bytes 479240 | tf_op jit(solution)/shard_map/ppermute | solution.py:414
  33.6 1.0 copy-start.12
  34.6 16.5 %all-to-all-start.1 = ((bf16[8,104,512]{2,1,0:T(8,128)(2,1)}), bf16[8,104,512]{2,1,0:T(8,128)(2,1)S(1)}, u32[]{:S(2)}, u32[]{:S(2)}) async-start(bf16[8,104,512]{2,1,0:T(8,128)(2,1)} %broadcast_in_dim.20), calls=%async_computation.1 | async-start | bytes 1703936 | tf_op jit(solution)/shard_map/all_to_all | solution.py:406
  45.7 1.3 copy-start.6
  47.1 1.0 copy-start.9
  51.1 9.2 %collective-permute-start.1 = (bf16[8,104,512]{2,1,0:T(8,128)(2,1)S(1)}, bf16[8,104,512]{2,1,0:T(8,128)(2,1)S(1)}, u32[]{:S(2)}, u32[]{:S(2)}) collective-permute-start(bf16[8,104,512]{2,1,0:T(8,128)(2,1)S(1)} %all-to-all-done.1.refs_0_), channel_id=1, source_target_pairs={{0,32},{32,0},{1,33},{33,1},{2,34},{34,2},{3,35},{35,3},{4,36},{36... | collective-permute-start | bytes 2555912 | tf_op jit(solution)/shard_map/ppermute | solution.py:414
  58.2 2.0 copy-start.10
  60.2 5.3 %copy-start.7 = (s32[2,2,8,64,256]{4,3,2,1,0:T(8,128)S(1)}, s32[2,2,8,64,256]{4,3,2,1,0:T(8,128)}, u32[]{:S(2)}) copy-start(s32[2,2,8,64,256]{4,3,2,1,0:T(8,128)} %copy-done.6) | copy-start | bytes 6291460
  62.2 6.1 %copy-start.13 = (bf16[104,768]{1,0:T(8,128)(2,1)S(1)}, bf16[104,768]{1,0:T(8,128)(2,1)}, u32[]{:S(2)}) copy-start(bf16[104,768]{1,0:T(8,128)(2,1)} %copy-done.12) | copy-start | bytes 479236
  62.2 6.1 %collective-permute-start.2 = (bf16[104,256]{1,0:T(8,128)(2,1)S(1)}, bf16[104,256]{1,0:T(8,128)(2,1)S(1)}, u32[]{:S(2)}, u32[]{:S(2)}) collective-permute-start(bf16[104,256]{1,0:T(8,128)(2,1)S(1)} %bags.5.pooled), channel_id=1, source_target_pairs={{0,16},{16,0},{1,17},{17,1},{2,18},{18,2},{3,19},{19,3},{4,20},{20... | collective-permute-start | bytes 159752 | tf_op jit(solution)/shard_map/ppermute | solution.py:414
  68.4 29.4 %copy-start.14 = (f32[104]{0:T(128)S(1)}, f32[104]{0:T(128)}, u32[]{:S(2)}) copy-start(f32[104]{0:T(128)} %param.12) | copy-start | bytes 1252
  86.7 24.2 %all-to-all-start.3 = ((bf16[16,32,256]{2,1,0:T(8,128)(2,1)}), bf16[16,32,256]{2,1,0:T(8,128)(2,1)S(1)}, u32[]{:S(2)}, u32[]{:S(2)}) async-start(bf16[16,32,256]{2,1,0:T(8,128)(2,1)} %broadcast_in_dim.21), calls=%async_computation.3 | async-start | bytes 524288 | tf_op jit(solution)/shard_map/all_to_all | solution.py:406
  110.9 8.6 %collective-permute-start.3 = (bf16[512,256]{1,0:T(8,128)(2,1)S(1)}, bf16[512,256]{1,0:T(8,128)(2,1)S(1)}, u32[]{:S(2)}, u32[]{:S(2)}) collective-permute-start(bf16[512,256]{1,0:T(8,128)(2,1)S(1)} %bitcast.27), channel_id=1, source_target_pairs={{0,16},{16,0},{1,17},{17,1},{2,18},{18,2},{3,19},{19,3},{4,20},{20... | collective-permute-start | bytes 786440 | tf_op jit(solution)/shard_map/ppermute | solution.py:414
  113.7 1.6 copy-start.8
  115.3 4.1 %copy-start.11 = (s32[2,1,8,64,256]{4,3,2,1,0:T(8,128)S(1)}, s32[2,1,8,64,256]{4,3,2,1,0:T(8,128)}, u32[]{:S(2)}) copy-start(s32[2,1,8,64,256]{4,3,2,1,0:T(8,128)} %copy-done.9) | copy-start | bytes 3145732
  122.8 11.0 %collective-permute-start.4 = (bf16[8,112,512]{2,1,0:T(8,128)(2,1)S(1)}, bf16[8,112,512]{2,1,0:T(8,128)(2,1)S(1)}, u32[]{:S(2)}, u32[]{:S(2)}) collective-permute-start(bf16[8,112,512]{2,1,0:T(8,128)(2,1)S(1)} %get-tuple-element.45), channel_id=1, source_target_pairs={{0,32},{32,0},{1,33},{33,1},{2,34},{34,2},{3,35},{35,3},{4,36},{36... | collective-permute-start | bytes 2752520 | tf_op jit(solution)/shard_map/ppermute | solution.py:414
  134.1 40.1 %copy-start.2 = (bf16[26,16,128]{2,1,0:T(8,128)(2,1)S(1)}, bf16[26,16,128]{2,1,0:T(8,128)(2,1)}, u32[]{:S(2)}) copy-start(bf16[26,16,128]{2,1,0:T(8,128)(2,1)} %get-tuple-element.46) | copy-start | bytes 319492
  153.3 20.8 %all-to-all-start.5 = ((bf16[32,16,104]{2,1,0:T(8,128)(2,1)}), bf16[32,16,104]{2,1,0:T(8,128)(2,1)S(1)}, u32[]{:S(2)}, u32[]{:S(2)}) async-start(bf16[32,16,104]{2,1,0:T(8,128)(2,1)} %bitcast.17), calls=%async_computation.5 | async-start | bytes 262144 | tf_op jit(solution)/shard_map/all_to_all | solution.py:406
  192.0 8.6 %collective-permute-start.5 = (bf16[8,464,128]{2,1,0:T(8,128)(2,1)S(1)}, bf16[8,464,128]{2,1,0:T(8,128)(2,1)S(1)}, u32[]{:S(2)}, u32[]{:S(2)}) collective-permute-start(bf16[8,464,128]{2,1,0:T(8,128)(2,1)S(1)} %all_to_all.37.own), channel_id=1, source_target_pairs={{0,32},{32,0},{1,33},{33,1},{2,34},{34,2},{3,35},{35,3},{4,36},{36... | collective-permute-start | bytes 2850824 | tf_op jit(solution)/shard_map/ppermute | solution.py:414

commit v6 on v5

--- a/solution.py
+++ b/solution.py
@@ -25,7 +25,7 @@
 ROW_ALL = ("x_lo", "z")
 BLOCK_OF = [(i & 1) * 16 + (i >> 1) for i in range(N_ROW)]
 CHUNK = TABLES * PART + 16 + 32
-UNROLL = 2
+UNROLL = 8
 VMEM = 16 << 20
 
 NT_DIMS = (((1,), (1,)), ((), ()))
@@ -306,6 +306,44 @@
     return call(ranks_kernel, "rank_terms", scalars, operands, jax.ShapeDtypeStruct((2 * RANK, HALF), bf16))
 
 
+def sum_and_copy_kernel(terms, out):
+    total = terms[0].astype(f32)
+    for i in range(1, terms.shape[0]):
+        total = total + terms[i].astype(f32)
+    total = total.astype(bf16)
+    for i in range(out.shape[0]):
+        out[i] = total
+
+
+def sum_and_copy(terms):
+    return pl.pallas_call(
+        sum_and_copy_kernel,
+        out_shape=jax.ShapeDtypeStruct(terms.shape, bf16),
+        compiler_params=pltpu.CompilerParams(vmem_limit_bytes=VMEM),
+        name="sum_and_copy",
+    )(terms)
+
+
+def sum_and_turn_kernel(terms, grads, cross_grads):
+    total = terms[0].astype(f32)
+    for i in range(1, 8):
+        total = total + terms[i].astype(f32)
+    grads[...] = total[:FEATS].T.astype(bf16)
+    cross_grads[...] = total[FEATS:]
+
+
+def sum_and_turn(terms):
+    return pl.pallas_call(
+        sum_and_turn_kernel,
+        out_shape=[
+            jax.ShapeDtypeStruct((STEP_ROWS, FEATS), bf16),
+            jax.ShapeDtypeStruct((GRAD_ROWS, 2 * RANK), f32),
+        ],
+        compiler_params=pltpu.CompilerParams(vmem_limit_bytes=VMEM),
+        name="sum_and_turn",
+    )(terms)
+
+
 def cross_layer(scalars, ranks, pooled_in, v, u, bias, upstream_in, grads, cross_grads):
     rank = ranks[:RANK]
     rank_grad = ranks[RANK:]
@@ -406,10 +444,6 @@
     return lax.all_to_all(x, axes, 0, 0, tiled=True)
 
 
-def spread(x, axes, count):
-    return exchange(jnp.broadcast_to(x, (count,) + x.shape), axes)
-
-
 def swap(x, axis):
     return lax.ppermute(x, axis, [(0, 1), (1, 0)])
 
@@ -435,12 +469,14 @@
     nibble = (jnp.arange(STEP_ROWS) >> 3) & 7
     mine = mine * jnp.where(nibble == 7, 1.0, jnp.exp2(-4.0 * nibble)).astype(bf16)
     mine, partner = lax.optimization_barrier((mine, partner))
-    own = spread(mine, DP_OUTER, 8)
+    own = exchange(jnp.broadcast_to(mine, (8, FEATS, STEP_ROWS)), DP_OUTER)
+
     keep = lax.axis_index("x_lo")
     scalars = jnp.stack([table_a, table_b, core, keep]).astype(jnp.int32)
     at_keep = jnp.stack([keep, n_a, core]).astype(jnp.int32)
     at_sent = jnp.stack([1 - keep, n_a, core]).astype(jnp.int32)
-    words = bag_words(scalars, bag_ids.transpose(1, 2, 0))
+    ids = bag_ids.transpose(1, 2, 0)
+    words = bag_words(scalars, ids)
     own, kept_words, own_words, other_words = lax.optimization_barrier((own, *words))
     other = to_other_core(own)
 
@@ -450,8 +486,8 @@
     kept_pooled = forward(at_keep, kept_words, [own, other])
 
     terms = rank_terms(at_keep, kept_pooled, partner_pooled, cross_v, cross_u, upstream_t, partner)
-    gathered = exchange(terms.reshape(16, 32, HALF), "z")
-    ranks = spread(jnp.sum(gathered.astype(f32), axis=0).astype(bf16), "z", 16).reshape(2 * RANK, HALF)
+    chunks = sum_and_copy(exchange(terms.reshape(16, 32, HALF), "z"))
+    ranks = exchange(chunks, "z").reshape(2 * RANK, HALF)
     sent_ranks = swap(ranks, "x_lo")
 
     cross = (cross_v, cross_u, cross_bias.reshape(FEATS, 1), upstream_t)
@@ -463,13 +499,13 @@
     own = rest_of_backward(at_sent, own_words, grads, cross_grads, own)
 
     chip_sum = (own.astype(f32) + from_other.astype(f32)).astype(bf16)
-    sums = jnp.sum(exchange(chip_sum, DP_OUTER).astype(f32), axis=0)
-    row_grad = exchange(sums[:FEATS].astype(bf16).T.reshape(N_ROW, PART, FEATS), ROW_AXES)
+    row_grad, cross_sums = sum_and_turn(exchange(chip_sum, DP_OUTER))
+    row_grad = exchange(row_grad.reshape(N_ROW, PART, FEATS), ROW_AXES)
     my_accum = lax.dynamic_slice(accum, (0, part * PART), (TABLES, PART))
     my_accum = jnp.broadcast_to(my_accum[:, :, None], (TABLES, PART, WIDTH)).reshape(TABLES * PART, WIDTH)
 
     own = exchange(
-        adagrad(row_grad, my_rows.reshape(TABLES * PART, WIDTH), my_accum, sums[FEATS:]), DP_OUTER
+        adagrad(row_grad, my_rows.reshape(TABLES * PART, WIDTH), my_accum, cross_sums), DP_OUTER
     )
     new_rows, new_accum, grad_v, grad_u, grad_bias = unpack(
         jnp.stack([core]).astype(jnp.int32), own, to_other_core(own)

time: 203 us -> 200 us (0.985)
    pallas_call x8, Pallas kernels: 19.1 us -> 16 us  [call(): pl.pallas_call(kernel, in_specs=[pl.BlockSpec(memory_space=pltpu.SMEM)] +...]
  transfers between devices with their start and end apart: 10 -> 10, of which waited for: 5 -> 6; matrix products, arithmetic and copies ran while one was open for 0% -> 0% of each run, Pallas kernels for 8% -> 7%
where the time goes in v6:
time: 200 us; the launch traced here: 199 us
  starting transfers between devices  73.5 us (37%)
  blocking collectives  51.4 us (26%)
  waiting for transfers between devices  42.5 us (21%)
  Pallas kernels  24.4 us (12%)
  local copies, waits for them, and re-layouts  5.43 us (3%)
    all_to_all x3, blocking collectives, exchange(): return lax.all_to_all(x, axes, 0, 0, tiled=True)  51.4 us
    all_to_all x4, starting transfers between devices, exchange(): return lax.all_to_all(x, axes, 0, 0, tiled=True)  41.2 us
    all_to_all x4, waiting for transfers between devices, exchange(): return lax.all_to_all(x, axes, 0, 0, tiled=True)  40 us
    ppermute x6, starting transfers between devices, swap(): return lax.ppermute(x, axis, [(0, 1), (1, 0)])  32.3 us
    pallas_call x8, Pallas kernels, call(): pl.pallas_call(kernel, in_specs=[pl.BlockSpec(memory_space=pltpu.SMEM)] +...  16 us
    pallas_call x1, Pallas kernels, bag_words(): pl.pallas_call(words_kernel, grid_spec=pltpu.PrefetchScalarGridSpec(num_s...  4.7 us
  transfers between devices with their start and end apart: 10, of which 6 were waited for; matrix products, arithmetic and copies ran while one was open for 0% of the time, Pallas kernels for 7%

profile of v6, /device:TPU:1, one launch (start us, length us, event | category | flops | bytes accessed | tf_op | source)
XLA Modules:
  0.0 198.8 jit_solution(2517121285637398283)
XLA Ops:
  0.6 0.0 copy-start
  0.6 0.0 copy-start.5
  0.7 0.0 copy-start.3
  0.7 0.0 copy-start.4
  0.7 1.7 pack_rows.1
  2.4 17.0 %all-to-all-start = ((bf16[32,16,104]{2,1,0:T(8,128)(2,1)}), bf16[32,16,104]{2,1,0:T(8,128)(2,1)S(1)}, u32[]{:S(2)}, u32[]{:S(2)}) async-start(bf16[32,16,104]{2,1,0:T(8,128)(2,1)} %get-tuple-element.31), calls=%async_computation | async-start | bytes 262144 | tf_op jit(solution)/shard_map/all_to_all | solution.py:444
  19.4 0.0 copy-start.1
  19.4 0.0 copy-done.5
  19.5 0.0 copy-done.3
  19.5 0.0 copy-done.4
  19.5 3.3 %collective-permute-start = (bf16[104,768]{1,0:T(8,128)(2,1)S(1)}, bf16[104,768]{1,0:T(8,128)(2,1)S(1)}, u32[]{:S(2)}, u32[]{:S(2)}) collective-permute-start(bf16[104,768]{1,0:T(8,128)(2,1)S(1)} %pad_maximum_fusion), channel_id=1, source_target_pairs={{0,16},{16,0},{1,17},{17,1},{2,18},{18,2},{3,19},{19,3},{4,20},{20... | collective-permute-start | bytes 479240 | tf_op jit(solution)/shard_map/ppermute | solution.py:448
  22.8 10.7 %all-to-all-done = bf16[32,16,104]{2,1,0:T(8,128)(2,1)S(1)} async-done(((bf16[32,16,104]{2,1,0:T(8,128)(2,1)}), bf16[32,16,104]{2,1,0:T(8,128)(2,1)S(1)}, u32[]{:S(2)}, u32[]{:S(2)}) %all-to-all-start) | async-done | bytes 106528 | tf_op jit(solution)/shard_map/all_to_all | solution.py:444
  33.4 0.1 copy.16
  33.6 0.0 collective-permute-done.partner
  33.6 0.0 copy-start.12
  33.6 1.0 broadcast_in_dim.17
  34.6 0.0 copy-done.12
  34.6 6.4 %all-to-all-start.1 = ((bf16[8,104,512]{2,1,0:T(8,128)(2,1)}), bf16[8,104,512]{2,1,0:T(8,128)(2,1)S(1)}, u32[]{:S(2)}, u32[]{:S(2)}) async-start(bf16[8,104,512]{2,1,0:T(8,128)(2,1)} %broadcast_in_dim.17), calls=%async_computation.1 | async-start | bytes 1703936 | tf_op jit(solution)/shard_map/all_to_all | solution.py:444
  40.9 0.1 pad_add_fusion.scalars
  41.0 0.0 copy-done.1
  41.0 4.7 %bag_words.1 = (s32[2,2,8,64,256]{4,3,2,1,0:T(8,128)S(1)}, s32[2,1,8,64,256]{4,3,2,1,0:T(8,128)S(1)}, s32[2,1,8,64,256]{4,3,2,1,0:T(8,128)S(1)}) custom-call(s32[4]{0:T(128)S(1)} %pad_add_fusion.scalars, s32[26,8,512]{2,1,0:T(8,128)S(1)} %bitcast.21, s32[26,8,512]{2,1,0:T(8,128)S(1)} %bitcast.22, s32[26,8,512]{2,1,0:T(8,128)S(1)} %bitcast.23, ...), custom_call_target="tpu_custom_call" | custom-call | flops 268435456 | bytes 5242880 | tf_op jit(solution)/shard_map/bag_words/pallas_call | solution.py:217
  45.7 1.3 copy-done.6
  47.1 1.0 copy-done.9
  48.1 3.0 %all-to-all-done.1.refs_0_ = bf16[8,104,512]{2,1,0:T(8,128)(2,1)S(1)} async-done(((bf16[8,104,512]{2,1,0:T(8,128)(2,1)}), bf16[8,104,512]{2,1,0:T(8,128)(2,1)S(1)}, u32[]{:S(2)}, u32[]{:S(2)}) %all-to-all-start.1) | async-done | bytes 852000 | tf_op jit(solution)/shard_map/all_to_all | solution.py:444
  51.1 7.0 %collective-permute-start.1 = (bf16[8,104,512]{2,1,0:T(8,128)(2,1)S(1)}, bf16[8,104,512]{2,1,0:T(8,128)(2,1)S(1)}, u32[]{:S(2)}, u32[]{:S(2)}) collective-permute-start(bf16[8,104,512]{2,1,0:T(8,128)(2,1)S(1)} %all-to-all-done.1.refs_0_), channel_id=1, source_target_pairs={{0,32},{32,0},{1,33},{33,1},{2,34},{34,2},{3,35},{35,3},{4,36},{36... | collective-permute-start | bytes 2555912 | tf_op jit(solution)/shard_map/ppermute | solution.py:448
  58.1 0.1 add_add_fusion.1.scalars
  58.2 0.1 add_add_fusion.scalars
  58.3 1.5 bags.4.refs_1_
  59.8 0.3 collective-permute-done.1.refs_1_.refs_0_
  60.1 0.0 copy-done.10
  60.1 1.5 bags.5.pooled
  61.6 3.3 %collective-permute-start.2 = (bf16[104,256]{1,0:T(8,128)(2,1)S(1)}, bf16[104,256]{1,0:T(8,128)(2,1)S(1)}, u32[]{:S(2)}, u32[]{:S(2)}) collective-permute-start(bf16[104,256]{1,0:T(8,128)(2,1)S(1)} %bags.5.pooled), channel_id=1, source_target_pairs={{0,16},{16,0},{1,17},{17,1},{2,18},{18,2},{3,19},{19,3},{4,20},{20... | collective-permute-start | bytes 159752 | tf_op jit(solution)/shard_map/ppermute | solution.py:448
  64.9 2.3 %bags.3.pooled_a.pooled = bf16[104,256]{1,0:T(8,128)(2,1)S(1)} custom-call(s32[3]{0:T(128)S(1)} %add_add_fusion.1.scalars, s32[2,2,8,64,256]{4,3,2,1,0:T(8,128)S(1)} %copy-done.7, bf16[8,104,512]{2,1,0:T(8,128)(2,1)S(1)} %all-to-all-done.1.refs_0_, bf16[8,104,512]{2,1,0:T(8,128)(2,1)S(1)} %collective-permute-done.1.refs_1_.refs_0_), custom_call_target="tpu_custom_call" | custom-call | flops 4294967296 | bytes 5242880 | tf_op jit(solution)/shard_map/bags/pallas_call | solution.py:242
  67.2 0.0 collective-permute-done.2.pooled_b
  67.2 0.0 copy-start.14
  67.2 0.9 rank_terms.1
  68.1 16.6 %all_to_all.35.terms = bf16[16,32,256]{2,1,0:T(8,128)(2,1)S(1)} all-to-all(bf16[16,32,256]{2,1,0:T(8,128)(2,1)S(1)} %bitcast.27), channel_id=1, replica_groups=mesh['y'=4,'x_hi'=2,'core'=2,'x_lo'=2,'z'=16] {'z'}, dimensions={0} | all-to-all | bytes 524288 | tf_op jit(solution)/shard_map/all_to_all | solution.py:444
  84.7 0.8 sum_and_copy.1
  85.5 10.6 %all-to-all-start.3 = ((bf16[16,32,256]{2,1,0:T(8,128)(2,1)}), bf16[16,32,256]{2,1,0:T(8,128)(2,1)S(1)}, u32[]{:S(2)}, u32[]{:S(2)}) async-start(bf16[16,32,256]{2,1,0:T(8,128)(2,1)} %sum_and_copy.1), calls=%async_computation.3 | async-start | bytes 524288 | tf_op jit(solution)/shard_map/all_to_all | solution.py:444
  96.1 0.1 copy.18.bias
  96.2 12.7 %all-to-all-done.3 = bf16[16,32,256]{2,1,0:T(8,128)(2,1)S(1)} async-done(((bf16[16,32,256]{2,1,0:T(8,128)(2,1)}), bf16[16,32,256]{2,1,0:T(8,128)(2,1)S(1)}, u32[]{:S(2)}, u32[]{:S(2)}) %all-to-all-start.3) | async-done | bytes 262176 | tf_op jit(solution)/shard_map/all_to_all | solution.py:444
  108.9 3.7 %collective-permute-start.3 = (bf16[512,256]{1,0:T(8,128)(2,1)S(1)}, bf16[512,256]{1,0:T(8,128)(2,1)S(1)}, u32[]{:S(2)}, u32[]{:S(2)}) collective-permute-start(bf16[512,256]{1,0:T(8,128)(2,1)S(1)} %bitcast.25), channel_id=1, source_target_pairs={{0,16},{16,0},{1,17},{17,1},{2,18},{18,2},{3,19},{19,3},{4,20},{20... | collective-permute-start | bytes 786440 | tf_op jit(solution)/shard_map/ppermute | solution.py:448
  112.6 1.6 copy-done.8
  114.2 3.5 %cross_and_row_grads.2 = (bf16[104,256]{1,0:T(8,128)(2,1)S(1)}, f32[8,112,512]{2,1,0:T(8,128)S(1)}, f32[8,112,512]{2,1,0:T(8,128)S(1)}) custom-call(s32[3]{0:T(128)S(1)} %add_add_fusion.1.scalars, s32[2,2,8,64,256]{4,3,2,1,0:T(8,128)S(1)} %copy-done.8, bf16[512,256]{1,0:T(8,128)(2,1)S(1)} %bitcast.26, bf16[104,256]{1,0:T(8,128)(2,1)S(1)} %bags.3.pooled_a.pooled, ...), custom_call_target="tpu_custom_call" | custom-call | flops 4294967296 | bytes 5242880 | tf_op jit(solution)/shard_map/cross_and_row_grads/pallas_call | solution.py:242
  117.7 0.0 collective-permute-done.3.ranks
  117.7 0.0 copy-done.11
  117.7 2.7 %cross_and_row_grads.3 = (bf16[104,512]{1,0:T(8,128)(2,1)}, bf16[2,104,256]{2,1,0:T(8,128)(2,1)S(1)}, f32[128,512]{1,0:T(8,128)S(1)}, bf16[8,112,512]{2,1,0:T(8,128)(2,1)S(1)}) custom-call(s32[3]{0:T(128)S(1)} %add_add_fusion.scalars, s32[2,1,8,64,256]{4,3,2,1,0:T(8,128)S(1)} %copy-done.11, bf16[512,256]{1,0:T(8,128)(2,1)S(1)} %collective-permute-done.3.ranks, ...), custom_call_target="tpu_custom_call" | custom-call | flops 4294967296 | bytes 5242880 | tf_op jit(solution)/shard_map/cross_and_row_grads/pallas_call | solution.py:242
  120.5 8.5 %collective-permute-start.4 = (bf16[8,112,512]{2,1,0:T(8,128)(2,1)S(1)}, bf16[8,112,512]{2,1,0:T(8,128)(2,1)S(1)}, u32[]{:S(2)}, u32[]{:S(2)}) collective-permute-start(bf16[8,112,512]{2,1,0:T(8,128)(2,1)S(1)} %get-tuple-element.47), channel_id=1, source_target_pairs={{0,32},{32,0},{1,33},{33,1},{2,34},{34,2},{3,35},{35,3},{4,36},{36... | collective-permute-start | bytes 2752520 | tf_op jit(solution)/shard_map/ppermute | solution.py:448
  129.0 2.0 %row_grads.1 = bf16[8,112,512]{2,1,0:T(8,128)(2,1)S(1)} custom-call(s32[3]{0:T(128)S(1)} %add_add_fusion.scalars, s32[2,1,8,64,256]{4,3,2,1,0:T(8,128)S(1)} %get-tuple-element.39.words, bf16[2,104,256]{2,1,0:T(8,128)(2,1)S(1)} %get-tuple-element.44.grads, f32[128,512]{1,0:T(8,128)S(1)} %get-tuple-element.45.cross_grads, ...), custom_call_target="tpu_custom_call" | custom-call | flops 4294967296 | bytes 5242880 | tf_op jit(solution)/shard_map/row_grads/pallas_call | solution.py:242
  131.1 0.0 collective-permute-done.4
  131.1 0.2 add_convert_fusion
  131.3 0.0 copy-start.2
  131.3 18.5 %all_to_all.36.terms = bf16[8,112,512]{2,1,0:T(8,128)(2,1)S(1)} all-to-all(bf16[8,112,512]{2,1,0:T(8,128)(2,1)S(1)} %add_convert_fusion), channel_id=1, replica_groups=mesh['y'=4,'x_hi'=2,'core'=2,'x_lo'=2,'z'=16] {'x_hi','y'}, dimensions={0} | all-to-all | bytes 1835008 | tf_op jit(solution)/shard_map/all_to_all | solution.py:444
  149.9 0.8 sum_and_turn.1
  150.7 7.3 %all-to-all-start.5 = ((bf16[32,16,104]{2,1,0:T(8,128)(2,1)}), bf16[32,16,104]{2,1,0:T(8,128)(2,1)S(1)}, u32[]{:S(2)}, u32[]{:S(2)}) async-start(bf16[32,16,104]{2,1,0:T(8,128)(2,1)} %bitcast.16), calls=%async_computation.5 | async-start | bytes 262144 | tf_op jit(solution)/shard_map/all_to_all | solution.py:444
  158.0 0.1 constant_dynamic-slice_fusion
  158.1 0.1 broadcast_in_dim.18
  158.2 13.6 %all-to-all-done.5.grads_in = bf16[32,16,104]{2,1,0:T(8,128)(2,1)S(1)} async-done(((bf16[32,16,104]{2,1,0:T(8,128)(2,1)}), bf16[32,16,104]{2,1,0:T(8,128)(2,1)S(1)}, u32[]{:S(2)}, u32[]{:S(2)}) %all-to-all-start.5) | async-done | bytes 106528 | tf_op jit(solution)/shard_map/all_to_all | solution.py:444
  171.8 0.1 broadcast_in_dim.19.accum
  172.0 0.3 adagrad.1
  172.3 16.3 %all_to_all.37.own = bf16[8,464,128]{2,1,0:T(8,128)(2,1)S(1)} all-to-all(bf16[8,464,128]{2,1,0:T(8,128)(2,1)S(1)} %adagrad.1), channel_id=1, replica_groups=mesh['y'=4,'x_hi'=2,'core'=2,'x_lo'=2,'z'=16] {'x_hi','y'}, dimensions={0} | all-to-all | bytes 1900544 | tf_op jit(solution)/shard_map/all_to_all | solution.py:444
  188.6 6.6 %collective-permute-start.5 = (bf16[8,464,128]{2,1,0:T(8,128)(2,1)S(1)}, bf16[8,464,128]{2,1,0:T(8,128)(2,1)S(1)}, u32[]{:S(2)}, u32[]{:S(2)}) collective-permute-start(bf16[8,464,128]{2,1,0:T(8,128)(2,1)S(1)} %all_to_all.37.own), channel_id=1, source_target_pairs={{0,32},{32,0},{1,33},{33,1},{2,34},{34,2},{3,35},{35,3},{4,36},{36... | collective-permute-start | bytes 2850824 | tf_op jit(solution)/shard_map/ppermute | solution.py:448
  195.1 2.1 %collective-permute-done.5.other = bf16[8,464,128]{2,1,0:T(8,128)(2,1)S(1)} collective-permute-done((bf16[8,464,128]{2,1,0:T(8,128)(2,1)S(1)}, bf16[8,464,128]{2,1,0:T(8,128)(2,1)S(1)}, u32[]{:S(2)}, u32[]{:S(2)}) %collective-permute-start.5) | collective-permute-done | bytes 950304 | tf_op jit(solution)/shard_map/ppermute | solution.py:448
  197.3 1.5 unpack.1
  (16 shorter events, 0.1 us)
Async XLA Ops:
  0.6 157.4 %copy-start = (f32[26,256]{1,0:T(8,128)S(1)}, f32[26,256]{1,0:T(8,128)}, u32[]{:S(2)}) copy-start(f32[26,256]{1,0:T(8,128)} %param.8) | copy-start | bytes 79876
  0.6 18.8 %copy-start.5 = (bf16[512,104]{0,1:T(8,128)(2,1)S(1)}, bf16[512,104]{0,1:T(8,128)(2,1)}, u32[]{:S(2)}) copy-start(bf16[512,104]{0,1:T(8,128)(2,1)} %param.13) | copy-start | bytes 319492
  0.7 18.8 %copy-start.3 = (bf16[104,256]{1,0:T(8,128)(2,1)S(1)}, bf16[104,256]{1,0:T(8,128)(2,1)}, u32[]{:S(2)}) copy-start(bf16[104,256]{1,0:T(8,128)(2,1)} %v.3) | copy-start | bytes 159748
  0.7 18.8 %copy-start.4 = (bf16[104,256]{1,0:T(8,128)(2,1)S(1)}, bf16[104,256]{1,0:T(8,128)(2,1)}, u32[]{:S(2)}) copy-start(bf16[104,256]{1,0:T(8,128)(2,1)} %u.3) | copy-start | bytes 159748
  2.4 31.0 %all-to-all-start = ((bf16[32,16,104]{2,1,0:T(8,128)(2,1)}), bf16[32,16,104]{2,1,0:T(8,128)(2,1)S(1)}, u32[]{:S(2)}, u32[]{:S(2)}) async-start(bf16[32,16,104]{2,1,0:T(8,128)(2,1)} %get-tuple-element.31), calls=%async_computation | async-start | bytes 262144 | tf_op jit(solution)/shard_map/all_to_all | solution.py:444
  19.4 21.6 %copy-start.1 = (s32[512,26,8]{0,2,1:T(8,128)S(1)}, s32[512,26,8]{0,2,1:T(8,128)}, u32[]{:S(2)}) copy-start(s32[512,26,8]{0,2,1:T(8,128)} %param.9) | copy-start | bytes 1277956
  19.5 14.1 %collective-permute-start = (bf16[104,768]{1,0:T(8,128)(2,1)S(1)}, bf16[104,768]{1,0:T(8,128)(2,1)S(1)}, u32[]{:S(2)}, u32[]{:S(2)}) collective-permute-start(bf16[104,768]{1,0:T(8,128)(2,1)S(1)} %pad_maximum_fusion), channel_id=1, source_target_pairs={{0,16},{16,0},{1,17},{17,1},{2,18},{18,2},{3,19},{19,3},{4,20},{20... | collective-permute-start | bytes 479240 | tf_op jit(solution)/shard_map/ppermute | solution.py:448
  33.6 1.0 copy-start.12
  34.6 16.5 %all-to-all-start.1 = ((bf16[8,104,512]{2,1,0:T(8,128)(2,1)}), bf16[8,104,512]{2,1,0:T(8,128)(2,1)S(1)}, u32[]{:S(2)}, u32[]{:S(2)}) async-start(bf16[8,104,512]{2,1,0:T(8,128)(2,1)} %broadcast_in_dim.17), calls=%async_computation.1 | async-start | bytes 1703936 | tf_op jit(solution)/shard_map/all_to_all | solution.py:444
  45.7 1.4 copy-start.6
  47.1 1.0 copy-start.9
  51.1 9.0 %collective-permute-start.1 = (bf16[8,104,512]{2,1,0:T(8,128)(2,1)S(1)}, bf16[8,104,512]{2,1,0:T(8,128)(2,1)S(1)}, u32[]{:S(2)}, u32[]{:S(2)}) collective-permute-start(bf16[8,104,512]{2,1,0:T(8,128)(2,1)S(1)} %all-to-all-done.1.refs_0_), channel_id=1, source_target_pairs={{0,32},{32,0},{1,33},{33,1},{2,34},{34,2},{3,35},{35,3},{4,36},{36... | collective-permute-start | bytes 2555912 | tf_op jit(solution)/shard_map/ppermute | solution.py:448
  58.3 1.8 copy-start.10
  59.8 5.1 %copy-start.7 = (s32[2,2,8,64,256]{4,3,2,1,0:T(8,128)S(1)}, s32[2,2,8,64,256]{4,3,2,1,0:T(8,128)}, u32[]{:S(2)}) copy-start(s32[2,2,8,64,256]{4,3,2,1,0:T(8,128)} %copy-done.6) | copy-start | bytes 6291460
  61.6 5.6 %copy-start.13 = (bf16[104,768]{1,0:T(8,128)(2,1)S(1)}, bf16[104,768]{1,0:T(8,128)(2,1)}, u32[]{:S(2)}) copy-start(bf16[104,768]{1,0:T(8,128)(2,1)} %copy-done.12) | copy-start | bytes 479236
  61.6 5.6 %collective-permute-start.2 = (bf16[104,256]{1,0:T(8,128)(2,1)S(1)}, bf16[104,256]{1,0:T(8,128)(2,1)S(1)}, u32[]{:S(2)}, u32[]{:S(2)}) collective-permute-start(bf16[104,256]{1,0:T(8,128)(2,1)S(1)} %bags.5.pooled), channel_id=1, source_target_pairs={{0,16},{16,0},{1,17},{17,1},{2,18},{18,2},{3,19},{19,3},{4,20},{20... | collective-permute-start | bytes 159752 | tf_op jit(solution)/shard_map/ppermute | solution.py:448
  67.2 28.9 %copy-start.14 = (f32[104]{0:T(128)S(1)}, f32[104]{0:T(128)}, u32[]{:S(2)}) copy-start(f32[104]{0:T(128)} %param.12) | copy-start | bytes 1252
  85.5 23.4 %all-to-all-start.3 = ((bf16[16,32,256]{2,1,0:T(8,128)(2,1)}), bf16[16,32,256]{2,1,0:T(8,128)(2,1)S(1)}, u32[]{:S(2)}, u32[]{:S(2)}) async-start(bf16[16,32,256]{2,1,0:T(8,128)(2,1)} %sum_and_copy.1), calls=%async_computation.3 | async-start | bytes 524288 | tf_op jit(solution)/shard_map/all_to_all | solution.py:444
  108.9 8.8 %collective-permute-start.3 = (bf16[512,256]{1,0:T(8,128)(2,1)S(1)}, bf16[512,256]{1,0:T(8,128)(2,1)S(1)}, u32[]{:S(2)}, u32[]{:S(2)}) collective-permute-start(bf16[512,256]{1,0:T(8,128)(2,1)S(1)} %bitcast.25), channel_id=1, source_target_pairs={{0,16},{16,0},{1,17},{17,1},{2,18},{18,2},{3,19},{19,3},{4,20},{20... | collective-permute-start | bytes 786440 | tf_op jit(solution)/shard_map/ppermute | solution.py:448
  112.6 1.6 copy-start.8
  114.2 3.6 %copy-start.11 = (s32[2,1,8,64,256]{4,3,2,1,0:T(8,128)S(1)}, s32[2,1,8,64,256]{4,3,2,1,0:T(8,128)}, u32[]{:S(2)}) copy-start(s32[2,1,8,64,256]{4,3,2,1,0:T(8,128)} %copy-done.9) | copy-start | bytes 3145732
  120.5 10.6 %collective-permute-start.4 = (bf16[8,112,512]{2,1,0:T(8,128)(2,1)S(1)}, bf16[8,112,512]{2,1,0:T(8,128)(2,1)S(1)}, u32[]{:S(2)}, u32[]{:S(2)}) collective-permute-start(bf16[8,112,512]{2,1,0:T(8,128)(2,1)S(1)} %get-tuple-element.47), channel_id=1, source_target_pairs={{0,32},{32,0},{1,33},{33,1},{2,34},{34,2},{3,35},{35,3},{4,36},{36... | collective-permute-start | bytes 2752520 | tf_op jit(solution)/shard_map/ppermute | solution.py:448
  131.3 40.6 %copy-start.2 = (bf16[26,16,128]{2,1,0:T(8,128)(2,1)S(1)}, bf16[26,16,128]{2,1,0:T(8,128)(2,1)}, u32[]{:S(2)}) copy-start(bf16[26,16,128]{2,1,0:T(8,128)(2,1)} %get-tuple-element.49) | copy-start | bytes 319492
  150.7 21.1 %all-to-all-start.5 = ((bf16[32,16,104]{2,1,0:T(8,128)(2,1)}), bf16[32,16,104]{2,1,0:T(8,128)(2,1)S(1)}, u32[]{:S(2)}, u32[]{:S(2)}) async-start(bf16[32,16,104]{2,1,0:T(8,128)(2,1)} %bitcast.16), calls=%async_computation.5 | async-start | bytes 262144 | tf_op jit(solution)/shard_map/all_to_all | solution.py:444
  188.6 8.7 %collective-permute-start.5 = (bf16[8,464,128]{2,1,0:T(8,128)(2,1)S(1)}, bf16[8,464,128]{2,1,0:T(8,128)(2,1)S(1)}, u32[]{:S(2)}, u32[]{:S(2)}) collective-permute-start(bf16[8,464,128]{2,1,0:T(8,128)(2,1)S(1)} %all_to_all.37.own), channel_id=1, source_target_pairs={{0,32},{32,0},{1,33},{33,1},{2,34},{34,2},{3,35},{35,3},{4,36},{36... | collective-permute-start | bytes 2850824 | tf_op jit(solution)/shard_map/ppermute | solution.py:448

commit v7 on v6

--- a/solution.py
+++ b/solution.py
@@ -24,7 +24,7 @@
 ROW_AXES = ("z", "x_lo")
 ROW_ALL = ("x_lo", "z")
 BLOCK_OF = [(i & 1) * 16 + (i >> 1) for i in range(N_ROW)]
-CHUNK = TABLES * PART + 16 + 32
+CHUNK = (TABLES + 3, PART, WIDTH)
 UNROLL = 8
 VMEM = 16 << 20
 
@@ -105,56 +105,107 @@
     wide = cross_grads[...]
     wide = jnp.concatenate([wide[:, at : at + WIDTH] for at in range(0, 2 * RANK, WIDTH)], axis=0).astype(bf16)
     for copy in range(8):
-        out[copy, : TABLES * PART, :] = new
-        out[copy, TABLES * PART : TABLES * PART + PART, :] = terms
-        out[copy, TABLES * PART + PART :, :] = wide
+        out[copy, :TABLES] = new.reshape(TABLES, PART, WIDTH)
+        out[copy, TABLES] = terms
+        out[copy, TABLES + 1 :] = wide.reshape(2, PART, WIDTH)
 
 
 def adagrad(grads, rows, accum, cross_grads):
     return pl.pallas_call(
         adagrad_kernel,
-        out_shape=jax.ShapeDtypeStruct((8, CHUNK, WIDTH), bf16),
+        out_shape=jax.ShapeDtypeStruct((8, *CHUNK), bf16),
         compiler_params=pltpu.CompilerParams(vmem_limit_bytes=VMEM),
         name="adagrad",
     )(grads, rows, accum, cross_grads)
 
 
-def unpack_kernel(scalars, own, other, rows_out, accum_out, grad_v, grad_u, grad_bias, accums, cross_grads):
+def start_rows(source, rows_out, turn, scalars, arrived):
+    copies = []
     for outer in range(8):
-        for turn, source in enumerate((own, other)):
-            part = part_of(outer, turn ^ scalars[0])
-            rows_out[:, pl.ds(part, 1)] = source[outer, : TABLES * PART].reshape(TABLES, 1, PART, WIDTH)
-            terms = source[outer, TABLES * PART : TABLES * PART + PART].astype(f32)
-            total = terms[:, :32] + terms[:, 32:64] + terms[:, 64:96]
-            accums[pl.ds(pl.multiple_of(part * PART, PART), PART), :] = jnp.concatenate(
-                [total, jnp.zeros((PART, WIDTH - 32), f32)], axis=1
-            )
-            wide = source[outer, TABLES * PART + PART :].astype(f32)
-            at = pl.multiple_of(part * GRAD_ROWS, GRAD_ROWS)
-            for i in range(4):
-                cross_grads[pl.ds(at, GRAD_ROWS), i * WIDTH : (i + 1) * WIDTH] = wide[i * 8 : (i + 1) * 8]
+        part = part_of(outer, turn ^ scalars[0])
+        copies.append(
+            pltpu.make_async_copy(source.at[outer, pl.ds(0, TABLES)], rows_out.at[:, part], arrived.at[outer])
+        )
+        copies[-1].start()
+    return copies
+
+
+def place_rest(source, turn, scalars, accums, cross_grads):
+    for outer in range(8):
+        part = part_of(outer, turn ^ scalars[0])
+        terms = source[outer, TABLES].astype(f32)
+        total = terms[:, :32] + terms[:, 32:64] + terms[:, 64:96]
+        accums[pl.ds(pl.multiple_of(part * PART, PART), PART), :] = jnp.concatenate(
+            [total, jnp.zeros((PART, WIDTH - 32), f32)], axis=1
+        )
+        wide = source[outer, TABLES + 1 :].astype(f32).reshape(2 * PART, WIDTH)
+        at = pl.multiple_of(part * GRAD_ROWS, GRAD_ROWS)
+        for i in range(4):
+            cross_grads[pl.ds(at, GRAD_ROWS), i * WIDTH : (i + 1) * WIDTH] = wide[i * 8 : (i + 1) * 8]
+
+
+def own_rows_kernel(scalars, own, rows_out, accums, cross_grads, arrived):
+    copies = start_rows(own, rows_out, 0, scalars, arrived)
+    accums[...] = jnp.zeros_like(accums)
+    cross_grads[...] = jnp.zeros_like(cross_grads)
+    place_rest(own, 0, scalars, accums, cross_grads)
+    for copy in copies:
+        copy.wait()
+
+
+def unpack_kernel(
+    scalars, other, own_accums, own_cross, _, rows_out, accum_out, grad_v, grad_u, grad_bias, accums, cross_grads, arrived
+):
+    copies = start_rows(other, rows_out, 1, scalars, arrived)
+    accums[...] = own_accums[...]
+    cross_grads[...] = own_cross[...]
+    place_rest(other, 1, scalars, accums, cross_grads)
     accum_out[...] = accums[...].T[:TABLES]
     grad_u[...] = cross_grads[:FEATS, :RANK]
     grad_v[...] = cross_grads[:FEATS, RANK:]
     grad_bias[...] = cross_grads[FEATS, :FEATS]
-
-
-def unpack(scalars, own, other):
-    shapes = [
-        ((TABLES, N_DP, PART, WIDTH), bf16),
-        ((TABLES, ROWS), f32),
-        ((FEATS, RANK), f32),
-        ((FEATS, RANK), f32),
-        ((FEATS,), f32),
-    ]
-    return call(
+    for copy in copies:
+        copy.wait()
+
+
+NEW_ROWS = jax.ShapeDtypeStruct((TABLES, N_DP, PART, WIDTH), bf16)
+
+
+def own_rows(scalars, own):
+    return pl.pallas_call(
+        own_rows_kernel,
+        in_specs=[pl.BlockSpec(memory_space=pltpu.SMEM), pl.BlockSpec(memory_space=pltpu.VMEM)],
+        out_specs=[pl.BlockSpec(memory_space=pl.ANY)] + [pl.BlockSpec(memory_space=pltpu.VMEM)] * 2,
+        out_shape=[
+            NEW_ROWS,
+            jax.ShapeDtypeStruct((ROWS, WIDTH), f32),
+            jax.ShapeDtypeStruct((N_DP * GRAD_ROWS, 2 * RANK), f32),
+        ],
+        scratch_shapes=[pltpu.SemaphoreType.DMA((8,))],
+        compiler_params=pltpu.CompilerParams(vmem_limit_bytes=VMEM),
+        cost_estimate=pl.CostEstimate(flops=1 << 28, bytes_accessed=2 << 20, transcendentals=0),
+        name="own_rows",
+    )(scalars, own)
+
+
+def unpack(scalars, other, rows, accums, cross_grads):
+    vmem = pl.BlockSpec(memory_space=pltpu.VMEM)
+    any_space = pl.BlockSpec(memory_space=pl.ANY)
+    shapes = [(TABLES, ROWS), (FEATS, RANK), (FEATS, RANK), (FEATS,)]
+    return pl.pallas_call(
         unpack_kernel,
-        "unpack",
-        scalars,
-        (own, other),
-        [jax.ShapeDtypeStruct(shape, kind) for shape, kind in shapes],
-        [pltpu.VMEM((ROWS, WIDTH), f32), pltpu.VMEM((N_DP * GRAD_ROWS, 2 * RANK), f32)],
-    )
+        in_specs=[pl.BlockSpec(memory_space=pltpu.SMEM), vmem, vmem, vmem, any_space],
+        out_specs=[any_space] + [vmem] * len(shapes),
+        out_shape=[NEW_ROWS] + [jax.ShapeDtypeStruct(shape, f32) for shape in shapes],
+        input_output_aliases={4: 0},
+        scratch_shapes=[
+            pltpu.VMEM((ROWS, WIDTH), f32),
+            pltpu.VMEM((N_DP * GRAD_ROWS, 2 * RANK), f32),
+            pltpu.SemaphoreType.DMA((8,)),
+        ],
+        compiler_params=pltpu.CompilerParams(vmem_limit_bytes=VMEM),
+        name="unpack",
+    )(scalars, other, accums, cross_grads, rows)
 
 
 def counts_of(words, scaled=False):
@@ -507,8 +558,9 @@
     own = exchange(
         adagrad(row_grad, my_rows.reshape(TABLES * PART, WIDTH), my_accum, cross_sums), DP_OUTER
     )
+    scalars = jnp.stack([core]).astype(jnp.int32)
     new_rows, new_accum, grad_v, grad_u, grad_bias = unpack(
-        jnp.stack([core]).astype(jnp.int32), own, to_other_core(own)
+        scalars, to_other_core(own), *own_rows(scalars, own)
     )
     return (crossed.T, new_rows.reshape(TABLES, ROWS, WIDTH), new_accum, grad_v, grad_u, grad_bias)
 

time: 200 us -> 200 us (level)
    pallas_call x1 -> x3, Pallas kernels: 0.35 us -> 3.01 us  [the longest x1 1.68 us: unpack(): pl.pallas_call(unpack_kernel, in_specs=[pl.BlockSpec(memory_space=pltpu.S...]
    pallas_call x8 -> x7, Pallas kernels: 16 us -> 14.4 us  [call(): pl.pallas_call(kernel, in_specs=[pl.BlockSpec(memory_space=pltpu.SMEM)] +...]
  transfers between devices with their start and end apart: 10 -> 10, of which waited for: 6 -> 6; matrix products, arithmetic and copies ran while one was open for 0% -> 0% of each run, Pallas kernels for 7% -> 8%
where the time goes in v7:
time: 200 us; the launch traced here: 199 us
  starting transfers between devices  73.6 us (37%)
  blocking collectives  51.4 us (26%)
  waiting for transfers between devices  41.5 us (21%)
  Pallas kernels  25.5 us (13%)
  local copies, waits for them, and re-layouts  5.42 us (3%)
    all_to_all x3, blocking collectives, exchange(): return lax.all_to_all(x, axes, 0, 0, tiled=True)  51.4 us
    all_to_all x4, starting transfers between devices, exchange(): return lax.all_to_all(x, axes, 0, 0, tiled=True)  41.2 us
    all_to_all x4, waiting for transfers between devices, exchange(): return lax.all_to_all(x, axes, 0, 0, tiled=True)  40 us
    ppermute x6, starting transfers between devices, swap(): return lax.ppermute(x, axis, [(0, 1), (1, 0)])  32.3 us
    pallas_call x7, Pallas kernels, call(): pl.pallas_call(kernel, in_specs=[pl.BlockSpec(memory_space=pltpu.SMEM)] +...  14.4 us
    pallas_call x1, Pallas kernels, bag_words(): pl.pallas_call(words_kernel, grid_spec=pltpu.PrefetchScalarGridSpec(num_s...  4.7 us
  transfers between devices with their start and end apart: 10, of which 6 were waited for; matrix products, arithmetic and copies ran while one was open for 0% of the time, Pallas kernels for 8%

profile of v7, /device:TPU:1, one launch (start us, length us, event | category | flops | bytes accessed | tf_op | source)
XLA Modules:
  0.0 198.9 jit_solution(6202217614066808815)
XLA Ops:
  0.6 0.0 copy-start
  0.6 0.0 copy-start.5
  0.7 0.0 copy-start.3
  0.7 0.0 copy-start.4
  0.7 1.7 pack_rows.1
  2.4 17.0 %all-to-all-start = ((bf16[32,16,104]{2,1,0:T(8,128)(2,1)}), bf16[32,16,104]{2,1,0:T(8,128)(2,1)S(1)}, u32[]{:S(2)}, u32[]{:S(2)}) async-start(bf16[32,16,104]{2,1,0:T(8,128)(2,1)} %get-tuple-element.34), calls=%async_computation | async-start | bytes 262144 | tf_op jit(solution)/shard_map/all_to_all | solution.py:495
  19.4 0.0 copy-start.1
  19.5 0.0 copy-done.3
  19.5 0.0 copy-done.4
  19.5 3.3 %collective-permute-start = (bf16[104,768]{1,0:T(8,128)(2,1)S(1)}, bf16[104,768]{1,0:T(8,128)(2,1)S(1)}, u32[]{:S(2)}, u32[]{:S(2)}) collective-permute-start(bf16[104,768]{1,0:T(8,128)(2,1)S(1)} %pad_maximum_fusion), channel_id=1, source_target_pairs={{0,16},{16,0},{1,17},{17,1},{2,18},{18,2},{3,19},{19,3},{4,20},{20... | collective-permute-start | bytes 479240 | tf_op jit(solution)/shard_map/ppermute | solution.py:499
  22.8 10.7 %all-to-all-done = bf16[32,16,104]{2,1,0:T(8,128)(2,1)S(1)} async-done(((bf16[32,16,104]{2,1,0:T(8,128)(2,1)}), bf16[32,16,104]{2,1,0:T(8,128)(2,1)S(1)}, u32[]{:S(2)}, u32[]{:S(2)}) %all-to-all-start) | async-done | bytes 106528 | tf_op jit(solution)/shard_map/all_to_all | solution.py:495
  33.4 0.1 copy.17
  33.6 0.0 collective-permute-done.partner
  33.6 1.0 broadcast_in_dim.17
  34.6 6.4 %all-to-all-start.1 = ((bf16[8,104,512]{2,1,0:T(8,128)(2,1)}), bf16[8,104,512]{2,1,0:T(8,128)(2,1)S(1)}, u32[]{:S(2)}, u32[]{:S(2)}) async-start(bf16[8,104,512]{2,1,0:T(8,128)(2,1)} %broadcast_in_dim.17), calls=%async_computation.1 | async-start | bytes 1703936 | tf_op jit(solution)/shard_map/all_to_all | solution.py:495
  40.9 0.1 pad_add_fusion.scalars
  41.0 4.7 %bag_words.1 = (s32[2,2,8,64,256]{4,3,2,1,0:T(8,128)S(1)}, s32[2,1,8,64,256]{4,3,2,1,0:T(8,128)S(1)}, s32[2,1,8,64,256]{4,3,2,1,0:T(8,128)S(1)}) custom-call(s32[4]{0:T(128)S(1)} %pad_add_fusion.scalars, s32[26,8,512]{2,1,0:T(8,128)S(1)} %bitcast.21, s32[26,8,512]{2,1,0:T(8,128)S(1)} %bitcast.22, s32[26,8,512]{2,1,0:T(8,128)S(1)} %bitcast.23, ...), custom_call_target="tpu_custom_call" | custom-call | flops 268435456 | bytes 5242880 | tf_op jit(solution)/shard_map/bag_words/pallas_call | solution.py:268
  45.7 1.3 copy-done.6
  47.1 1.0 copy-done.9
  48.0 3.0 %all-to-all-done.1.refs_0_ = bf16[8,104,512]{2,1,0:T(8,128)(2,1)S(1)} async-done(((bf16[8,104,512]{2,1,0:T(8,128)(2,1)}), bf16[8,104,512]{2,1,0:T(8,128)(2,1)S(1)}, u32[]{:S(2)}, u32[]{:S(2)}) %all-to-all-start.1) | async-done | bytes 852000 | tf_op jit(solution)/shard_map/all_to_all | solution.py:495
  51.1 7.0 %collective-permute-start.1 = (bf16[8,104,512]{2,1,0:T(8,128)(2,1)S(1)}, bf16[8,104,512]{2,1,0:T(8,128)(2,1)S(1)}, u32[]{:S(2)}, u32[]{:S(2)}) collective-permute-start(bf16[8,104,512]{2,1,0:T(8,128)(2,1)S(1)} %all-to-all-done.1.refs_0_), channel_id=1, source_target_pairs={{0,32},{32,0},{1,33},{33,1},{2,34},{34,2},{3,35},{35,3},{4,36},{36... | collective-permute-start | bytes 2555912 | tf_op jit(solution)/shard_map/ppermute | solution.py:499
  58.1 0.1 add_add_fusion.1.scalars
  58.2 0.1 add_add_fusion.scalars
  58.3 1.5 bags.4.refs_1_
  59.8 0.3 collective-permute-done.1.refs_1_.refs_0_
  60.1 1.5 bags.5.pooled
  61.6 3.3 %collective-permute-start.2 = (bf16[104,256]{1,0:T(8,128)(2,1)S(1)}, bf16[104,256]{1,0:T(8,128)(2,1)S(1)}, u32[]{:S(2)}, u32[]{:S(2)}) collective-permute-start(bf16[104,256]{1,0:T(8,128)(2,1)S(1)} %bags.5.pooled), channel_id=1, source_target_pairs={{0,16},{16,0},{1,17},{17,1},{2,18},{18,2},{3,19},{19,3},{4,20},{20... | collective-permute-start | bytes 159752 | tf_op jit(solution)/shard_map/ppermute | solution.py:499
  64.9 0.0 copy-done.7
  64.9 2.3 %bags.3.pooled_a.pooled = bf16[104,256]{1,0:T(8,128)(2,1)S(1)} custom-call(s32[3]{0:T(128)S(1)} %add_add_fusion.1.scalars, s32[2,2,8,64,256]{4,3,2,1,0:T(8,128)S(1)} %copy-done.7, bf16[8,104,512]{2,1,0:T(8,128)(2,1)S(1)} %all-to-all-done.1.refs_0_, bf16[8,104,512]{2,1,0:T(8,128)(2,1)S(1)} %collective-permute-done.1.refs_1_.refs_0_), custom_call_target="tpu_custom_call" | custom-call | flops 4294967296 | bytes 5242880 | tf_op jit(solution)/shard_map/bags/pallas_call | solution.py:293
  67.2 0.0 collective-permute-done.2.pooled_b
  67.2 0.0 copy-done.13
  67.2 0.0 copy-start.14
  67.2 0.9 rank_terms.1
  68.1 16.6 %all_to_all.35.terms = bf16[16,32,256]{2,1,0:T(8,128)(2,1)S(1)} all-to-all(bf16[16,32,256]{2,1,0:T(8,128)(2,1)S(1)} %bitcast.27), channel_id=1, replica_groups=mesh['y'=4,'x_hi'=2,'core'=2,'x_lo'=2,'z'=16] {'z'}, dimensions={0} | all-to-all | bytes 524288 | tf_op jit(solution)/shard_map/all_to_all | solution.py:495
  84.7 0.8 sum_and_copy.1
  85.5 10.7 %all-to-all-start.3 = ((bf16[16,32,256]{2,1,0:T(8,128)(2,1)}), bf16[16,32,256]{2,1,0:T(8,128)(2,1)S(1)}, u32[]{:S(2)}, u32[]{:S(2)}) async-start(bf16[16,32,256]{2,1,0:T(8,128)(2,1)} %sum_and_copy.1), calls=%async_computation.3 | async-start | bytes 524288 | tf_op jit(solution)/shard_map/all_to_all | solution.py:495
  96.1 0.0 copy-done.14
  96.1 0.1 copy.19.bias
  96.3 12.7 %all-to-all-done.3 = bf16[16,32,256]{2,1,0:T(8,128)(2,1)S(1)} async-done(((bf16[16,32,256]{2,1,0:T(8,128)(2,1)}), bf16[16,32,256]{2,1,0:T(8,128)(2,1)S(1)}, u32[]{:S(2)}, u32[]{:S(2)}) %all-to-all-start.3) | async-done | bytes 262176 | tf_op jit(solution)/shard_map/all_to_all | solution.py:495
  108.9 3.6 %collective-permute-start.3 = (bf16[512,256]{1,0:T(8,128)(2,1)S(1)}, bf16[512,256]{1,0:T(8,128)(2,1)S(1)}, u32[]{:S(2)}, u32[]{:S(2)}) collective-permute-start(bf16[512,256]{1,0:T(8,128)(2,1)S(1)} %bitcast.25), channel_id=1, source_target_pairs={{0,16},{16,0},{1,17},{17,1},{2,18},{18,2},{3,19},{19,3},{4,20},{20... | collective-permute-start | bytes 786440 | tf_op jit(solution)/shard_map/ppermute | solution.py:499
  112.6 0.0 copy-start.8
  112.6 1.6 copy-done.8
  114.2 3.5 %cross_and_row_grads.2 = (bf16[104,256]{1,0:T(8,128)(2,1)S(1)}, f32[8,112,512]{2,1,0:T(8,128)S(1)}, f32[8,112,512]{2,1,0:T(8,128)S(1)}) custom-call(s32[3]{0:T(128)S(1)} %add_add_fusion.1.scalars, s32[2,2,8,64,256]{4,3,2,1,0:T(8,128)S(1)} %copy-done.8, bf16[512,256]{1,0:T(8,128)(2,1)S(1)} %bitcast.26, bf16[104,256]{1,0:T(8,128)(2,1)S(1)} %bags.3.pooled_a.pooled, ...), custom_call_target="tpu_custom_call" | custom-call | flops 4294967296 | bytes 5242880 | tf_op jit(solution)/shard_map/cross_and_row_grads/pallas_call | solution.py:293
  117.7 0.0 collective-permute-done.3.ranks
  117.7 2.7 %cross_and_row_grads.3 = (bf16[104,512]{1,0:T(8,128)(2,1)}, bf16[2,104,256]{2,1,0:T(8,128)(2,1)S(1)}, f32[128,512]{1,0:T(8,128)S(1)}, bf16[8,112,512]{2,1,0:T(8,128)(2,1)S(1)}) custom-call(s32[3]{0:T(128)S(1)} %add_add_fusion.scalars, s32[2,1,8,64,256]{4,3,2,1,0:T(8,128)S(1)} %copy-done.11, bf16[512,256]{1,0:T(8,128)(2,1)S(1)} %collective-permute-done.3.ranks, ...), custom_call_target="tpu_custom_call" | custom-call | flops 4294967296 | bytes 5242880 | tf_op jit(solution)/shard_map/cross_and_row_grads/pallas_call | solution.py:293
  120.4 8.5 %collective-permute-start.4 = (bf16[8,112,512]{2,1,0:T(8,128)(2,1)S(1)}, bf16[8,112,512]{2,1,0:T(8,128)(2,1)S(1)}, u32[]{:S(2)}, u32[]{:S(2)}) collective-permute-start(bf16[8,112,512]{2,1,0:T(8,128)(2,1)S(1)} %get-tuple-element.50), channel_id=1, source_target_pairs={{0,32},{32,0},{1,33},{33,1},{2,34},{34,2},{3,35},{35,3},{4,36},{36... | collective-permute-start | bytes 2752520 | tf_op jit(solution)/shard_map/ppermute | solution.py:499
  129.0 2.0 %row_grads.1 = bf16[8,112,512]{2,1,0:T(8,128)(2,1)S(1)} custom-call(s32[3]{0:T(128)S(1)} %add_add_fusion.scalars, s32[2,1,8,64,256]{4,3,2,1,0:T(8,128)S(1)} %get-tuple-element.42.words, bf16[2,104,256]{2,1,0:T(8,128)(2,1)S(1)} %get-tuple-element.47.grads, f32[128,512]{1,0:T(8,128)S(1)} %get-tuple-element.48.cross_grads, ...), custom_call_target="tpu_custom_call" | custom-call | flops 4294967296 | bytes 5242880 | tf_op jit(solution)/shard_map/row_grads/pallas_call | solution.py:293
  131.0 0.0 collective-permute-done.4
  131.1 0.2 add_convert_fusion
  131.3 0.0 copy-start.2
  131.3 18.5 %all_to_all.36.terms = bf16[8,112,512]{2,1,0:T(8,128)(2,1)S(1)} all-to-all(bf16[8,112,512]{2,1,0:T(8,128)(2,1)S(1)} %add_convert_fusion), channel_id=1, replica_groups=mesh['y'=4,'x_hi'=2,'core'=2,'x_lo'=2,'z'=16] {'x_hi','y'}, dimensions={0} | all-to-all | bytes 1835008 | tf_op jit(solution)/shard_map/all_to_all | solution.py:495
  149.9 0.8 sum_and_turn.1
  150.7 7.3 %all-to-all-start.5 = ((bf16[32,16,104]{2,1,0:T(8,128)(2,1)}), bf16[32,16,104]{2,1,0:T(8,128)(2,1)S(1)}, u32[]{:S(2)}, u32[]{:S(2)}) async-start(bf16[32,16,104]{2,1,0:T(8,128)(2,1)} %bitcast.16), calls=%async_computation.5 | async-start | bytes 262144 | tf_op jit(solution)/shard_map/all_to_all | solution.py:495
  158.0 0.0 copy-done
  158.0 0.1 constant_dynamic-slice_fusion
  158.1 0.1 broadcast_in_dim.18
  158.2 13.6 %all-to-all-done.5.grads_in = bf16[32,16,104]{2,1,0:T(8,128)(2,1)S(1)} async-done(((bf16[32,16,104]{2,1,0:T(8,128)(2,1)}), bf16[32,16,104]{2,1,0:T(8,128)(2,1)S(1)}, u32[]{:S(2)}, u32[]{:S(2)}) %all-to-all-start.5) | async-done | bytes 106528 | tf_op jit(solution)/shard_map/all_to_all | solution.py:495
  171.8 0.1 broadcast_in_dim.19.accum
  171.9 0.3 adagrad.1
  172.3 16.3 %all_to_all.37.own = bf16[8,29,16,128]{3,2,1,0:T(8,128)(2,1)S(1)} all-to-all(bf16[8,29,16,128]{3,2,1,0:T(8,128)(2,1)S(1)} %adagrad.1), channel_id=1, replica_groups=mesh['y'=4,'x_hi'=2,'core'=2,'x_lo'=2,'z'=16] {'x_hi','y'}, dimensions={0} | all-to-all | bytes 1900544 | tf_op jit(solution)/shard_map/all_to_all | solution.py:495
  188.6 6.6 %collective-permute-start.5 = (bf16[8,29,16,128]{3,2,1,0:T(8,128)(2,1)S(1)}, bf16[8,29,16,128]{3,2,1,0:T(8,128)(2,1)S(1)}, u32[]{:S(2)}, u32[]{:S(2)}) collective-permute-start(bf16[8,29,16,128]{3,2,1,0:T(8,128)(2,1)S(1)} %all_to_all.37.own), channel_id=1, source_target_pairs={{0,32},{32,0},{1,33},{33,1},{2,34},{34,2},{3,35},{35,3},{4,36},{36... | collective-permute-start | bytes 2850824 | tf_op jit(solution)/shard_map/ppermute | solution.py:499
  195.1 1.0 own_rows.1
  196.1 1.1 collective-permute-done.5.other
  197.3 1.7 unpack.1
  (17 shorter events, 0.1 us)
Async XLA Ops:
  0.6 157.4 %copy-start = (f32[26,256]{1,0:T(8,128)S(1)}, f32[26,256]{1,0:T(8,128)}, u32[]{:S(2)}) copy-start(f32[26,256]{1,0:T(8,128)} %param.8) | copy-start | bytes 79876
  0.6 18.8 %copy-start.5 = (bf16[512,104]{0,1:T(8,128)(2,1)S(1)}, bf16[512,104]{0,1:T(8,128)(2,1)}, u32[]{:S(2)}) copy-start(bf16[512,104]{0,1:T(8,128)(2,1)} %param.13) | copy-start | bytes 319492
  0.7 18.8 %copy-start.3 = (bf16[104,256]{1,0:T(8,128)(2,1)S(1)}, bf16[104,256]{1,0:T(8,128)(2,1)}, u32[]{:S(2)}) copy-start(bf16[104,256]{1,0:T(8,128)(2,1)} %v.3) | copy-start | bytes 159748
  0.7 18.8 %copy-start.4 = (bf16[104,256]{1,0:T(8,128)(2,1)S(1)}, bf16[104,256]{1,0:T(8,128)(2,1)}, u32[]{:S(2)}) copy-start(bf16[104,256]{1,0:T(8,128)(2,1)} %u.3) | copy-start | bytes 159748
  2.4 31.0 %all-to-all-start = ((bf16[32,16,104]{2,1,0:T(8,128)(2,1)}), bf16[32,16,104]{2,1,0:T(8,128)(2,1)S(1)}, u32[]{:S(2)}, u32[]{:S(2)}) async-start(bf16[32,16,104]{2,1,0:T(8,128)(2,1)} %get-tuple-element.34), calls=%async_computation | async-start | bytes 262144 | tf_op jit(solution)/shard_map/all_to_all | solution.py:495
  19.4 21.6 %copy-start.1 = (s32[512,26,8]{0,2,1:T(8,128)S(1)}, s32[512,26,8]{0,2,1:T(8,128)}, u32[]{:S(2)}) copy-start(s32[512,26,8]{0,2,1:T(8,128)} %param.9) | copy-start | bytes 1277956
  19.5 14.1 %collective-permute-start = (bf16[104,768]{1,0:T(8,128)(2,1)S(1)}, bf16[104,768]{1,0:T(8,128)(2,1)S(1)}, u32[]{:S(2)}, u32[]{:S(2)}) collective-permute-start(bf16[104,768]{1,0:T(8,128)(2,1)S(1)} %pad_maximum_fusion), channel_id=1, source_target_pairs={{0,16},{16,0},{1,17},{17,1},{2,18},{18,2},{3,19},{19,3},{4,20},{20... | collective-permute-start | bytes 479240 | tf_op jit(solution)/shard_map/ppermute | solution.py:499
  33.6 1.0 copy-start.12
  34.6 16.5 %all-to-all-start.1 = ((bf16[8,104,512]{2,1,0:T(8,128)(2,1)}), bf16[8,104,512]{2,1,0:T(8,128)(2,1)S(1)}, u32[]{:S(2)}, u32[]{:S(2)}) async-start(bf16[8,104,512]{2,1,0:T(8,128)(2,1)} %broadcast_in_dim.17), calls=%async_computation.1 | async-start | bytes 1703936 | tf_op jit(solution)/shard_map/all_to_all | solution.py:495
  45.7 1.3 copy-start.6
  47.1 1.0 copy-start.9
  51.1 9.0 %collective-permute-start.1 = (bf16[8,104,512]{2,1,0:T(8,128)(2,1)S(1)}, bf16[8,104,512]{2,1,0:T(8,128)(2,1)S(1)}, u32[]{:S(2)}, u32[]{:S(2)}) collective-permute-start(bf16[8,104,512]{2,1,0:T(8,128)(2,1)S(1)} %all-to-all-done.1.refs_0_), channel_id=1, source_target_pairs={{0,32},{32,0},{1,33},{33,1},{2,34},{34,2},{3,35},{35,3},{4,36},{36... | collective-permute-start | bytes 2555912 | tf_op jit(solution)/shard_map/ppermute | solution.py:499
  58.3 1.8 copy-start.10
  59.7 5.2 %copy-start.7 = (s32[2,2,8,64,256]{4,3,2,1,0:T(8,128)S(1)}, s32[2,2,8,64,256]{4,3,2,1,0:T(8,128)}, u32[]{:S(2)}) copy-start(s32[2,2,8,64,256]{4,3,2,1,0:T(8,128)} %copy-done.6) | copy-start | bytes 6291460
  61.6 5.6 %copy-start.13 = (bf16[104,768]{1,0:T(8,128)(2,1)S(1)}, bf16[104,768]{1,0:T(8,128)(2,1)}, u32[]{:S(2)}) copy-start(bf16[104,768]{1,0:T(8,128)(2,1)} %copy-done.12) | copy-start | bytes 479236
  61.6 5.6 %collective-permute-start.2 = (bf16[104,256]{1,0:T(8,128)(2,1)S(1)}, bf16[104,256]{1,0:T(8,128)(2,1)S(1)}, u32[]{:S(2)}, u32[]{:S(2)}) collective-permute-start(bf16[104,256]{1,0:T(8,128)(2,1)S(1)} %bags.5.pooled), channel_id=1, source_target_pairs={{0,16},{16,0},{1,17},{17,1},{2,18},{18,2},{3,19},{19,3},{4,20},{20... | collective-permute-start | bytes 159752 | tf_op jit(solution)/shard_map/ppermute | solution.py:499
  67.2 29.0 %copy-start.14 = (f32[104]{0:T(128)S(1)}, f32[104]{0:T(128)}, u32[]{:S(2)}) copy-start(f32[104]{0:T(128)} %param.12) | copy-start | bytes 1252
  85.5 23.4 %all-to-all-start.3 = ((bf16[16,32,256]{2,1,0:T(8,128)(2,1)}), bf16[16,32,256]{2,1,0:T(8,128)(2,1)S(1)}, u32[]{:S(2)}, u32[]{:S(2)}) async-start(bf16[16,32,256]{2,1,0:T(8,128)(2,1)} %sum_and_copy.1), calls=%async_computation.3 | async-start | bytes 524288 | tf_op jit(solution)/shard_map/all_to_all | solution.py:495
  108.9 8.8 %collective-permute-start.3 = (bf16[512,256]{1,0:T(8,128)(2,1)S(1)}, bf16[512,256]{1,0:T(8,128)(2,1)S(1)}, u32[]{:S(2)}, u32[]{:S(2)}) collective-permute-start(bf16[512,256]{1,0:T(8,128)(2,1)S(1)} %bitcast.25), channel_id=1, source_target_pairs={{0,16},{16,0},{1,17},{17,1},{2,18},{18,2},{3,19},{19,3},{4,20},{20... | collective-permute-start | bytes 786440 | tf_op jit(solution)/shard_map/ppermute | solution.py:499
  112.6 1.6 copy-start.8
  114.2 3.6 %copy-start.11 = (s32[2,1,8,64,256]{4,3,2,1,0:T(8,128)S(1)}, s32[2,1,8,64,256]{4,3,2,1,0:T(8,128)}, u32[]{:S(2)}) copy-start(s32[2,1,8,64,256]{4,3,2,1,0:T(8,128)} %copy-done.9) | copy-start | bytes 3145732
  120.4 10.6 %collective-permute-start.4 = (bf16[8,112,512]{2,1,0:T(8,128)(2,1)S(1)}, bf16[8,112,512]{2,1,0:T(8,128)(2,1)S(1)}, u32[]{:S(2)}, u32[]{:S(2)}) collective-permute-start(bf16[8,112,512]{2,1,0:T(8,128)(2,1)S(1)} %get-tuple-element.50), channel_id=1, source_target_pairs={{0,32},{32,0},{1,33},{33,1},{2,34},{34,2},{3,35},{35,3},{4,36},{36... | collective-permute-start | bytes 2752520 | tf_op jit(solution)/shard_map/ppermute | solution.py:499
  131.3 40.6 %copy-start.2 = (bf16[26,16,128]{2,1,0:T(8,128)(2,1)S(1)}, bf16[26,16,128]{2,1,0:T(8,128)(2,1)}, u32[]{:S(2)}) copy-start(bf16[26,16,128]{2,1,0:T(8,128)(2,1)} %get-tuple-element.52) | copy-start | bytes 319492
  150.7 21.1 %all-to-all-start.5 = ((bf16[32,16,104]{2,1,0:T(8,128)(2,1)}), bf16[32,16,104]{2,1,0:T(8,128)(2,1)S(1)}, u32[]{:S(2)}, u32[]{:S(2)}) async-start(bf16[32,16,104]{2,1,0:T(8,128)(2,1)} %bitcast.16), calls=%async_computation.5 | async-start | bytes 262144 | tf_op jit(solution)/shard_map/all_to_all | solution.py:495
  188.6 8.7 %collective-permute-start.5 = (bf16[8,29,16,128]{3,2,1,0:T(8,128)(2,1)S(1)}, bf16[8,29,16,128]{3,2,1,0:T(8,128)(2,1)S(1)}, u32[]{:S(2)}, u32[]{:S(2)}) collective-permute-start(bf16[8,29,16,128]{3,2,1,0:T(8,128)(2,1)S(1)} %all_to_all.37.own), channel_id=1, source_target_pairs={{0,32},{32,0},{1,33},{33,1},{2,34},{34,2},{3,35},{35,3},{4,36},{36... | collective-permute-start | bytes 2850824 | tf_op jit(solution)/shard_map/ppermute | solution.py:499
